TPU v7x, 1024 devices: a whole 8x8x8 slice. The times are simulated.
1024 devices in a mesh: rep: 8 (over z), outer: 8 (over y), local: 16 (over x, core).
Axes of the slice: x: 8, y: 8, z: 8, core: 2. Of those that a mesh axis runs over, the one named last changes fastest.
Arguments:
- tokens: bfloat16 [4096, 4096], P(('outer', 'local'), 'rep'), may hold values from -6 to 6
- out_grad: bfloat16 [4096, 4096], P(('outer', 'local'), 'rep'), may hold values from -6 to 6
- expert_ids: int32 [4096, 8], P(('outer', 'local')), may hold values from 0 to 127, all different within a row
- route_weights: float32 [4096, 8], P(('outer', 'local')), may hold values from 0.1 to 1
- gate_weight: bfloat16 [128, 4096, 1024], P(('outer', 'local'), 'rep'), may hold values from -0.09375 to 0.09375
- up_weight: bfloat16 [128, 4096, 1024], P(('outer', 'local'), 'rep'), may hold values from -0.09375 to 0.09375
- down_weight: bfloat16 [128, 1024, 4096], P(('outer', 'local'), None, 'rep'), may hold values from -0.1875 to 0.1875
Outputs:
- x_grad: bfloat16 [4096, 4096], P(('outer', 'local'), 'rep')
Inputs may be any that keep to these rules, and one draw needn't show every extreme that they name: `expert_ids`: each token names 8 different experts.
All inputs are finite; a program needn't handle non-finite values.
Results may differ from a plain program's by a relative error of at most 0.0064.
Values may be sent and summed in bfloat16 or wider, within the bound.
No kernel may reach another device: no remote copies, remote signals or barrier semaphores. Data moves between devices by JAX's collectives and lax.ppermute only.
A program may use at most 64 MiB of HBM per device.

v0:
```python
import jax
import jax.numpy as jnp
from jax import lax
from jax.sharding import PartitionSpec as P

TOP = 8


def routing(expert_ids, experts, capacity):
    row_count = expert_ids.shape[0] * expert_ids.shape[1]
    expert_list = expert_ids.reshape(row_count)
    onehot = (expert_list[:, None] == jnp.arange(experts, dtype=jnp.int32)[None, :]).astype(
        jnp.int32
    )
    before = jnp.cumsum(onehot, axis=0) - onehot
    slot_index = jnp.sum(before * onehot, axis=1)
    placed = (slot_index[:, None] == jnp.arange(capacity, dtype=jnp.int32)[None, :]).astype(
        jnp.int32
    )
    return (onehot[:, :, None] * placed[:, None, :]).reshape(row_count, experts * capacity)


def activate(gate_sum, up_sum, hidden_sum):
    gate_sigmoid = jax.nn.sigmoid(gate_sum)
    up_rows = (hidden_sum * gate_sum * gate_sigmoid).astype(jnp.bfloat16)
    gate_rows = (
        hidden_sum * up_sum * gate_sigmoid * (1.0 + gate_sum * (1.0 - gate_sigmoid))
    ).astype(jnp.bfloat16)
    return (gate_rows, up_rows)


def combine_partials(gate_part, up_part, hidden_part):
    gate_sum, up_sum, hidden_sum = (
        lax.psum_scatter(gate_part, "rep", scatter_dimension=1, tiled=True),
        lax.psum_scatter(up_part, "rep", scatter_dimension=1, tiled=True),
        lax.psum_scatter(hidden_part, "rep", scatter_dimension=1, tiled=True),
    )
    gate_rows, up_rows = activate(gate_sum, up_sum, hidden_sum)
    return (
        lax.all_gather(gate_rows, "rep", axis=1, tiled=True),
        lax.all_gather(up_rows, "rep", axis=1, tiled=True),
    )


def forward_parts(x_rows, dy_rows, w_gate, w_up, w_down):
    gate_part = jnp.dot(x_rows, w_gate, preferred_element_type=jnp.float32)
    up_part = jnp.dot(x_rows, w_up, preferred_element_type=jnp.float32)
    hidden_part = lax.dot_general(
        dy_rows, w_down, (((1,), (1,)), ((), ())), preferred_element_type=jnp.float32
    )
    return (gate_part, up_part, hidden_part)


def input_rows(gate_rows, up_rows, w_gate, w_up):
    contract = (((1,), (1,)), ((), ()))
    return lax.dot_general(
        gate_rows, w_gate, contract, preferred_element_type=jnp.float32
    ) + lax.dot_general(up_rows, w_up, contract, preferred_element_type=jnp.float32)


def per_device(tokens, out_grad, expert_ids, route_weights, gate_weight, up_weight, down_weight):
    tok_count, slice_width = tokens.shape
    n_outer = lax.axis_size("outer")
    n_local = lax.axis_size("local")
    experts = n_outer * n_local
    capacity = max(2, 2 * tok_count * TOP // experts)
    slot_total = experts * capacity
    dispatch_table = routing(expert_ids, experts, capacity)
    per_token = jnp.sum(dispatch_table.reshape(tok_count, TOP, slot_total), axis=1).astype(
        jnp.bfloat16
    )
    scaled = (route_weights[:, :, None] * out_grad.astype(jnp.float32)[:, None, :]).astype(
        jnp.bfloat16
    )
    scaled = scaled.reshape(tok_count * TOP, slice_width)
    grid_shape = (n_outer, n_local, capacity, slice_width)
    send_x = (
        jnp.dot(per_token.T, tokens, preferred_element_type=jnp.float32)
        .astype(jnp.bfloat16)
        .reshape(grid_shape)
    )
    send_dy = (
        jnp.dot(dispatch_table.astype(jnp.bfloat16).T, scaled, preferred_element_type=jnp.float32)
        .astype(jnp.bfloat16)
        .reshape(grid_shape)
    )
    w_gate = gate_weight[0]
    w_up = up_weight[0]
    w_down = down_weight[0]
    received_x, received_dy = (
        lax.all_to_all(
            lax.all_to_all(send_x, "outer", split_axis=0, concat_axis=0, tiled=True),
            "local",
            split_axis=1,
            concat_axis=1,
            tiled=True,
        ),
        lax.all_to_all(
            lax.all_to_all(send_dy, "outer", split_axis=0, concat_axis=0, tiled=True),
            "local",
            split_axis=1,
            concat_axis=1,
            tiled=True,
        ),
    )
    x_rows = received_x.reshape(slot_total, slice_width)
    dy_rows = received_dy.reshape(slot_total, slice_width)
    gate_part, up_part, hidden_part = forward_parts(x_rows, dy_rows, w_gate, w_up, w_down)
    gate_rows, up_rows = combine_partials(gate_part, up_part, hidden_part)
    row_grad = input_rows(gate_rows, up_rows, w_gate, w_up).astype(jnp.bfloat16)
    returned = lax.all_to_all(
        lax.all_to_all(
            row_grad.reshape(grid_shape), "outer", split_axis=0, concat_axis=0, tiled=True
        ),
        "local",
        split_axis=1,
        concat_axis=1,
        tiled=True,
    )
    x_grad = jnp.dot(
        per_token, returned.reshape(slot_total, slice_width), preferred_element_type=jnp.float32
    ).astype(jnp.bfloat16)
    return x_grad


def solution(mesh):
    return jax.shard_map(
        per_device,
        mesh=mesh,
        in_specs=(
            P(("outer", "local"), "rep"),
            P(("outer", "local"), "rep"),
            P(("outer", "local"), None),
            P(("outer", "local"), None),
            P(("outer", "local"), "rep", None),
            P(("outer", "local"), "rep", None),
            P(("outer", "local"), None, "rep"),
        ),
        out_specs=P(("outer", "local"), "rep"),
        check_vma=False,
    )
```

profile of v0, /device:TPU:1, one launch (start us, length us, event | category | flops | bytes accessed | tf_op | source)
XLA Modules:
  0.0 376.2 jit_solution(5940672827310330231)
XLA Ops:
  6.5 0.0 copy-start
  6.5 0.0 reduce-scatter.4.cloned.1.call-start
  6.5 0.8 copy.36
  7.4 0.1 eq.46
  7.5 0.1 eq.50
  7.6 0.8 copy.41
  8.3 0.1 copy.39
  8.4 0.2 fusion.14
  8.8 0.1 fusion.18
  8.9 0.2 fusion.16
  9.0 0.8 convert_element_type.73
  9.8 0.1 copy.37
  9.9 0.1 fusion.22
  10.1 0.1 convert_element_type.72
  10.1 0.4 convolution_convert_fusion
  10.5 0.1 reshape.130
  10.6 20.0 %all_to_all.30 = bf16[8,16,4,512]{3,2,1,0:T(4,128)(2,1)S(1)} all-to-all(bf16[8,16,4,512]{3,2,1,0:T(4,128)(2,1)S(1)} %reshape.130), channel_id=1, replica_groups=mesh['rep'=8,'outer'=8,'local'=16] {'outer'}, dimensions={0} | all-to-all | bytes 1048576 | tf_op jit(solution)/shard_map/all_to_all | solution.py:99
  30.7 0.2 copy.42
  30.9 30.2 %all_to_all.31 = bf16[8,16,4,512]{3,2,0,1:T(4,128)(2,1)S(1)} all-to-all(bf16[8,16,4,512]{3,2,0,1:T(4,128)(2,1)S(1)} %copy.42), channel_id=1, replica_groups=mesh['rep'=8,'outer'=8,'local'=16] {'local'}, dimensions={1} | all-to-all | bytes 1048576 | tf_op jit(solution)/shard_map/all_to_all | solution.py:98
  61.1 0.2 copy.43
  61.3 0.1 reshape.131
  61.4 3.4 fusion.8
  64.8 0.0 reduce-scatter.4.cloned.1.call-update
  64.8 0.0 reduce-scatter.8.cloned.1.call-start
  64.9 6.1 %mul.71 = s32[32,8,512]{1,0,2:T(8,128)} reshape(s32[256,128,4]{0,2,1:T(4,128)S(1)} %get-tuple-element.8) | data formatting | bytes 1048576 | tf_op jit(solution)/shard_map/mul | solution.py:20
  71.0 0.0 copy-start.2
  71.0 12.1 %reduce_sum.19 = s32[32,512]{0,1:T(8,128)S(1)} reduce(s32[32,8,512]{1,0,2:T(8,128)} %mul.71, s32[]{:T(128)} %constant.6.clone.1), dimensions={1}, to_apply=%region_3.4 | reduce | flops 114688 | bytes 589828 | tf_op jit(solution)/shard_map/reduce_sum | solution.py:69
  83.1 0.0 copy-done.2
  83.1 0.3 convolution_convert_fusion.1
  83.4 0.1 reshape.132
  83.5 19.4 %all_to_all.32 = bf16[8,16,4,512]{3,2,1,0:T(4,128)(2,1)S(1)} all-to-all(bf16[8,16,4,512]{3,2,1,0:T(4,128)(2,1)S(1)} %reshape.132), channel_id=1, replica_groups=mesh['rep'=8,'outer'=8,'local'=16] {'outer'}, dimensions={0} | all-to-all | bytes 1048576 | tf_op jit(solution)/shard_map/all_to_all | solution.py:92
  102.9 0.2 copy.44
  103.2 21.0 %all_to_all.33 = bf16[8,16,4,512]{3,2,0,1:T(4,128)(2,1)S(1)} all-to-all(bf16[8,16,4,512]{3,2,0,1:T(4,128)(2,1)S(1)} %copy.44), channel_id=1, replica_groups=mesh['rep'=8,'outer'=8,'local'=16] {'local'}, dimensions={1} | all-to-all | bytes 1048576 | tf_op jit(solution)/shard_map/all_to_all | solution.py:91
  124.2 0.2 copy.45
  124.4 0.1 reshape.133
  124.5 0.0 copy-done
  124.6 0.0 copy-start.1
  124.6 2.1 fusion.3
  126.6 0.0 reduce-scatter.8.cloned.1.call-update
  126.7 0.0 reduce-scatter.6.cloned.1.call-start
  126.7 0.0 copy-done.1
  126.7 2.0 fusion.6
  128.7 0.0 reduce-scatter.6.cloned.1.call-update
  128.8 0.0 all-gather.3.cloned.1.call-start
  128.8 0.0 reduce-scatter.4.cloned.1.call-done
  128.8 43.9 %reduce-scatter.8.cloned.1.call-done = f32[512,128]{1,0:T(8,128)} async-done(((f32[512,1024]{1,0:T(8,128)}), f32[512,128]{1,0:T(8,128)}) %reduce-scatter.8.cloned.1.call-update) | async-done | bytes 262160 | tf_op jit(solution)/shard_map/reduce_scatter | solution.py:34
  172.8 50.6 %reduce-scatter.6.cloned.1.call-done = f32[512,128]{1,0:T(8,128)} async-done(((f32[512,1024]{1,0:T(8,128)}), f32[512,128]{1,0:T(8,128)}) %reduce-scatter.6.cloned.1.call-update) | async-done | bytes 262160 | tf_op jit(solution)/shard_map/reduce_scatter | solution.py:35
  223.4 2.0 multiply_convert_fusion.1
  225.3 0.0 all-gather.3.cloned.1.call-update
  225.4 0.2 all-gather.5.cloned.1.call-start
  225.6 0.4 all-gather.5.cloned.1.call-update
  226.0 43.7 %all-gather.3.cloned.1.call-done = bf16[512,1024]{1,0:T(8,128)(2,1)} async-done(((bf16[512,128]{1,0:T(8,128)(2,1)}), bf16[512,1024]{1,0:T(8,128)(2,1)}) %all-gather.3.cloned.1.call-update) | async-done | bytes 1048592 | tf_op jit(solution)/shard_map/all_gather | solution.py:40
  269.6 2.9 fusion.1
  272.6 44.4 %all-gather.5.cloned.1.call-done = bf16[512,1024]{1,0:T(8,128)(2,1)} async-done(((bf16[512,128]{1,0:T(8,128)(2,1)}), bf16[512,1024]{1,0:T(8,128)(2,1)}) %all-gather.5.cloned.1.call-update) | async-done | bytes 1048592 | tf_op jit(solution)/shard_map/all_gather | solution.py:41
  317.0 2.3 fusion
  319.3 0.1 reshape.134
  319.4 18.6 %all_to_all.34 = bf16[8,16,4,512]{3,2,1,0:T(4,128)(2,1)S(1)} all-to-all(bf16[8,16,4,512]{3,2,1,0:T(4,128)(2,1)S(1)} %reshape.134), channel_id=1, replica_groups=mesh['rep'=8,'outer'=8,'local'=16] {'outer'}, dimensions={0} | all-to-all | bytes 1048576 | tf_op jit(solution)/shard_map/all_to_all | solution.py:112
  338.0 0.2 copy.46
  338.2 30.2 %all_to_all.35 = bf16[8,16,4,512]{3,2,0,1:T(4,128)(2,1)S(1)} all-to-all(bf16[8,16,4,512]{3,2,0,1:T(4,128)(2,1)S(1)} %copy.46), channel_id=1, replica_groups=mesh['rep'=8,'outer'=8,'local'=16] {'local'}, dimensions={1} | all-to-all | bytes 1048576 | tf_op jit(solution)/shard_map/all_to_all | solution.py:111
  368.5 0.2 copy.47
  368.7 0.1 reshape.135
  368.8 0.8 convolution_convert_fusion.2
  (7 shorter events, 0.1 us)
Async XLA Ops:
  6.5 118.0 %copy-start = (bf16[1,512,1024]{2,1,0:T(8,128)(2,1)S(1)}, bf16[1,512,1024]{2,1,0:T(8,128)(2,1)}, u32[]{:S(2)}) copy-start(bf16[1,512,1024]{2,1,0:T(8,128)(2,1)} %param.11) | copy-start | bytes 3145732
  6.5 122.3 %reduce-scatter.4.cloned.1.call-start = ((), (), s32[]{:S(2)}) async-start(), calls=%async_computation.9 | async-start | bytes 2359296 | tf_op jit(solution)/shard_map/reduce_scatter | solution.py:36
  64.8 107.9 %reduce-scatter.8.cloned.1.call-start = ((), (), s32[]{:S(2)}) async-start(), calls=%async_computation.11 | async-start | bytes 2359296 | tf_op jit(solution)/shard_map/reduce_scatter | solution.py:34
  71.0 12.1 %copy-start.2 = (bf16[32,512]{1,0:T(8,128)(2,1)S(1)}, bf16[32,512]{1,0:T(8,128)(2,1)}, u32[]{:S(2)}) copy-start(bf16[32,512]{1,0:T(8,128)(2,1)} %param.7) | copy-start | bytes 98308
  124.6 2.2 copy-start.1
  126.7 96.7 %reduce-scatter.6.cloned.1.call-start = ((), (), s32[]{:S(2)}) async-start(), calls=%async_computation.10 | async-start | bytes 2359296 | tf_op jit(solution)/shard_map/reduce_scatter | solution.py:35
  128.8 140.9 %all-gather.3.cloned.1.call-start = ((), (), s32[]{:S(2)}) async-start(), calls=%async_computation.12 | async-start | bytes 1179648 | tf_op jit(solution)/shard_map/all_gather | solution.py:40
  225.4 91.6 %all-gather.5.cloned.1.call-start = ((), (), s32[]{:S(2)}) async-start(), calls=%async_computation.13 | async-start | bytes 1179648 | tf_op jit(solution)/shard_map/all_gather | solution.py:41
Sparse Core Ops, SparseCore 0:
  64.9 46.1 reduce-scatter.3
  126.8 45.9 reduce-scatter.7
  176.2 47.1 reduce-scatter.5
  225.8 43.7 all-gather.2
  272.1 44.8 all-gather.4
where the time goes:
time: 377 us; the launch traced here: 376 us
  waiting for transfers between devices  183 us (49%)
  blocking collectives  140 us (37%)
  other arithmetic  15.5 us (4%)
  matrix products  14.1 us (4%)
  between operations  13.4 us (4%)
  local copies, waits for them, and re-layouts  10.2 us (3%)
    reduce_scatter x1, waiting for transfers between devices, combine_partials(): lax.psum_scatter(up_part, 'rep', scatter_dimension=1, tiled=True)  50.6 us
    all_gather x1, waiting for transfers between devices, combine_partials(): lax.all_gather(up_rows, 'rep', axis=1, tiled=True)  44.4 us
    reduce_scatter x1, waiting for transfers between devices, combine_partials(): lax.psum_scatter(gate_part, 'rep', scatter_dimension=1, tiled=True)  43.9 us
    all_gather x1, waiting for transfers between devices, combine_partials(): lax.all_gather(gate_rows, 'rep', axis=1, tiled=True)  43.7 us
    all_to_all x1, blocking collectives, per_device(): lax.all_to_all(lax.all_to_all(row_grad.reshape(grid_shape), 'outer', spli...  30.2 us
    all_to_all x1, blocking collectives, per_device(): lax.all_to_all(lax.all_to_all(send_dy, 'outer', split_axis=0, concat_axis...  30.2 us
    all_to_all x1, blocking collectives, per_device(): lax.all_to_all(lax.all_to_all(send_x, 'outer', split_axis=0, concat_axis=...  21 us
    all_to_all x1, blocking collectives, per_device(): lax.all_to_all(send_dy, 'outer', split_axis=0, concat_axis=0, tiled=True)  20 us
  transfers between devices with their start and end apart: 5, of which 4 were waited for; matrix products, arithmetic and copies ran while one was open for 7% of the time, Pallas kernels for 0%

commit v1 on v0

v1 whole, which is shorter than its diff:
```python
import jax
import jax.numpy as jnp
from jax import lax
from jax.experimental import pallas as pl
from jax.experimental.pallas import tpu as pltpu
from jax.sharding import PartitionSpec as P

F32 = jnp.float32
BF16 = jnp.bfloat16
TRANS_B = (((1,), (1,)), ((), ()))


def params(mib=48):
    return pltpu.CompilerParams(vmem_limit_bytes=mib * 1024 * 1024)


def route_kernel(capacity, ids_ref, w_ref, tok_ref, og_ref, dy_ref, x_ref, pt_ref, scaled_ref):
    top, tok = ids_ref.shape
    rows = top * tok
    slots = dy_ref.shape[0]
    c_row = lax.broadcasted_iota(jnp.int32, (rows, tok), 0)
    pick_i = (c_row % tok == lax.broadcasted_iota(jnp.int32, (rows, tok), 1)).astype(BF16)
    c_k = lax.broadcasted_iota(jnp.int32, (rows, top), 0)
    pick_k = (c_k // tok == lax.broadcasted_iota(jnp.int32, (rows, top), 1)).astype(F32)

    def column(values):
        spread = lax.dot_general(pick_i, values, TRANS_B, preferred_element_type=F32)
        return jnp.sum(spread * pick_k, axis=1, keepdims=True)

    ids_col = column(ids_ref[...].astype(F32).astype(BF16))
    w = w_ref[...]
    w_hi = w.astype(BF16)
    rest = w - w_hi.astype(F32)
    w_mid = rest.astype(BF16)
    w_lo = (rest - w_mid.astype(F32)).astype(BF16)
    w_col = column(w_hi) + (column(w_mid) + column(w_lo))
    sub = lax.broadcasted_iota(jnp.int32, (rows, rows), 0)
    lane = lax.broadcasted_iota(jnp.int32, (rows, rows), 1)
    ids_row = jnp.sum(jnp.where(sub == lane, ids_col, 0.0), axis=0, keepdims=True)
    order_sub = (sub % tok) * top + sub // tok
    order_lane = (lane % tok) * top + lane // tok
    earlier = (ids_col == ids_row) & (order_sub < order_lane)
    slot_row = jnp.sum(jnp.where(earlier, 1.0, 0.0), axis=0, keepdims=True)
    code = jnp.where(slot_row < capacity, ids_row * capacity + slot_row, -1.0).astype(jnp.int32)
    table = (lax.broadcasted_iota(jnp.int32, (slots, rows), 0) == code).astype(F32).astype(BF16)
    per_token = jnp.dot(table, pick_i, preferred_element_type=F32).astype(BF16)
    pt_ref[...] = lax.dot_general(
        pick_i, table, (((0,), (1,)), ((), ())), preferred_element_type=F32
    ).astype(BF16)
    og = jnp.dot(pick_i, og_ref[...], preferred_element_type=F32)
    scaled_ref[...] = (w_col * og).astype(BF16)
    dy_ref[...] = jnp.dot(table, scaled_ref[...], preferred_element_type=F32).astype(BF16)
    x_ref[...] = jnp.dot(per_token, tok_ref[...], preferred_element_type=F32).astype(BF16)


def route(tokens, out_grad, expert_ids, route_weights, experts, capacity):
    tok, width = tokens.shape
    top = expert_ids.shape[1]
    slots = experts * capacity
    return pl.pallas_call(
        lambda *refs: route_kernel(capacity, *refs),
        out_shape=(
            jax.ShapeDtypeStruct((slots, width), BF16),
            jax.ShapeDtypeStruct((slots, width), BF16),
            jax.ShapeDtypeStruct((tok, slots), BF16),
        ),
        scratch_shapes=[pltpu.VMEM((tok * top, width), BF16)],
        compiler_params=params(),
        name="route",
    )(expert_ids.T, route_weights.T, tokens, out_grad)


def hidden_kernel(dy_ref, w_ref, out_ref):
    part = out_ref.shape[2]
    out = lax.dot_general(dy_ref[...], w_ref[0], TRANS_B, preferred_element_type=F32)
    for j in range(out_ref.shape[0]):
        out_ref[j] = out[:, j * part : (j + 1) * part].astype(BF16)


def hidden_parts(dy_rows, w_down, n_rep):
    rows, width = dy_rows.shape
    part = w_down.shape[1] // n_rep
    per = 2
    return pl.pallas_call(
        hidden_kernel,
        grid=(n_rep // per,),
        in_specs=[
            pl.BlockSpec((rows, width), lambda c: (0, 0)),
            pl.BlockSpec((1, per * part, width), lambda c: (0, c, 0)),
        ],
        out_specs=pl.BlockSpec((per, rows, part), lambda c: (c, 0, 0)),
        out_shape=jax.ShapeDtypeStruct((n_rep, rows, part), BF16),
        compiler_params=params(),
        name="hidden",
    )(dy_rows, w_down)


def gate_up_kernel(x_ref, wg_ref, wu_ref, out_ref):
    part = out_ref.shape[2]
    rows = x_ref.shape[0]
    gate = jnp.dot(x_ref[...], wg_ref[0], preferred_element_type=F32)
    up = jnp.dot(x_ref[...], wu_ref[0], preferred_element_type=F32)
    for j in range(out_ref.shape[0]):
        out_ref[j, :rows] = gate[:, j * part : (j + 1) * part].astype(BF16)
        out_ref[j, rows:] = up[:, j * part : (j + 1) * part].astype(BF16)


def gate_up_parts(x_rows, w_gate, w_up, n_rep):
    rows, width = x_rows.shape
    part = w_gate.shape[2] // n_rep
    per = 2
    w_spec = pl.BlockSpec((1, width, per * part), lambda c: (0, 0, c))
    return pl.pallas_call(
        gate_up_kernel,
        grid=(n_rep // per,),
        in_specs=[pl.BlockSpec((rows, width), lambda c: (0, 0)), w_spec, w_spec],
        out_specs=pl.BlockSpec((per, 2 * rows, part), lambda c: (c, 0, 0)),
        out_shape=jax.ShapeDtypeStruct((n_rep, 2 * rows, part), BF16),
        compiler_params=params(),
        name="gate_up",
    )(x_rows, w_gate, w_up)


def activate_kernel(h_ref, g_ref, u_ref, out_ref):
    part = h_ref.shape[2]
    hidden = jnp.sum(h_ref[...].astype(F32), axis=0)
    gate = jnp.sum(g_ref[...].astype(F32), axis=0)
    up = jnp.sum(u_ref[...].astype(F32), axis=0)
    s = jax.nn.sigmoid(gate)
    out_ref[:, :part] = (hidden * up * s * (1.0 + gate * (1.0 - s))).astype(BF16)
    out_ref[:, part:] = (hidden * gate * s).astype(BF16)


def activate(hid, gu):
    n_rep, rows, part = hid.shape
    block = 128
    blocks = rows // block
    return pl.pallas_call(
        activate_kernel,
        grid=(blocks,),
        in_specs=[
            pl.BlockSpec((n_rep, block, part), lambda i: (0, i, 0)),
            pl.BlockSpec((n_rep, block, part), lambda i: (0, i, 0)),
            pl.BlockSpec((n_rep, block, part), lambda i: (0, blocks + i, 0)),
        ],
        out_specs=pl.BlockSpec((block, 2 * part), lambda i: (i, 0)),
        out_shape=jax.ShapeDtypeStruct((rows, 2 * part), BF16),
        compiler_params=params(),
        name="activate",
    )(hid, gu, gu)


def row_grad_kernel(r_ref, wg_ref, wu_ref, out_ref, acc_ref):
    c = pl.program_id(0)
    part = r_ref.shape[2] // 2
    total = None
    for j in range(r_ref.shape[0]):
        cols = slice(j * part, (j + 1) * part)
        term = lax.dot_general(
            r_ref[j, :, :part], wg_ref[0, :, cols], TRANS_B, preferred_element_type=F32
        ) + lax.dot_general(
            r_ref[j, :, part:], wu_ref[0, :, cols], TRANS_B, preferred_element_type=F32
        )
        total = term if total is None else total + term

    @pl.when(c == 0)
    def _():
        acc_ref[...] = total

    @pl.when(c > 0)
    def _():
        acc_ref[...] += total

    @pl.when(c == pl.num_programs(0) - 1)
    def _():
        out_ref[...] = acc_ref[...].astype(BF16)


def row_grad(rows_all, w_gate, w_up):
    n_rep, rows, part2 = rows_all.shape
    part = part2 // 2
    width = w_gate.shape[1]
    per = 2
    w_spec = pl.BlockSpec((1, width, per * part), lambda c: (0, 0, c))
    return pl.pallas_call(
        row_grad_kernel,
        grid=(n_rep // per,),
        in_specs=[pl.BlockSpec((per, rows, part2), lambda c: (c, 0, 0)), w_spec, w_spec],
        out_specs=pl.BlockSpec((rows, width), lambda c: (0, 0)),
        out_shape=jax.ShapeDtypeStruct((rows, width), BF16),
        scratch_shapes=[pltpu.VMEM((rows, width), F32)],
        compiler_params=params(),
        name="row_grad",
    )(rows_all, w_gate, w_up)


def per_device(tokens, out_grad, expert_ids, route_weights, gate_weight, up_weight, down_weight):
    tok, width = tokens.shape
    top = expert_ids.shape[1]
    n_rep = lax.axis_size("rep")
    experts = lax.axis_size("outer") * lax.axis_size("local")
    capacity = max(2, 2 * tok * top // experts)
    slots = experts * capacity
    both = ("outer", "local")
    send_dy, send_x, per_token_t = route(
        tokens, out_grad, expert_ids, route_weights, experts, capacity
    )

    def exchange(rows):
        blocks = rows.reshape(experts, capacity, width)
        return lax.all_to_all(blocks, both, 0, 0, tiled=True).reshape(slots, width)

    def over_rep(parts):
        return lax.all_to_all(parts, "rep", 0, 0, tiled=True)

    dy_rows = exchange(send_dy)
    x_rows = exchange(send_x)
    hid = over_rep(hidden_parts(dy_rows, down_weight, n_rep))
    gu = over_rep(gate_up_parts(x_rows, gate_weight, up_weight, n_rep))
    own = activate(hid, gu)
    rows_all = over_rep(jnp.broadcast_to(own[None], (n_rep,) + own.shape))
    returned = exchange(row_grad(rows_all, gate_weight, up_weight))
    return jnp.dot(per_token_t, returned, preferred_element_type=F32).astype(BF16)


def solution(mesh):
    return jax.shard_map(
        per_device,
        mesh=mesh,
        in_specs=(
            P(("outer", "local"), "rep"),
            P(("outer", "local"), "rep"),
            P(("outer", "local"), None),
            P(("outer", "local"), None),
            P(("outer", "local"), "rep", None),
            P(("outer", "local"), "rep", None),
            P(("outer", "local"), None, "rep"),
        ),
        out_specs=P(("outer", "local"), "rep"),
        check_vma=False,
    )
```

time: 377 us -> 253 us (0.67)
  waiting for transfers between devices: 183 us -> 60.5 us
  starting transfers between devices: 0.35 us -> 37.1 us
  other arithmetic: 15.5 us -> 0 us
  between operations: 13.4 us -> 0.11 us
  matrix products: 14.1 us -> 0.81 us
  Pallas kernels: 0 us -> 9.98 us
  blocking collectives: 140 us -> 134 us
    reduce_scatter x3 -> x0, waiting for transfers between devices: 94.6 us -> none  [the longest x1 50.6 us: combine_partials(): lax.psum_scatter(up_part, 'rep', scatter_dimension=1, tiled=True)]
    all_gather x2 -> x0, waiting for transfers between devices: 88.1 us -> none  [the longest x1 44.4 us: combine_partials(): lax.all_gather(up_rows, 'rep', axis=1, tiled=True)]
    all_to_all x0 -> x3, waiting for transfers between devices: none -> 60.5 us  [the longest x2 37.7 us: exchange(): return lax.all_to_all(blocks, both, 0, 0, tiled=True).reshape(slots, width)]
    all_to_all x0 -> x3, starting transfers between devices: none -> 37.1 us  [the longest x2 24.9 us: exchange(): return lax.all_to_all(blocks, both, 0, 0, tiled=True).reshape(slots, width)]
    dot_general x8 -> x1, matrix products: 14.1 us -> 0.81 us  [per_device(): jnp.dot(per_token_t, returned, preferred_element_type=F32).astype(BF16)]
    reduce_sum x2 -> x0, other arithmetic: 12.3 us -> none  [the longest x1 12.1 us: per_device(): jnp.sum(dispatch_table.reshape(tok_count, TOP, slot_total), axis=1)]
    pallas_call x0 -> x5, Pallas kernels: none -> 9.98 us  [the longest x1 3.56 us: row_grad(): pl.pallas_call(row_grad_kernel, grid=(n_rep // per,), in_specs=[pl.BlockS...]
    mul x1 -> x0, local copies, waits for them, and re-layouts: 6.13 us -> none  [routing(): onehot[:, :, None] * placed[:, None, :]]
  transfers between devices with their start and end apart: 5 -> 3, of which waited for: 4 -> 3; matrix products, arithmetic and copies ran while one was open for 7% -> 1% of each run, Pallas kernels for 0% -> 2%
where the time goes in v1:
time: 253 us; the launch traced here: 252 us
  blocking collectives  134 us (53%)
  waiting for transfers between devices  60.5 us (24%)
  starting transfers between devices  37.1 us (15%)
  Pallas kernels  9.98 us (4%)
  local copies, waits for them, and re-layouts  9.72 us (4%)
    all_to_all x2, blocking collectives, over_rep(): return lax.all_to_all(parts, 'rep', 0, 0, tiled=True)  108 us
    all_to_all x2, waiting for transfers between devices, exchange(): return lax.all_to_all(blocks, both, 0, 0, tiled=True).reshape(slots, width)  37.7 us
    all_to_all x1, blocking collectives, exchange(): return lax.all_to_all(blocks, both, 0, 0, tiled=True).reshape(slots, width)  26.3 us
    all_to_all x2, starting transfers between devices, exchange(): return lax.all_to_all(blocks, both, 0, 0, tiled=True).reshape(slots, width)  24.9 us
    all_to_all x1, waiting for transfers between devices, over_rep(): return lax.all_to_all(parts, 'rep', 0, 0, tiled=True)  22.8 us
    all_to_all x1, starting transfers between devices, over_rep(): return lax.all_to_all(parts, 'rep', 0, 0, tiled=True)  12.3 us
    unnamed x20, local copies, waits for them, and re-layouts  6.39 us
  transfers between devices with their start and end apart: 3, of which 3 were waited for; matrix products, arithmetic and copies ran while one was open for 1% of the time, Pallas kernels for 2%

profile of v1, /device:TPU:1, one launch (start us, length us, event | category | flops | bytes accessed | tf_op | source)
XLA Modules:
  0.0 252.3 jit_solution(1641946802821410259)
XLA Ops:
  0.0 0.0 copy-start.6
  0.0 0.8 copy-done.6
  0.8 0.0 copy-start.7
  0.8 0.8 copy-done.7
  1.5 0.0 copy-start.8
  1.5 0.7 copy-done.8
  2.2 0.0 copy-start.9
  2.2 0.7 copy-done.9
  2.9 1.1 route.1
  4.0 0.9 reshape.19
  4.9 0.0 copy-start.5
  4.9 19.5 %all-to-all-start = ((bf16[128,4,512]{2,1,0:T(4,128)(2,1)}), bf16[128,4,512]{2,1,0:T(4,128)(2,1)S(1)}, u32[]{:S(2)}, u32[]{:S(2)}) async-start(bf16[128,4,512]{2,1,0:T(4,128)(2,1)} %reshape.19), calls=%async_computation | async-start | bytes 1048576 | tf_op jit(solution)/shard_map/all_to_all | solution.py:211
  24.3 0.9 reshape.21
  25.3 19.7 %all-to-all-done = bf16[128,4,512]{2,1,0:T(4,128)(2,1)S(1)} async-done(((bf16[128,4,512]{2,1,0:T(4,128)(2,1)}), bf16[128,4,512]{2,1,0:T(4,128)(2,1)S(1)}, u32[]{:S(2)}, u32[]{:S(2)}) %all-to-all-start) | async-done | bytes 524320 | tf_op jit(solution)/shard_map/all_to_all | solution.py:211
  45.0 5.4 %all-to-all-start.2 = ((bf16[128,4,512]{2,1,0:T(4,128)(2,1)}), bf16[128,4,512]{2,1,0:T(4,128)(2,1)S(1)}, u32[]{:S(2)}, u32[]{:S(2)}) async-start(bf16[128,4,512]{2,1,0:T(4,128)(2,1)} %reshape.21), calls=%async_computation.2 | async-start | bytes 1048576 | tf_op jit(solution)/shard_map/all_to_all | solution.py:211
  50.4 0.1 reshape.20.dy_ref
  50.6 0.0 copy-done.5
  50.6 2.4 hidden.1
  53.0 18.0 %all-to-all-done.2 = bf16[128,4,512]{2,1,0:T(4,128)(2,1)S(1)} async-done(((bf16[128,4,512]{2,1,0:T(4,128)(2,1)}), bf16[128,4,512]{2,1,0:T(4,128)(2,1)S(1)}, u32[]{:S(2)}, u32[]{:S(2)}) %all-to-all-start.2) | async-done | bytes 524320 | tf_op jit(solution)/shard_map/all_to_all | solution.py:211
  71.0 12.3 %all-to-all-start.1 = ((bf16[8,512,128]{2,1,0:T(8,128)(2,1)}), bf16[8,512,128]{2,1,0:T(8,128)(2,1)S(1)}, u32[]{:S(2)}, u32[]{:S(2)}) async-start(bf16[8,512,128]{2,1,0:T(8,128)(2,1)} %hidden.1), calls=%async_computation.1 | async-start | bytes 2097152 | tf_op jit(solution)/shard_map/all_to_all | solution.py:214
  83.3 0.9 reshape.22.x_ref
  84.3 0.0 copy-start
  84.3 1.2 copy-done
  85.5 0.0 copy-start.2
  85.5 1.2 copy-done.2
  86.7 0.0 copy-start.4
  86.7 1.0 copy-done.4
  87.7 2.1 gate_up.1
  89.9 22.8 %all-to-all-done.1.h_ref = bf16[8,512,128]{2,1,0:T(8,128)(2,1)S(1)} async-done(((bf16[8,512,128]{2,1,0:T(8,128)(2,1)}), bf16[8,512,128]{2,1,0:T(8,128)(2,1)S(1)}, u32[]{:S(2)}, u32[]{:S(2)}) %all-to-all-start.1) | async-done | bytes 1048608 | tf_op jit(solution)/shard_map/all_to_all | solution.py:214
  112.7 54.0 %all_to_all.30.g_ref.u_ref = bf16[8,1024,128]{2,1,0:T(8,128)(2,1)S(1)} all-to-all(bf16[8,1024,128]{2,1,0:T(8,128)(2,1)S(1)} %gate_up.1), channel_id=1, replica_groups=mesh['rep'=8,'outer'=8,'local'=16] {'rep'}, dimensions={0} | all-to-all | bytes 4194304 | tf_op jit(solution)/shard_map/all_to_all | solution.py:214
  166.7 0.8 activate.1
  167.5 0.1 broadcast_in_dim.2
  167.6 0.0 copy-start.1
  167.7 0.0 copy-start.3
  167.7 53.6 %all_to_all.31.r_ref = bf16[8,512,256]{2,1,0:T(8,128)(2,1)S(1)} all-to-all(bf16[8,512,256]{2,1,0:T(8,128)(2,1)S(1)} %broadcast_in_dim.2), channel_id=1, replica_groups=mesh['rep'=8,'outer'=8,'local'=16] {'rep'}, dimensions={0} | all-to-all | bytes 4194304 | tf_op jit(solution)/shard_map/all_to_all | solution.py:214
  221.3 0.0 copy-done.1
  221.3 0.0 copy-done.3
  221.3 3.6 %row_grad.1 = bf16[512,512]{1,0:T(8,128)(2,1)S(1)} custom-call(bf16[8,512,256]{2,1,0:T(8,128)(2,1)S(1)} %all_to_all.31.r_ref, bf16[1,512,1024]{2,1,0:T(8,128)(2,1)S(1)} %copy-done.1, bf16[1,512,1024]{2,1,0:T(8,128)(2,1)S(1)} %copy-done.3), custom_call_target="tpu_custom_call" | custom-call | tf_op jit(solution)/shard_map/row_grad/pallas_call | solution.py:185
  224.9 0.1 reshape.23
  225.0 26.3 %all_to_all.32 = bf16[128,4,512]{2,1,0:T(4,128)(2,1)S(1)} all-to-all(bf16[128,4,512]{2,1,0:T(4,128)(2,1)S(1)} %reshape.23), channel_id=1, replica_groups=mesh['rep'=8,'outer'=8,'local'=16] {'outer','local'}, dimensions={0} | all-to-all | bytes 1048576 | tf_op jit(solution)/shard_map/all_to_all | solution.py:211
  251.3 0.1 reshape.24
  251.4 0.8 convolution_convert_fusion
Async XLA Ops:
  0.0 0.8 copy-start.6
  0.8 0.8 copy-start.7
  1.5 0.7 copy-start.8
  2.2 0.7 copy-start.9
  4.9 45.7 %copy-start.5 = (bf16[1,1024,512]{2,1,0:T(8,128)(2,1)S(1)}, bf16[1,1024,512]{2,1,0:T(8,128)(2,1)}, u32[]{:S(2)}) copy-start(bf16[1,1024,512]{2,1,0:T(8,128)(2,1)} %w_ref.1) | copy-start | bytes 3145732
  4.9 40.2 %all-to-all-start = ((bf16[128,4,512]{2,1,0:T(4,128)(2,1)}), bf16[128,4,512]{2,1,0:T(4,128)(2,1)S(1)}, u32[]{:S(2)}, u32[]{:S(2)}) async-start(bf16[128,4,512]{2,1,0:T(4,128)(2,1)} %reshape.19), calls=%async_computation | async-start | bytes 1048576 | tf_op jit(solution)/shard_map/all_to_all | solution.py:211
  45.0 26.0 %all-to-all-start.2 = ((bf16[128,4,512]{2,1,0:T(4,128)(2,1)}), bf16[128,4,512]{2,1,0:T(4,128)(2,1)S(1)}, u32[]{:S(2)}, u32[]{:S(2)}) async-start(bf16[128,4,512]{2,1,0:T(4,128)(2,1)} %reshape.21), calls=%async_computation.2 | async-start | bytes 1048576 | tf_op jit(solution)/shard_map/all_to_all | solution.py:211
  71.0 41.6 %all-to-all-start.1 = ((bf16[8,512,128]{2,1,0:T(8,128)(2,1)}), bf16[8,512,128]{2,1,0:T(8,128)(2,1)S(1)}, u32[]{:S(2)}, u32[]{:S(2)}) async-start(bf16[8,512,128]{2,1,0:T(8,128)(2,1)} %hidden.1), calls=%async_computation.1 | async-start | bytes 2097152 | tf_op jit(solution)/shard_map/all_to_all | solution.py:214
  84.3 1.2 copy-start
  85.5 1.2 copy-start.2
  86.7 1.0 copy-start.4
  167.6 53.6 %copy-start.1 = (bf16[1,512,1024]{2,1,0:T(8,128)(2,1)S(1)}, bf16[1,512,1024]{2,1,0:T(8,128)(2,1)}, u32[]{:S(2)}) copy-start(bf16[1,512,1024]{2,1,0:T(8,128)(2,1)} %wg_ref.3) | copy-start | bytes 3145732
  167.7 53.6 %copy-start.3 = (bf16[1,512,1024]{2,1,0:T(8,128)(2,1)S(1)}, bf16[1,512,1024]{2,1,0:T(8,128)(2,1)}, u32[]{:S(2)}) copy-start(bf16[1,512,1024]{2,1,0:T(8,128)(2,1)} %wu_ref.3) | copy-start | bytes 3145732

commit v2 on v1

--- a/solution.py
+++ b/solution.py
@@ -96,102 +96,113 @@
 
 
 def gate_up_kernel(x_ref, wg_ref, wu_ref, out_ref):
-    part = out_ref.shape[2]
-    rows = x_ref.shape[0]
-    gate = jnp.dot(x_ref[...], wg_ref[0], preferred_element_type=F32)
-    up = jnp.dot(x_ref[...], wu_ref[0], preferred_element_type=F32)
-    for j in range(out_ref.shape[0]):
-        out_ref[j, :rows] = gate[:, j * part : (j + 1) * part].astype(BF16)
-        out_ref[j, rows:] = up[:, j * part : (j + 1) * part].astype(BF16)
+    part = wg_ref.shape[2]
+    out_ref[0, :, :part] = jnp.dot(x_ref[...], wg_ref[0], preferred_element_type=F32)
+    out_ref[0, :, part:] = jnp.dot(x_ref[...], wu_ref[0], preferred_element_type=F32)
 
 
 def gate_up_parts(x_rows, w_gate, w_up, n_rep):
     rows, width = x_rows.shape
     part = w_gate.shape[2] // n_rep
-    per = 2
-    w_spec = pl.BlockSpec((1, width, per * part), lambda c: (0, 0, c))
+    w_spec = pl.BlockSpec((1, width, part), lambda c: (0, 0, c))
     return pl.pallas_call(
         gate_up_kernel,
-        grid=(n_rep // per,),
+        grid=(n_rep,),
         in_specs=[pl.BlockSpec((rows, width), lambda c: (0, 0)), w_spec, w_spec],
-        out_specs=pl.BlockSpec((per, 2 * rows, part), lambda c: (c, 0, 0)),
-        out_shape=jax.ShapeDtypeStruct((n_rep, 2 * rows, part), BF16),
+        out_specs=pl.BlockSpec((1, rows, 2 * part), lambda c: (c, 0, 0)),
+        out_shape=jax.ShapeDtypeStruct((n_rep, rows, 2 * part), F32),
         compiler_params=params(),
         name="gate_up",
     )(x_rows, w_gate, w_up)
 
 
-def activate_kernel(h_ref, g_ref, u_ref, out_ref):
+def activate_kernel(h_ref, gu_ref, out_ref):
     part = h_ref.shape[2]
     hidden = jnp.sum(h_ref[...].astype(F32), axis=0)
-    gate = jnp.sum(g_ref[...].astype(F32), axis=0)
-    up = jnp.sum(u_ref[...].astype(F32), axis=0)
+    gate = gu_ref[:, :part]
+    up = gu_ref[:, part:]
     s = jax.nn.sigmoid(gate)
     out_ref[:, :part] = (hidden * up * s * (1.0 + gate * (1.0 - s))).astype(BF16)
     out_ref[:, part:] = (hidden * gate * s).astype(BF16)
 
 
-def activate(hid, gu):
+def activate(hid, gate_up):
     n_rep, rows, part = hid.shape
     block = 128
-    blocks = rows // block
     return pl.pallas_call(
         activate_kernel,
-        grid=(blocks,),
+        grid=(rows // block,),
         in_specs=[
             pl.BlockSpec((n_rep, block, part), lambda i: (0, i, 0)),
-            pl.BlockSpec((n_rep, block, part), lambda i: (0, i, 0)),
-            pl.BlockSpec((n_rep, block, part), lambda i: (0, blocks + i, 0)),
+            pl.BlockSpec((block, 2 * part), lambda i: (i, 0)),
         ],
         out_specs=pl.BlockSpec((block, 2 * part), lambda i: (i, 0)),
         out_shape=jax.ShapeDtypeStruct((rows, 2 * part), BF16),
         compiler_params=params(),
         name="activate",
-    )(hid, gu, gu)
-
-
-def row_grad_kernel(r_ref, wg_ref, wu_ref, out_ref, acc_ref):
-    c = pl.program_id(0)
-    part = r_ref.shape[2] // 2
-    total = None
-    for j in range(r_ref.shape[0]):
-        cols = slice(j * part, (j + 1) * part)
-        term = lax.dot_general(
-            r_ref[j, :, :part], wg_ref[0, :, cols], TRANS_B, preferred_element_type=F32
-        ) + lax.dot_general(
-            r_ref[j, :, part:], wu_ref[0, :, cols], TRANS_B, preferred_element_type=F32
-        )
+    )(hid, gate_up)
+
+
+def row_grad_kernel(offsets, has_start, n_rep, me_ref, *refs):
+    blocks = refs[: len(offsets)]
+    wg_ref, wu_ref = refs[len(offsets) : len(offsets) + 2]
+    out_ref = refs[-1]
+    part = blocks[0].shape[1] // 2
+    total = refs[-2][...] if has_start else None
+    for offset, block in zip(offsets, blocks):
+        c = lax.rem(me_ref[0] + offset, n_rep)
+        cols = pl.ds(pl.multiple_of(c * part, part), part)
+        weights = jnp.concatenate([wg_ref[0, :, cols], wu_ref[0, :, cols]], axis=1)
+        term = lax.dot_general(block[...], weights, TRANS_B, preferred_element_type=F32)
         total = term if total is None else total + term
-
-    @pl.when(c == 0)
-    def _():
-        acc_ref[...] = total
-
-    @pl.when(c > 0)
-    def _():
-        acc_ref[...] += total
-
-    @pl.when(c == pl.num_programs(0) - 1)
-    def _():
-        out_ref[...] = acc_ref[...].astype(BF16)
-
-
-def row_grad(rows_all, w_gate, w_up):
-    n_rep, rows, part2 = rows_all.shape
-    part = part2 // 2
+    out_ref[...] = total.astype(out_ref.dtype)
+
+
+def row_grad(me, blocks, offsets, w_gate, w_up, n_rep, start, dtype, name):
+    rows = blocks[0].shape[0]
     width = w_gate.shape[1]
-    per = 2
-    w_spec = pl.BlockSpec((1, width, per * part), lambda c: (0, 0, c))
-    return pl.pallas_call(
-        row_grad_kernel,
-        grid=(n_rep // per,),
-        in_specs=[pl.BlockSpec((per, rows, part2), lambda c: (c, 0, 0)), w_spec, w_spec],
-        out_specs=pl.BlockSpec((rows, width), lambda c: (0, 0)),
-        out_shape=jax.ShapeDtypeStruct((rows, width), BF16),
-        scratch_shapes=[pltpu.VMEM((rows, width), F32)],
-        compiler_params=params(),
-        name="row_grad",
-    )(rows_all, w_gate, w_up)
+    vmem = pl.BlockSpec(memory_space=pltpu.VMEM)
+    extra = () if start is None else (start,)
+    return pl.pallas_call(
+        lambda *refs: row_grad_kernel(offsets, start is not None, n_rep, *refs),
+        in_specs=[pl.BlockSpec(memory_space=pltpu.SMEM)]
+        + [vmem] * (len(blocks) + 2 + len(extra)),
+        out_specs=vmem,
+        out_shape=jax.ShapeDtypeStruct((rows, width), dtype),
+        compiler_params=params(),
+        name=name,
+    )(me, *blocks, w_gate, w_up, *extra)
+
+
+def gather_matmul(own, w_gate, w_up, n_rep):
+    me = lax.axis_index("rep").astype(jnp.int32).reshape(1)
+
+    def shift(rows, by):
+        return lax.ppermute(rows, "rep", [(i, (i + by) % n_rep) for i in range(n_rep)])
+
+    blocks, offsets = [own], [0]
+    up = down = own
+    for step in range(1, n_rep // 2):
+        up, down = shift(up, 1), shift(down, -1)
+        blocks += [up, down]
+        offsets += [n_rep - step, step]
+    half = own.shape[0] // 2
+    far = jnp.concatenate([shift(up[:half], 1), shift(down[half:], -1)])
+    early = len(blocks) - 2
+    total = row_grad(
+        me, blocks[:early], offsets[:early], w_gate, w_up, n_rep, None, F32, "row_grad_a"
+    )
+    return row_grad(
+        me,
+        blocks[early:] + [far],
+        offsets[early:] + [n_rep // 2],
+        w_gate,
+        w_up,
+        n_rep,
+        total,
+        BF16,
+        "row_grad_b",
+    )
 
 
 def per_device(tokens, out_grad, expert_ids, route_weights, gate_weight, up_weight, down_weight):
@@ -213,13 +224,14 @@
     def over_rep(parts):
         return lax.all_to_all(parts, "rep", 0, 0, tiled=True)
 
+    x_rows = exchange(send_x)
+    gate_up = lax.psum_scatter(
+        gate_up_parts(x_rows, gate_weight, up_weight, n_rep), "rep", scatter_dimension=0
+    )
     dy_rows = exchange(send_dy)
-    x_rows = exchange(send_x)
     hid = over_rep(hidden_parts(dy_rows, down_weight, n_rep))
-    gu = over_rep(gate_up_parts(x_rows, gate_weight, up_weight, n_rep))
-    own = activate(hid, gu)
-    rows_all = over_rep(jnp.broadcast_to(own[None], (n_rep,) + own.shape))
-    returned = exchange(row_grad(rows_all, gate_weight, up_weight))
+    own = activate(hid, gate_up)
+    returned = exchange(gather_matmul(own, gate_weight, up_weight, n_rep))
     return jnp.dot(per_token_t, returned, preferred_element_type=F32).astype(BF16)
 
 

time: 253 us -> 230 us (0.909)
  waiting for transfers between devices: 60.5 us -> 9.75 us
  blocking collectives: 134 us -> 156 us
  between operations: 0.11 us -> 13.6 us
  starting transfers between devices: 37.1 us -> 25.9 us
  local copies, waits for them, and re-layouts: 9.72 us -> 12.4 us
    all_to_all x1 -> x3, blocking collectives: 26.3 us -> 103 us  [exchange(): return lax.all_to_all(blocks, both, 0, 0, tiled=True).reshape(slots, width)]
    all_to_all x3 -> x0, waiting for transfers between devices: 60.5 us -> none  [the longest x2 37.7 us: exchange(): return lax.all_to_all(blocks, both, 0, 0, tiled=True).reshape(slots, width)]
    all_to_all x2 -> x1, blocking collectives: 108 us -> 53.2 us  [over_rep(): return lax.all_to_all(parts, 'rep', 0, 0, tiled=True)]
    all_to_all x3 -> x0, starting transfers between devices: 37.1 us -> none  [the longest x2 24.9 us: exchange(): return lax.all_to_all(blocks, both, 0, 0, tiled=True).reshape(slots, width)]
    ppermute x0 -> x8, starting transfers between devices: none -> 25.9 us  [shift(): lax.ppermute(rows, 'rep', [(i, (i + by) % n_rep) for i in range(n_rep)])]
    ppermute x0 -> x8, waiting for transfers between devices: none -> 7.85 us  [shift(): lax.ppermute(rows, 'rep', [(i, (i + by) % n_rep) for i in range(n_rep)])]
    unnamed x20 -> x28, local copies, waits for them, and re-layouts: 6.39 us -> 10.3 us
    pallas_call x3 -> x4, Pallas kernels: 6.49 us -> 7.71 us  [the longest x1 5.77 us: gate_up_parts(): pl.pallas_call(gate_up_kernel, grid=(n_rep,), in_specs=[pl.BlockSpec((row...]
  transfers between devices with their start and end apart: 3 -> 9, of which waited for: 3 -> 4; matrix products, arithmetic and copies ran while one was open for 1% -> 1% of each run, Pallas kernels for 2% -> 1%
where the time goes in v2:
time: 230 us; the launch traced here: 229 us
  blocking collectives  156 us (68%)
  starting transfers between devices  25.9 us (11%)
  between operations  13.6 us (6%)
  local copies, waits for them, and re-layouts  12.4 us (5%)
  Pallas kernels  10.1 us (4%)
  waiting for transfers between devices  9.75 us (4%)
    all_to_all x3, blocking collectives, exchange(): return lax.all_to_all(blocks, both, 0, 0, tiled=True).reshape(slots, width)  103 us
    all_to_all x1, blocking collectives, over_rep(): return lax.all_to_all(parts, 'rep', 0, 0, tiled=True)  53.2 us
    ppermute x8, starting transfers between devices, shift(): lax.ppermute(rows, 'rep', [(i, (i + by) % n_rep) for i in range(n_rep)])  25.9 us
    unnamed x28, local copies, waits for them, and re-layouts  10.3 us
    ppermute x8, waiting for transfers between devices, shift(): lax.ppermute(rows, 'rep', [(i, (i + by) % n_rep) for i in range(n_rep)])  7.85 us
    pallas_call x1, Pallas kernels, gate_up_parts(): pl.pallas_call(gate_up_kernel, grid=(n_rep,), in_specs=[pl.BlockSpec((row...  5.77 us
  transfers between devices with their start and end apart: 9, of which 4 were waited for; matrix products, arithmetic and copies ran while one was open for 1% of the time, Pallas kernels for 1%

profile of v2, /device:TPU:1, one launch (start us, length us, event | category | flops | bytes accessed | tf_op | source)
XLA Modules:
  0.0 229.5 jit_solution(16452309141606420875)
XLA Ops:
  6.5 0.0 reduce-scatter.2.cloned.1.call-start
  6.5 0.0 copy-start.10
  6.5 0.8 copy-done.10
  7.3 0.0 copy-start.11
  7.3 0.8 copy-done.11
  8.1 0.0 copy-start.12
  8.1 0.7 copy-done.12
  8.7 0.0 copy-start.13
  8.7 0.7 copy-done.13
  9.4 1.1 route.1
  10.5 0.1 reshape.24
  10.6 39.4 %all_to_all.20 = bf16[128,4,512]{2,1,0:T(4,128)(2,1)S(1)} all-to-all(bf16[128,4,512]{2,1,0:T(4,128)(2,1)S(1)} %reshape.24), channel_id=1, replica_groups=mesh['rep'=8,'outer'=8,'local'=16] {'outer','local'}, dimensions={0} | all-to-all | bytes 1048576 | tf_op jit(solution)/shard_map/all_to_all | solution.py:222
  50.0 0.1 reshape.25.x_ref
  50.1 0.0 copy-start
  50.1 1.2 copy-done
  51.3 0.0 copy-start.2
  51.3 1.2 copy-done.2
  52.6 5.8 %gate_up.1 = f32[8,512,256]{2,1,0:T(8,128)} custom-call(bf16[512,512]{1,0:T(8,128)(2,1)S(1)} %reshape.25.x_ref, bf16[1,512,1024]{2,1,0:T(8,128)(2,1)S(1)} %copy-done, bf16[1,512,1024]{2,1,0:T(8,128)(2,1)S(1)} %copy-done.2), custom_call_target="tpu_custom_call" | custom-call | tf_op jit(solution)/shard_map/gate_up/pallas_call | solution.py:108
  58.3 0.0 reduce-scatter.2.cloned.1.call-update
  58.4 0.1 reshape.22
  58.5 25.8 %all_to_all.21 = bf16[128,4,512]{2,1,0:T(4,128)(2,1)S(1)} all-to-all(bf16[128,4,512]{2,1,0:T(4,128)(2,1)S(1)} %reshape.22), channel_id=1, replica_groups=mesh['rep'=8,'outer'=8,'local'=16] {'outer','local'}, dimensions={0} | all-to-all | bytes 1048576 | tf_op jit(solution)/shard_map/all_to_all | solution.py:222
  84.3 0.0 copy-start.1
  84.3 0.0 copy-start.3
  84.3 0.1 reshape.23.dy_ref
  84.4 0.0 copy-start.4
  84.4 1.4 copy-done.4
  85.8 1.4 hidden.1
  87.2 53.2 %all_to_all.22.h_ref = bf16[8,512,128]{2,1,0:T(8,128)(2,1)S(1)} all-to-all(bf16[8,512,128]{2,1,0:T(8,128)(2,1)S(1)} %hidden.1), channel_id=1, replica_groups=mesh['rep'=8,'outer'=8,'local'=16] {'rep'}, dimensions={0} | all-to-all | bytes 2097152 | tf_op jit(solution)/shard_map/all_to_all | solution.py:225
  140.4 1.9 reduce-scatter.2.cloned.1.call-done
  142.3 1.0 copy-done.5
  143.3 0.4 activate.1.refs_1_
  143.7 1.9 collective-permute-start
  145.6 4.6 %collective-permute-start.3 = (bf16[512,256]{1,0:T(8,128)(2,1)S(1)}, bf16[512,256]{1,0:T(8,128)(2,1)S(1)}, u32[]{:S(2)}, u32[]{:S(2)}) collective-permute-start(bf16[512,256]{1,0:T(8,128)(2,1)S(1)} %activate.1.refs_1_), channel_id=1, source_target_pairs={{0,896},{128,0},{256,128},{384,256},{512,384},{640,512},{768,640},... | collective-permute-start | bytes 786440 | tf_op jit(solution)/shard_map/ppermute | solution.py:181
  150.2 3.8 %collective-permute-done.refs_2_ = bf16[512,256]{1,0:T(8,128)(2,1)S(1)} collective-permute-done((bf16[512,256]{1,0:T(8,128)(2,1)S(1)}, bf16[512,256]{1,0:T(8,128)(2,1)S(1)}, u32[]{:S(2)}, u32[]{:S(2)}) %collective-permute-start) | collective-permute-done | bytes 262176 | tf_op jit(solution)/shard_map/ppermute | solution.py:181
  154.0 1.9 collective-permute-start.1
  155.9 0.0 collective-permute-done.3.refs_3_
  156.0 4.6 %collective-permute-start.4 = (bf16[512,256]{1,0:T(8,128)(2,1)S(1)}, bf16[512,256]{1,0:T(8,128)(2,1)S(1)}, u32[]{:S(2)}, u32[]{:S(2)}) collective-permute-start(bf16[512,256]{1,0:T(8,128)(2,1)S(1)} %collective-permute-done.3.refs_3_), channel_id=1, source_target_pairs={{0,896},{128,0},{256,128},{384,256},{512,384},{640,512},{768,640},... | collective-permute-start | bytes 786440 | tf_op jit(solution)/shard_map/ppermute | solution.py:181
  160.5 2.9 %collective-permute-done.1.refs_4_ = bf16[512,256]{1,0:T(8,128)(2,1)S(1)} collective-permute-done((bf16[512,256]{1,0:T(8,128)(2,1)S(1)}, bf16[512,256]{1,0:T(8,128)(2,1)S(1)}, u32[]{:S(2)}, u32[]{:S(2)}) %collective-permute-start.1) | collective-permute-done | bytes 262176 | tf_op jit(solution)/shard_map/ppermute | solution.py:181
  163.4 1.9 collective-permute-start.2
  165.3 0.0 copy-start.6
  165.4 0.7 copy-done.6
  166.0 0.0 collective-permute-done.4.refs_5_
  166.1 4.6 %collective-permute-start.5 = (bf16[512,256]{1,0:T(8,128)(2,1)S(1)}, bf16[512,256]{1,0:T(8,128)(2,1)S(1)}, u32[]{:S(2)}, u32[]{:S(2)}) collective-permute-start(bf16[512,256]{1,0:T(8,128)(2,1)S(1)} %collective-permute-done.4.refs_5_), channel_id=1, source_target_pairs={{0,896},{128,0},{256,128},{384,256},{512,384},{640,512},{768,640},... | collective-permute-start | bytes 786440 | tf_op jit(solution)/shard_map/ppermute | solution.py:181
  170.6 1.1 collective-permute-done.2.refs_1_
  171.7 0.7 slice.8
  172.4 1.9 collective-permute-start.6
  174.3 0.0 collective-permute-done.5.refs_2_
  174.3 0.0 copy-done.8
  174.3 0.7 slice.9
  175.0 4.6 %collective-permute-start.7 = (bf16[256,256]{1,0:T(8,128)(2,1)}, bf16[256,256]{1,0:T(8,128)(2,1)}, u32[]{:S(2)}, u32[]{:S(2)}) collective-permute-start(bf16[256,256]{1,0:T(8,128)(2,1)} %slice.9), channel_id=1, source_target_pairs={{0,896},{128,0},{256,128},{384,256},{512,384},{640,512},{768,640},... | collective-permute-start | bytes 393224 | tf_op jit(solution)/shard_map/ppermute | solution.py:181
  179.6 0.0 copy-done.1
  179.6 0.0 copy-done.3
  179.6 0.0 copy-start.7
  179.6 0.9 copy-done.7
  180.6 0.9 copy-done.9
  181.5 0.9 row_grad_a.1.refs_6_
  182.4 0.0 collective-permute-done.6
  182.4 0.0 collective-permute-done.7
  182.4 1.0 pad_maximum_fusion.refs_3_
  183.4 0.6 row_grad_b.1
  184.1 0.1 reshape.26
  184.2 37.5 %all_to_all.23 = bf16[128,4,512]{2,1,0:T(4,128)(2,1)S(1)} all-to-all(bf16[128,4,512]{2,1,0:T(4,128)(2,1)S(1)} %reshape.26), channel_id=1, replica_groups=mesh['rep'=8,'outer'=8,'local'=16] {'outer','local'}, dimensions={0} | all-to-all | bytes 1048576 | tf_op jit(solution)/shard_map/all_to_all | solution.py:222
  221.7 0.1 reshape.27
  221.8 0.8 convolution_convert_fusion
  (3 shorter events, 0.0 us)
Async XLA Ops:
  6.5 135.7 %reduce-scatter.2.cloned.1.call-start = ((), (), s32[]{:S(2)}) async-start(), calls=%async_computation.5 | async-start | bytes 4718592 | tf_op jit(solution)/shard_map/reduce_scatter | solution.py:228
  6.5 0.8 copy-start.10
  7.3 0.8 copy-start.11
  8.1 0.7 copy-start.12
  8.7 0.7 copy-start.13
  50.1 1.2 copy-start
  51.3 1.2 copy-start.2
  84.3 95.3 %copy-start.1 = (bf16[1,512,1024]{2,1,0:T(8,128)(2,1)S(1)}, bf16[1,512,1024]{2,1,0:T(8,128)(2,1)}, u32[]{:S(2)}) copy-start(bf16[1,512,1024]{2,1,0:T(8,128)(2,1)} %refs_4_.1) | copy-start | bytes 3145732
  84.3 95.3 %copy-start.3 = (bf16[1,512,1024]{2,1,0:T(8,128)(2,1)S(1)}, bf16[1,512,1024]{2,1,0:T(8,128)(2,1)}, u32[]{:S(2)}) copy-start(bf16[1,512,1024]{2,1,0:T(8,128)(2,1)} %refs_5_.1) | copy-start | bytes 3145732
  84.4 1.4 copy-start.4
  142.3 1.0 copy-start.5
  143.7 10.3 %collective-permute-start = (bf16[512,256]{1,0:T(8,128)(2,1)S(1)}, bf16[512,256]{1,0:T(8,128)(2,1)S(1)}, u32[]{:S(2)}, u32[]{:S(2)}) collective-permute-start(bf16[512,256]{1,0:T(8,128)(2,1)S(1)} %activate.1.refs_1_), channel_id=1, source_target_pairs={{0,128},{128,256},{256,384},{384,512},{512,640},{640,768},{768,896... | collective-permute-start | bytes 786440 | tf_op jit(solution)/shard_map/ppermute | solution.py:181
  145.6 10.3 %collective-permute-start.3 = (bf16[512,256]{1,0:T(8,128)(2,1)S(1)}, bf16[512,256]{1,0:T(8,128)(2,1)S(1)}, u32[]{:S(2)}, u32[]{:S(2)}) collective-permute-start(bf16[512,256]{1,0:T(8,128)(2,1)S(1)} %activate.1.refs_1_), channel_id=1, source_target_pairs={{0,896},{128,0},{256,128},{384,256},{512,384},{640,512},{768,640},... | collective-permute-start | bytes 786440 | tf_op jit(solution)/shard_map/ppermute | solution.py:181
  154.0 9.4 %collective-permute-start.1 = (bf16[512,256]{1,0:T(8,128)(2,1)S(1)}, bf16[512,256]{1,0:T(8,128)(2,1)S(1)}, u32[]{:S(2)}, u32[]{:S(2)}) collective-permute-start(bf16[512,256]{1,0:T(8,128)(2,1)S(1)} %collective-permute-done.refs_2_), channel_id=1, source_target_pairs={{0,128},{128,256},{256,384},{384,512},{512,640},{640,768},{768,896... | collective-permute-start | bytes 786440 | tf_op jit(solution)/shard_map/ppermute | solution.py:181
  156.0 10.1 %collective-permute-start.4 = (bf16[512,256]{1,0:T(8,128)(2,1)S(1)}, bf16[512,256]{1,0:T(8,128)(2,1)S(1)}, u32[]{:S(2)}, u32[]{:S(2)}) collective-permute-start(bf16[512,256]{1,0:T(8,128)(2,1)S(1)} %collective-permute-done.3.refs_3_), channel_id=1, source_target_pairs={{0,896},{128,0},{256,128},{384,256},{512,384},{640,512},{768,640},... | collective-permute-start | bytes 786440 | tf_op jit(solution)/shard_map/ppermute | solution.py:181
  163.4 8.3 %collective-permute-start.2 = (bf16[512,256]{1,0:T(8,128)(2,1)S(1)}, bf16[512,256]{1,0:T(8,128)(2,1)S(1)}, u32[]{:S(2)}, u32[]{:S(2)}) collective-permute-start(bf16[512,256]{1,0:T(8,128)(2,1)S(1)} %collective-permute-done.1.refs_4_), channel_id=1, source_target_pairs={{0,128},{128,256},{256,384},{384,512},{512,640},{640,768},{768,896... | collective-permute-start | bytes 786440 | tf_op jit(solution)/shard_map/ppermute | solution.py:181
  165.3 0.7 copy-start.6
  166.0 8.3 %copy-start.8 = (bf16[512,256]{1,0:T(8,128)(2,1)}, bf16[512,256]{1,0:T(8,128)(2,1)S(1)}, u32[]{:S(2)}) copy-start(bf16[512,256]{1,0:T(8,128)(2,1)S(1)} %collective-permute-done.4.refs_5_) | copy-start | bytes 786436
  166.1 8.3 %collective-permute-start.5 = (bf16[512,256]{1,0:T(8,128)(2,1)S(1)}, bf16[512,256]{1,0:T(8,128)(2,1)S(1)}, u32[]{:S(2)}, u32[]{:S(2)}) collective-permute-start(bf16[512,256]{1,0:T(8,128)(2,1)S(1)} %collective-permute-done.4.refs_5_), channel_id=1, source_target_pairs={{0,896},{128,0},{256,128},{384,256},{512,384},{640,512},{768,640},... | collective-permute-start | bytes 786440 | tf_op jit(solution)/shard_map/ppermute | solution.py:181
  172.4 10.0 %collective-permute-start.6 = (bf16[256,256]{1,0:T(8,128)(2,1)}, bf16[256,256]{1,0:T(8,128)(2,1)}, u32[]{:S(2)}, u32[]{:S(2)}) collective-permute-start(bf16[256,256]{1,0:T(8,128)(2,1)} %slice.8), channel_id=1, source_target_pairs={{0,128},{128,256},{256,384},{384,512},{512,640},{640,768},{768,896... | collective-permute-start | bytes 393224 | tf_op jit(solution)/shard_map/ppermute | solution.py:181
  175.0 7.4 %collective-permute-start.7 = (bf16[256,256]{1,0:T(8,128)(2,1)}, bf16[256,256]{1,0:T(8,128)(2,1)}, u32[]{:S(2)}, u32[]{:S(2)}) collective-permute-start(bf16[256,256]{1,0:T(8,128)(2,1)} %slice.9), channel_id=1, source_target_pairs={{0,896},{128,0},{256,128},{384,256},{512,384},{640,512},{768,640},... | collective-permute-start | bytes 393224 | tf_op jit(solution)/shard_map/ppermute | solution.py:181
  179.6 1.0 copy-start.7
  180.6 0.9 copy-start.9
Sparse Core Ops, SparseCore 0:
  58.5 83.7 reduce-scatter.1

commit v3 on v2

v3 whole, which is shorter than its diff:
```python
import jax
import jax.numpy as jnp
from jax import lax
from jax.experimental import pallas as pl
from jax.experimental.pallas import tpu as pltpu
from jax.sharding import PartitionSpec as P

F32 = jnp.float32
BF16 = jnp.bfloat16
TRANS_B = (((1,), (1,)), ((), ()))
VMEM_SPEC = pl.BlockSpec(memory_space=pltpu.VMEM)


def params(mib=16):
    return pltpu.CompilerParams(vmem_limit_bytes=mib * 1024 * 1024)


def route_kernel(capacity, ids_hbm, w_hbm, tok_hbm, og_hbm, send_ref, pt_ref, *scratch):
    ids_ref, w_ref, tok_ref, og_ref, scaled_ref, sems = scratch
    copies = [
        pltpu.make_async_copy(src, dst, sems.at[n])
        for n, (src, dst) in enumerate(
            ((ids_hbm, ids_ref), (w_hbm, w_ref), (og_hbm, og_ref), (tok_hbm, tok_ref))
        )
    ]
    for copy in copies:
        copy.start()
    top, tok = ids_ref.shape
    width = tok_ref.shape[1]
    rows = top * tok
    slots = send_ref.shape[0]
    c_row = lax.broadcasted_iota(jnp.int32, (rows, tok), 0)
    pick_i = (c_row % tok == lax.broadcasted_iota(jnp.int32, (rows, tok), 1)).astype(BF16)
    c_k = lax.broadcasted_iota(jnp.int32, (rows, top), 0)
    pick_k = (c_k // tok == lax.broadcasted_iota(jnp.int32, (rows, top), 1)).astype(F32)
    sub = lax.broadcasted_iota(jnp.int32, (rows, rows), 0)
    lane = lax.broadcasted_iota(jnp.int32, (rows, rows), 1)
    order_sub = (sub % tok) * top + sub // tok
    order_lane = (lane % tok) * top + lane // tok
    for copy in copies:
        copy.wait()

    def column(values):
        spread = lax.dot_general(pick_i, values, TRANS_B, preferred_element_type=F32)
        return jnp.sum(spread * pick_k, axis=1, keepdims=True)

    ids_col = column(ids_ref[...].astype(F32).astype(BF16))
    w = w_ref[...]
    w_hi = w.astype(BF16)
    rest = w - w_hi.astype(F32)
    w_mid = rest.astype(BF16)
    w_lo = (rest - w_mid.astype(F32)).astype(BF16)
    w_col = column(w_hi) + (column(w_mid) + column(w_lo))
    ids_row = jnp.sum(jnp.where(sub == lane, ids_col, 0.0), axis=0, keepdims=True)
    earlier = (ids_col == ids_row) & (order_sub < order_lane)
    slot_row = jnp.sum(jnp.where(earlier, 1.0, 0.0), axis=0, keepdims=True)
    code = jnp.where(slot_row < capacity, ids_row * capacity + slot_row, -1.0).astype(jnp.int32)
    table = (lax.broadcasted_iota(jnp.int32, (slots, rows), 0) == code).astype(F32).astype(BF16)
    per_token = jnp.dot(table, pick_i, preferred_element_type=F32).astype(BF16)
    pt_ref[...] = lax.dot_general(
        pick_i, table, (((0,), (1,)), ((), ())), preferred_element_type=F32
    ).astype(BF16)
    og = jnp.dot(pick_i, og_ref[...], preferred_element_type=F32)
    scaled_ref[...] = (w_col * og).astype(BF16)
    send_ref[:, :width] = jnp.dot(
        per_token, tok_ref[...], preferred_element_type=F32
    ).astype(BF16)
    send_ref[:, width:] = jnp.dot(
        table, scaled_ref[...], preferred_element_type=F32
    ).astype(BF16)


def route(tokens, out_grad, expert_ids, route_weights, experts, capacity):
    tok, width = tokens.shape
    top = expert_ids.shape[1]
    slots = experts * capacity
    return pl.pallas_call(
        lambda *refs: route_kernel(capacity, *refs),
        in_specs=[pl.BlockSpec(memory_space=pltpu.HBM)] * 4,
        out_specs=(VMEM_SPEC, VMEM_SPEC),
        out_shape=(
            jax.ShapeDtypeStruct((slots, 2 * width), BF16),
            jax.ShapeDtypeStruct((tok, slots), BF16),
        ),
        scratch_shapes=[
            pltpu.VMEM((top, tok), jnp.int32),
            pltpu.VMEM((top, tok), F32),
            pltpu.VMEM((tok, width), BF16),
            pltpu.VMEM((tok, width), BF16),
            pltpu.VMEM((tok * top, width), BF16),
            pltpu.SemaphoreType.DMA((4,)),
        ],
        compiler_params=params(63),
        name="route",
    )(expert_ids.T, route_weights.T, tokens, out_grad)


def hidden_kernel(rows_ref, w_ref, out_ref):
    part = out_ref.shape[2]
    out = lax.dot_general(rows_ref[...], w_ref[0], TRANS_B, preferred_element_type=F32)
    for j in range(out_ref.shape[0]):
        out_ref[j] = out[:, j * part : (j + 1) * part]


def hidden_parts(both_rows, w_down, n_rep):
    rows = both_rows.shape[0]
    width = both_rows.shape[1] // 2
    part = w_down.shape[1] // n_rep
    per = 2
    return pl.pallas_call(
        hidden_kernel,
        grid=(n_rep // per,),
        in_specs=[
            pl.BlockSpec((rows, width), lambda c: (0, 1)),
            pl.BlockSpec((1, per * part, width), lambda c: (0, c, 0)),
        ],
        out_specs=pl.BlockSpec((per, rows, part), lambda c: (c, 0, 0)),
        out_shape=jax.ShapeDtypeStruct((n_rep, rows, part), F32),
        compiler_params=params(62),
        name="hidden",
    )(both_rows, w_down)


def chunk_weights(me_ref, offset, n_rep, wg_ref, wu_ref):
    part = wg_ref.shape[2] // n_rep
    c = lax.rem(me_ref[0] + offset, n_rep)
    cols = pl.ds(pl.multiple_of(c * part, part), part)
    return jnp.concatenate([wg_ref[0, :, cols], wu_ref[0, :, cols]], axis=1)


def gate_up_kernel(offset, n_rep, me_ref, rows_ref, wg_ref, wu_ref, *refs):
    width = wg_ref.shape[1]
    weights = chunk_weights(me_ref, offset, n_rep, wg_ref, wu_ref)
    total = jnp.dot(rows_ref[:, :width], weights, preferred_element_type=F32)
    for arrived in refs[:-1]:
        total = total + arrived[...].astype(F32)
    refs[-1][...] = total.astype(refs[-1].dtype)


def gate_up(me, both_rows, w_gate, w_up, n_rep, offset, arrived, dtype, name):
    rows = both_rows.shape[0]
    part = w_gate.shape[2] // n_rep
    return pl.pallas_call(
        lambda *refs: gate_up_kernel(offset, n_rep, *refs),
        in_specs=[pl.BlockSpec(memory_space=pltpu.SMEM)] + [VMEM_SPEC] * (3 + len(arrived)),
        out_specs=VMEM_SPEC,
        out_shape=jax.ShapeDtypeStruct((rows, 2 * part), dtype),
        compiler_params=params(),
        name=name,
    )(me, both_rows, w_gate, w_up, *arrived)


def shift(rows, by):
    n_rep = lax.axis_size("rep")
    return lax.ppermute(rows, "rep", [(i, (i + by) % n_rep) for i in range(n_rep)])


def gate_up_sums(me, both_rows, w_gate, w_up, n_rep):
    half = n_rep // 2
    up, down = (), ()
    for hop in range(half, 0, -1):
        term = gate_up(
            me, both_rows, w_gate, w_up, n_rep, hop, up, BF16, "gate_up_rise_%d" % hop
        )
        up = (shift(term, 1),)
        if hop < half:
            term = gate_up(
                me, both_rows, w_gate, w_up, n_rep, n_rep - hop, down, BF16, "gate_up_fall_%d" % hop
            )
            down = (shift(term, -1),)
    own = gate_up(me, both_rows, w_gate, w_up, n_rep, 0, (), F32, "gate_up_own")
    return own, up[0], down[0]


def activate_kernel(h_ref, own_ref, up_ref, down_ref, out_ref):
    part = h_ref.shape[1]
    sums = own_ref[...] + up_ref[...].astype(F32) + down_ref[...].astype(F32)
    hidden = h_ref[...]
    gate = sums[:, :part]
    up = sums[:, part:]
    s = jax.nn.sigmoid(gate)
    out_ref[:, :part] = (hidden * up * s * (1.0 + gate * (1.0 - s))).astype(BF16)
    out_ref[:, part:] = (hidden * gate * s).astype(BF16)


def activate(hidden, own, up, down):
    rows, part2 = own.shape
    block = 128
    spec = pl.BlockSpec((block, part2), lambda i: (i, 0))
    return pl.pallas_call(
        activate_kernel,
        grid=(rows // block,),
        in_specs=[pl.BlockSpec((block, part2 // 2), lambda i: (i, 0)), spec, spec, spec],
        out_specs=spec,
        out_shape=jax.ShapeDtypeStruct(own.shape, BF16),
        compiler_params=params(62),
        name="activate",
    )(hidden, own, up, down)


def row_grad_kernel(offsets, has_start, n_rep, me_ref, *refs):
    blocks = refs[: len(offsets)]
    wg_ref, wu_ref = refs[len(offsets) : len(offsets) + 2]
    out_ref = refs[-1]
    total = refs[-2][...] if has_start else None
    for offset, block in zip(offsets, blocks):
        weights = chunk_weights(me_ref, offset, n_rep, wg_ref, wu_ref)
        term = lax.dot_general(block[...], weights, TRANS_B, preferred_element_type=F32)
        total = term if total is None else total + term
    out_ref[...] = total.astype(out_ref.dtype)


def row_grad(me, blocks, offsets, w_gate, w_up, n_rep, start, dtype, name):
    rows = blocks[0].shape[0]
    width = w_gate.shape[1]
    extra = () if start is None else (start,)
    return pl.pallas_call(
        lambda *refs: row_grad_kernel(offsets, start is not None, n_rep, *refs),
        in_specs=[pl.BlockSpec(memory_space=pltpu.SMEM)]
        + [VMEM_SPEC] * (len(blocks) + 2 + len(extra)),
        out_specs=VMEM_SPEC,
        out_shape=jax.ShapeDtypeStruct((rows, width), dtype),
        compiler_params=params(),
        name=name,
    )(me, *blocks, w_gate, w_up, *extra)


def gather_matmul(me, own, w_gate, w_up, n_rep):
    half = n_rep // 2
    blocks, offsets = [own], [0]
    up = down = own
    for step in range(1, half):
        up, down = shift(up, 1), shift(down, -1)
        blocks += [up, down]
        offsets += [n_rep - step, step]
    last = shift(up, 1)
    total = row_grad(me, blocks, offsets, w_gate, w_up, n_rep, None, F32, "row_grad_near")
    return row_grad(me, [last], [half], w_gate, w_up, n_rep, total, BF16, "row_grad_far")


def per_device(tokens, out_grad, expert_ids, route_weights, gate_weight, up_weight, down_weight):
    tok, width = tokens.shape
    top = expert_ids.shape[1]
    n_rep = lax.axis_size("rep")
    experts = lax.axis_size("outer") * lax.axis_size("local")
    capacity = max(2, 2 * tok * top // experts)
    slots = experts * capacity
    me = lax.axis_index("rep").astype(jnp.int32).reshape(1)
    send, per_token_t = route(tokens, out_grad, expert_ids, route_weights, experts, capacity)

    def exchange(rows):
        blocks = rows.reshape(experts, capacity, rows.shape[1])
        return lax.all_to_all(blocks, ("outer", "local"), 0, 0, tiled=True).reshape(rows.shape)

    both_rows = exchange(send)
    hidden = lax.psum_scatter(
        hidden_parts(both_rows, down_weight, n_rep), "rep", scatter_dimension=0
    )
    sums = gate_up_sums(me, both_rows, gate_weight, up_weight, n_rep)
    own = activate(hidden, *sums)
    returned = exchange(gather_matmul(me, own, gate_weight, up_weight, n_rep))
    return jnp.dot(per_token_t, returned, preferred_element_type=F32).astype(BF16)


def solution(mesh):
    return jax.shard_map(
        per_device,
        mesh=mesh,
        in_specs=(
            P(("outer", "local"), "rep"),
            P(("outer", "local"), "rep"),
            P(("outer", "local"), None),
            P(("outer", "local"), None),
            P(("outer", "local"), "rep", None),
            P(("outer", "local"), "rep", None),
            P(("outer", "local"), None, "rep"),
        ),
        out_specs=P(("outer", "local"), "rep"),
        check_vma=False,
    )
```

time: 230 us -> 216 us (0.939)
  blocking collectives: 156 us -> 87.4 us
  starting transfers between devices: 25.9 us -> 57.1 us
  waiting for transfers between devices: 9.75 us -> 32.2 us
  Pallas kernels: 10.1 us -> 14.7 us
  local copies, waits for them, and re-layouts: 12.4 us -> 9.24 us
    all_to_all x4 -> x2, blocking collectives: 156 us -> 87.4 us  [exchange(): lax.all_to_all(blocks, ('outer', 'local'), 0, 0, tiled=True)]
    ppermute x8 -> x14, starting transfers between devices: 25.9 us -> 57.1 us  [shift(): lax.ppermute(rows, 'rep', [(i, (i + by) % n_rep) for i in range(n_rep)])]
    ppermute x8 -> x14, waiting for transfers between devices: 7.85 us -> 32.2 us  [shift(): lax.ppermute(rows, 'rep', [(i, (i + by) % n_rep) for i in range(n_rep)])]
    unnamed x28 -> x18, local copies, waits for them, and re-layouts: 10.3 us -> 6.42 us
    pallas_call x1, Pallas kernels: 1.36 us -> 4.36 us  [hidden_parts(): pl.pallas_call(hidden_kernel, grid=(n_rep // per,), in_specs=[pl.BlockSpe...]
    pallas_call x1, Pallas kernels: 0.39 us -> 3.3 us  [activate(): pl.pallas_call(activate_kernel, grid=(rows // block,), in_specs=[pl.Block...]
    pallas_call x2 -> x9, Pallas kernels: 6.82 us -> 5.48 us  [the longest x1 2.75 us: route(): pl.pallas_call(lambda *refs: route_kernel(capacity, *refs), in_specs=[pl....]
  transfers between devices with their start and end apart: 9 -> 15, of which waited for: 4 -> 11; matrix products, arithmetic and copies ran while one was open for 1% -> 0% of each run, Pallas kernels for 1% -> 2%
where the time goes in v3:
time: 216 us; the launch traced here: 215 us
  blocking collectives  87.4 us (40%)
  starting transfers between devices  57.1 us (26%)
  waiting for transfers between devices  32.2 us (15%)
  Pallas kernels  14.7 us (7%)
  between operations  13.6 us (6%)
  local copies, waits for them, and re-layouts  9.24 us (4%)
    all_to_all x2, blocking collectives, exchange(): lax.all_to_all(blocks, ('outer', 'local'), 0, 0, tiled=True)  87.4 us
    ppermute x14, starting transfers between devices, shift(): lax.ppermute(rows, 'rep', [(i, (i + by) % n_rep) for i in range(n_rep)])  57.1 us
    ppermute x14, waiting for transfers between devices, shift(): lax.ppermute(rows, 'rep', [(i, (i + by) % n_rep) for i in range(n_rep)])  32.2 us
    unnamed x18, local copies, waits for them, and re-layouts  6.42 us
    pallas_call x1, Pallas kernels, hidden_parts(): pl.pallas_call(hidden_kernel, grid=(n_rep // per,), in_specs=[pl.BlockSpe...  4.36 us
  transfers between devices with their start and end apart: 15, of which 11 were waited for; matrix products, arithmetic and copies ran while one was open for 0% of the time, Pallas kernels for 2%

profile of v3, /device:TPU:1, one launch (start us, length us, event | category | flops | bytes accessed | tf_op | source)
XLA Modules:
  0.0 215.0 jit_solution(7321942881850957581)
XLA Ops:
  6.5 0.0 reduce-scatter.2.cloned.1.call-start
  6.5 2.7 %route.1 = (bf16[512,1024]{1,0:T(8,128)(2,1)}, bf16[32,512]{1,0:T(8,128)(2,1)}) custom-call(s32[8,32]{1,0:T(8,128)} %bitcast.7, f32[8,32]{1,0:T(8,128)} %bitcast.8, bf16[32,512]{1,0:T(8,128)(2,1)} %refs_2_.10, bf16[32,512]{1,0:T(8,128)(2,1)} %refs_3_.10), custom_call_target="tpu_custom_call" | custom-call | tf_op jit(solution)/shard_map/route/pallas_call | solution.py:77
  9.3 1.5 reshape.16
  10.8 49.7 %all_to_all.10 = bf16[128,4,1024]{2,1,0:T(4,128)(2,1)S(1)} all-to-all(bf16[128,4,1024]{2,1,0:T(4,128)(2,1)S(1)} %reshape.16), channel_id=1, replica_groups=mesh['rep'=8,'outer'=8,'local'=16] {'outer','local'}, dimensions={0} | all-to-all | bytes 2097152 | tf_op jit(solution)/shard_map/all_to_all | solution.py:253
  60.5 1.1 reshape.17.rows_ref.refs_1_
  61.6 4.4 %hidden.1 = f32[8,512,128]{2,1,0:T(8,128)} custom-call(bf16[512,1024]{1,0:T(8,128)(2,1)} %reshape.17.rows_ref.refs_1_, bf16[1,1024,512]{2,1,0:T(8,128)(2,1)} %w_ref.1), custom_call_target="tpu_custom_call" | custom-call | tf_op jit(solution)/shard_map/hidden/pallas_call | solution.py:110
  65.9 0.0 copy-start
  65.9 0.0 copy-start.1
  65.9 0.0 reduce-scatter.2.cloned.1.call-update
  66.0 1.2 copy-done
  67.2 0.3 copy-done.1
  67.5 1.2 copy-done.3
  68.7 0.3 gate_up_rise_4.1
  69.1 1.9 collective-permute-start
  71.0 0.3 gate_up_fall_3.1
  71.3 13.4 %collective-permute-start.4 = (bf16[512,256]{1,0:T(8,128)(2,1)S(1)}, bf16[512,256]{1,0:T(8,128)(2,1)S(1)}, u32[]{:S(2)}, u32[]{:S(2)}) collective-permute-start(bf16[512,256]{1,0:T(8,128)(2,1)S(1)} %gate_up_fall_3.1), channel_id=1, source_target_pairs={{0,896},{128,0},{256,128},{384,256},{512,384},{640,512},{768,640},... | collective-permute-start | bytes 786440 | tf_op jit(solution)/shard_map/ppermute | solution.py:155
  84.7 4.8 %collective-permute-done.refs_4_ = bf16[512,256]{1,0:T(8,128)(2,1)S(1)} collective-permute-done((bf16[512,256]{1,0:T(8,128)(2,1)S(1)}, bf16[512,256]{1,0:T(8,128)(2,1)S(1)}, u32[]{:S(2)}, u32[]{:S(2)}) %collective-permute-start) | collective-permute-done | bytes 262176 | tf_op jit(solution)/shard_map/ppermute | solution.py:155
  89.6 0.3 gate_up_rise_3.1
  89.9 1.9 collective-permute-start.1
  91.8 1.4 collective-permute-done.4.refs_4_
  93.2 0.3 gate_up_fall_2.1
  93.5 5.4 %collective-permute-start.5 = (bf16[512,256]{1,0:T(8,128)(2,1)S(1)}, bf16[512,256]{1,0:T(8,128)(2,1)S(1)}, u32[]{:S(2)}, u32[]{:S(2)}) collective-permute-start(bf16[512,256]{1,0:T(8,128)(2,1)S(1)} %gate_up_fall_2.1), channel_id=1, source_target_pairs={{0,896},{128,0},{256,128},{384,256},{512,384},{640,512},{768,640},... | collective-permute-start | bytes 786440 | tf_op jit(solution)/shard_map/ppermute | solution.py:155
  99.0 4.7 %collective-permute-done.1.refs_4_ = bf16[512,256]{1,0:T(8,128)(2,1)S(1)} collective-permute-done((bf16[512,256]{1,0:T(8,128)(2,1)S(1)}, bf16[512,256]{1,0:T(8,128)(2,1)S(1)}, u32[]{:S(2)}, u32[]{:S(2)}) %collective-permute-start.1) | collective-permute-done | bytes 262176 | tf_op jit(solution)/shard_map/ppermute | solution.py:155
  103.7 0.3 gate_up_rise_2.1
  104.1 3.2 %collective-permute-start.2 = (bf16[512,256]{1,0:T(8,128)(2,1)S(1)}, bf16[512,256]{1,0:T(8,128)(2,1)S(1)}, u32[]{:S(2)}, u32[]{:S(2)}) collective-permute-start(bf16[512,256]{1,0:T(8,128)(2,1)S(1)} %gate_up_rise_2.1), channel_id=1, source_target_pairs={{0,128},{128,256},{256,384},{384,512},{512,640},{640,768},{768,896... | collective-permute-start | bytes 786440 | tf_op jit(solution)/shard_map/ppermute | solution.py:155
  107.2 0.7 collective-permute-done.5.refs_4_
  108.0 0.3 gate_up_fall_1.1
  108.3 5.4 %collective-permute-start.6 = (bf16[512,256]{1,0:T(8,128)(2,1)S(1)}, bf16[512,256]{1,0:T(8,128)(2,1)S(1)}, u32[]{:S(2)}, u32[]{:S(2)}) collective-permute-start(bf16[512,256]{1,0:T(8,128)(2,1)S(1)} %gate_up_fall_1.1), channel_id=1, source_target_pairs={{0,896},{128,0},{256,128},{384,256},{512,384},{640,512},{768,640},... | collective-permute-start | bytes 786440 | tf_op jit(solution)/shard_map/ppermute | solution.py:155
  113.7 3.6 %collective-permute-done.2.refs_4_ = bf16[512,256]{1,0:T(8,128)(2,1)S(1)} collective-permute-done((bf16[512,256]{1,0:T(8,128)(2,1)S(1)}, bf16[512,256]{1,0:T(8,128)(2,1)S(1)}, u32[]{:S(2)}, u32[]{:S(2)}) %collective-permute-start.2) | collective-permute-done | bytes 262176 | tf_op jit(solution)/shard_map/ppermute | solution.py:155
  117.4 0.3 gate_up_rise_1.1
  117.7 4.2 %collective-permute-start.3 = (bf16[512,256]{1,0:T(8,128)(2,1)S(1)}, bf16[512,256]{1,0:T(8,128)(2,1)S(1)}, u32[]{:S(2)}, u32[]{:S(2)}) collective-permute-start(bf16[512,256]{1,0:T(8,128)(2,1)S(1)} %gate_up_rise_1.1), channel_id=1, source_target_pairs={{0,128},{128,256},{256,384},{384,512},{512,640},{640,768},{768,896... | collective-permute-start | bytes 786440 | tf_op jit(solution)/shard_map/ppermute | solution.py:155
  121.9 0.3 gate_up_own.1.own_ref
  122.3 0.0 copy-start.4
  122.3 0.8 copy-done.4
  123.1 0.0 collective-permute-done.6.down_ref
  123.1 0.0 copy-start.6
  123.1 2.9 %collective-permute-done.3.up_ref = bf16[512,256]{1,0:T(8,128)(2,1)S(1)} collective-permute-done((bf16[512,256]{1,0:T(8,128)(2,1)S(1)}, bf16[512,256]{1,0:T(8,128)(2,1)S(1)}, u32[]{:S(2)}, u32[]{:S(2)}) %collective-permute-start.3) | collective-permute-done | bytes 262176 | tf_op jit(solution)/shard_map/ppermute | solution.py:155
  126.0 0.0 copy-done.6
  126.0 0.7 copy-done.7
  126.7 3.3 %activate.1.refs_1_ = bf16[512,256]{1,0:T(8,128)(2,1)} custom-call(f32[512,128]{1,0:T(8,128)} %bitcast.6, f32[512,256]{1,0:T(8,128)} %copy-done.4, bf16[512,256]{1,0:T(8,128)(2,1)} %copy-done.7, bf16[512,256]{1,0:T(8,128)(2,1)} %copy-done.6), custom_call_target="tpu_custom_call" | custom-call | tf_op jit(solution)/shard_map/activate/pallas_call | solution.py:190
  130.0 3.0 %collective-permute-start.7 = (bf16[512,256]{1,0:T(8,128)(2,1)}, bf16[512,256]{1,0:T(8,128)(2,1)S(1)}, u32[]{:S(2)}, u32[]{:S(2)}) collective-permute-start(bf16[512,256]{1,0:T(8,128)(2,1)} %activate.1.refs_1_), channel_id=1, source_target_pairs={{0,128},{128,256},{256,384},{384,512},{512,640},{640,768},{768,896... | collective-permute-start | bytes 786440 | tf_op jit(solution)/shard_map/ppermute | solution.py:155
  133.1 3.5 %collective-permute-start.11 = (bf16[512,256]{1,0:T(8,128)(2,1)}, bf16[512,256]{1,0:T(8,128)(2,1)S(1)}, u32[]{:S(2)}, u32[]{:S(2)}) collective-permute-start(bf16[512,256]{1,0:T(8,128)(2,1)} %activate.1.refs_1_), channel_id=1, source_target_pairs={{0,896},{128,0},{256,128},{384,256},{512,384},{640,512},{768,640},... | collective-permute-start | bytes 786440 | tf_op jit(solution)/shard_map/ppermute | solution.py:155
  136.5 2.0 collective-permute-done.7.refs_2_
  138.6 1.9 collective-permute-start.8
  140.5 0.0 collective-permute-done.11.refs_3_
  140.5 4.6 %collective-permute-start.12 = (bf16[512,256]{1,0:T(8,128)(2,1)S(1)}, bf16[512,256]{1,0:T(8,128)(2,1)S(1)}, u32[]{:S(2)}, u32[]{:S(2)}) collective-permute-start(bf16[512,256]{1,0:T(8,128)(2,1)S(1)} %collective-permute-done.11.refs_3_), channel_id=1, source_target_pairs={{0,896},{128,0},{256,128},{384,256},{512,384},{640,512},{768,640},... | collective-permute-start | bytes 786440 | tf_op jit(solution)/shard_map/ppermute | solution.py:155
  145.1 2.6 %collective-permute-done.8.refs_4_ = bf16[512,256]{1,0:T(8,128)(2,1)S(1)} collective-permute-done((bf16[512,256]{1,0:T(8,128)(2,1)S(1)}, bf16[512,256]{1,0:T(8,128)(2,1)S(1)}, u32[]{:S(2)}, u32[]{:S(2)}) %collective-permute-start.8) | collective-permute-done | bytes 262176 | tf_op jit(solution)/shard_map/ppermute | solution.py:155
  147.7 1.9 collective-permute-start.9
  149.6 0.0 collective-permute-done.12.refs_5_
  149.6 4.8 %collective-permute-start.13 = (bf16[512,256]{1,0:T(8,128)(2,1)S(1)}, bf16[512,256]{1,0:T(8,128)(2,1)S(1)}, u32[]{:S(2)}, u32[]{:S(2)}) collective-permute-start(bf16[512,256]{1,0:T(8,128)(2,1)S(1)} %collective-permute-done.12.refs_5_), channel_id=1, source_target_pairs={{0,896},{128,0},{256,128},{384,256},{512,384},{640,512},{768,640},... | collective-permute-start | bytes 786440 | tf_op jit(solution)/shard_map/ppermute | solution.py:155
  154.4 3.4 %collective-permute-done.9.refs_6_ = bf16[512,256]{1,0:T(8,128)(2,1)S(1)} collective-permute-done((bf16[512,256]{1,0:T(8,128)(2,1)S(1)}, bf16[512,256]{1,0:T(8,128)(2,1)S(1)}, u32[]{:S(2)}, u32[]{:S(2)}) %collective-permute-start.9) | collective-permute-done | bytes 262176 | tf_op jit(solution)/shard_map/ppermute | solution.py:155
  157.8 1.9 collective-permute-start.10
  159.7 0.1 collective-permute-done.13.refs_7_
  159.9 1.2 copy-done.2
  161.1 0.9 copy-done.5
  162.0 1.2 row_grad_near.1.refs_4_
  163.2 5.8 %collective-permute-done.10.refs_1_ = bf16[512,256]{1,0:T(8,128)(2,1)S(1)} collective-permute-done((bf16[512,256]{1,0:T(8,128)(2,1)S(1)}, bf16[512,256]{1,0:T(8,128)(2,1)S(1)}, u32[]{:S(2)}, u32[]{:S(2)}) %collective-permute-start.10) | collective-permute-done | bytes 262176 | tf_op jit(solution)/shard_map/ppermute | solution.py:155
  169.0 0.3 row_grad_far.1
  169.4 0.0 copy-start.8
  169.4 0.1 reshape.18
  169.5 37.7 %all_to_all.11 = bf16[128,4,512]{2,1,0:T(4,128)(2,1)S(1)} all-to-all(bf16[128,4,512]{2,1,0:T(4,128)(2,1)S(1)} %reshape.18), channel_id=1, replica_groups=mesh['rep'=8,'outer'=8,'local'=16] {'outer','local'}, dimensions={0} | all-to-all | bytes 1048576 | tf_op jit(solution)/shard_map/all_to_all | solution.py:253
  207.2 0.1 reshape.19
  207.4 0.0 copy-done.8
  207.4 0.8 convolution_convert_fusion
  (5 shorter events, 0.0 us)
Async XLA Ops:
  6.5 119.5 %reduce-scatter.2.cloned.1.call-start = ((), (), s32[]{:S(2)}) async-start(), calls=%async_computation.3 | async-start | bytes 2359296 | tf_op jit(solution)/shard_map/reduce_scatter | solution.py:256
  65.9 1.2 copy-start
  65.9 1.5 copy-start.1
  67.5 1.2 copy-start.3
  69.1 20.5 %collective-permute-start = (bf16[512,256]{1,0:T(8,128)(2,1)S(1)}, bf16[512,256]{1,0:T(8,128)(2,1)S(1)}, u32[]{:S(2)}, u32[]{:S(2)}) collective-permute-start(bf16[512,256]{1,0:T(8,128)(2,1)S(1)} %gate_up_rise_4.1), channel_id=1, source_target_pairs={{0,128},{128,256},{256,384},{384,512},{512,640},{640,768},{768,896... | collective-permute-start | bytes 786440 | tf_op jit(solution)/shard_map/ppermute | solution.py:155
  71.3 21.9 %collective-permute-start.4 = (bf16[512,256]{1,0:T(8,128)(2,1)S(1)}, bf16[512,256]{1,0:T(8,128)(2,1)S(1)}, u32[]{:S(2)}, u32[]{:S(2)}) collective-permute-start(bf16[512,256]{1,0:T(8,128)(2,1)S(1)} %gate_up_fall_3.1), channel_id=1, source_target_pairs={{0,896},{128,0},{256,128},{384,256},{512,384},{640,512},{768,640},... | collective-permute-start | bytes 786440 | tf_op jit(solution)/shard_map/ppermute | solution.py:155
  89.9 13.8 %collective-permute-start.1 = (bf16[512,256]{1,0:T(8,128)(2,1)S(1)}, bf16[512,256]{1,0:T(8,128)(2,1)S(1)}, u32[]{:S(2)}, u32[]{:S(2)}) collective-permute-start(bf16[512,256]{1,0:T(8,128)(2,1)S(1)} %gate_up_rise_3.1), channel_id=1, source_target_pairs={{0,128},{128,256},{256,384},{384,512},{512,640},{640,768},{768,896... | collective-permute-start | bytes 786440 | tf_op jit(solution)/shard_map/ppermute | solution.py:155
  93.5 14.4 %collective-permute-start.5 = (bf16[512,256]{1,0:T(8,128)(2,1)S(1)}, bf16[512,256]{1,0:T(8,128)(2,1)S(1)}, u32[]{:S(2)}, u32[]{:S(2)}) collective-permute-start(bf16[512,256]{1,0:T(8,128)(2,1)S(1)} %gate_up_fall_2.1), channel_id=1, source_target_pairs={{0,896},{128,0},{256,128},{384,256},{512,384},{640,512},{768,640},... | collective-permute-start | bytes 786440 | tf_op jit(solution)/shard_map/ppermute | solution.py:155
  104.1 13.3 %collective-permute-start.2 = (bf16[512,256]{1,0:T(8,128)(2,1)S(1)}, bf16[512,256]{1,0:T(8,128)(2,1)S(1)}, u32[]{:S(2)}, u32[]{:S(2)}) collective-permute-start(bf16[512,256]{1,0:T(8,128)(2,1)S(1)} %gate_up_rise_2.1), channel_id=1, source_target_pairs={{0,128},{128,256},{256,384},{384,512},{512,640},{640,768},{768,896... | collective-permute-start | bytes 786440 | tf_op jit(solution)/shard_map/ppermute | solution.py:155
  108.3 14.8 %collective-permute-start.6 = (bf16[512,256]{1,0:T(8,128)(2,1)S(1)}, bf16[512,256]{1,0:T(8,128)(2,1)S(1)}, u32[]{:S(2)}, u32[]{:S(2)}) collective-permute-start(bf16[512,256]{1,0:T(8,128)(2,1)S(1)} %gate_up_fall_1.1), channel_id=1, source_target_pairs={{0,896},{128,0},{256,128},{384,256},{512,384},{640,512},{768,640},... | collective-permute-start | bytes 786440 | tf_op jit(solution)/shard_map/ppermute | solution.py:155
  117.7 8.3 %collective-permute-start.3 = (bf16[512,256]{1,0:T(8,128)(2,1)S(1)}, bf16[512,256]{1,0:T(8,128)(2,1)S(1)}, u32[]{:S(2)}, u32[]{:S(2)}) collective-permute-start(bf16[512,256]{1,0:T(8,128)(2,1)S(1)} %gate_up_rise_1.1), channel_id=1, source_target_pairs={{0,128},{128,256},{256,384},{384,512},{512,640},{640,768},{768,896... | collective-permute-start | bytes 786440 | tf_op jit(solution)/shard_map/ppermute | solution.py:155
  122.3 0.8 copy-start.4
  123.1 2.9 %copy-start.6 = (bf16[512,256]{1,0:T(8,128)(2,1)}, bf16[512,256]{1,0:T(8,128)(2,1)S(1)}, u32[]{:S(2)}) copy-start(bf16[512,256]{1,0:T(8,128)(2,1)S(1)} %collective-permute-done.6.down_ref) | copy-start | bytes 786436
  126.0 0.7 copy-start.7
  130.0 8.5 %collective-permute-start.7 = (bf16[512,256]{1,0:T(8,128)(2,1)}, bf16[512,256]{1,0:T(8,128)(2,1)S(1)}, u32[]{:S(2)}, u32[]{:S(2)}) collective-permute-start(bf16[512,256]{1,0:T(8,128)(2,1)} %activate.1.refs_1_), channel_id=1, source_target_pairs={{0,128},{128,256},{256,384},{384,512},{512,640},{640,768},{768,896... | collective-permute-start | bytes 786440 | tf_op jit(solution)/shard_map/ppermute | solution.py:155
  133.1 7.4 %collective-permute-start.11 = (bf16[512,256]{1,0:T(8,128)(2,1)}, bf16[512,256]{1,0:T(8,128)(2,1)S(1)}, u32[]{:S(2)}, u32[]{:S(2)}) collective-permute-start(bf16[512,256]{1,0:T(8,128)(2,1)} %activate.1.refs_1_), channel_id=1, source_target_pairs={{0,896},{128,0},{256,128},{384,256},{512,384},{640,512},{768,640},... | collective-permute-start | bytes 786440 | tf_op jit(solution)/shard_map/ppermute | solution.py:155
  138.6 9.1 %collective-permute-start.8 = (bf16[512,256]{1,0:T(8,128)(2,1)S(1)}, bf16[512,256]{1,0:T(8,128)(2,1)S(1)}, u32[]{:S(2)}, u32[]{:S(2)}) collective-permute-start(bf16[512,256]{1,0:T(8,128)(2,1)S(1)} %collective-permute-done.7.refs_2_), channel_id=1, source_target_pairs={{0,128},{128,256},{256,384},{384,512},{512,640},{640,768},{768,896... | collective-permute-start | bytes 786440 | tf_op jit(solution)/shard_map/ppermute | solution.py:155
  140.5 9.1 %collective-permute-start.12 = (bf16[512,256]{1,0:T(8,128)(2,1)S(1)}, bf16[512,256]{1,0:T(8,128)(2,1)S(1)}, u32[]{:S(2)}, u32[]{:S(2)}) collective-permute-start(bf16[512,256]{1,0:T(8,128)(2,1)S(1)} %collective-permute-done.11.refs_3_), channel_id=1, source_target_pairs={{0,896},{128,0},{256,128},{384,256},{512,384},{640,512},{768,640},... | collective-permute-start | bytes 786440 | tf_op jit(solution)/shard_map/ppermute | solution.py:155
  147.7 10.2 %collective-permute-start.9 = (bf16[512,256]{1,0:T(8,128)(2,1)S(1)}, bf16[512,256]{1,0:T(8,128)(2,1)S(1)}, u32[]{:S(2)}, u32[]{:S(2)}) collective-permute-start(bf16[512,256]{1,0:T(8,128)(2,1)S(1)} %collective-permute-done.8.refs_4_), channel_id=1, source_target_pairs={{0,128},{128,256},{256,384},{384,512},{512,640},{640,768},{768,896... | collective-permute-start | bytes 786440 | tf_op jit(solution)/shard_map/ppermute | solution.py:155
  149.6 10.3 %collective-permute-start.13 = (bf16[512,256]{1,0:T(8,128)(2,1)S(1)}, bf16[512,256]{1,0:T(8,128)(2,1)S(1)}, u32[]{:S(2)}, u32[]{:S(2)}) collective-permute-start(bf16[512,256]{1,0:T(8,128)(2,1)S(1)} %collective-permute-done.12.refs_5_), channel_id=1, source_target_pairs={{0,896},{128,0},{256,128},{384,256},{512,384},{640,512},{768,640},... | collective-permute-start | bytes 786440 | tf_op jit(solution)/shard_map/ppermute | solution.py:155
  157.8 11.2 %collective-permute-start.10 = (bf16[512,256]{1,0:T(8,128)(2,1)S(1)}, bf16[512,256]{1,0:T(8,128)(2,1)S(1)}, u32[]{:S(2)}, u32[]{:S(2)}) collective-permute-start(bf16[512,256]{1,0:T(8,128)(2,1)S(1)} %collective-permute-done.9.refs_6_), channel_id=1, source_target_pairs={{0,128},{128,256},{256,384},{384,512},{512,640},{640,768},{768,896... | collective-permute-start | bytes 786440 | tf_op jit(solution)/shard_map/ppermute | solution.py:155
  159.9 1.2 copy-start.2
  161.1 0.9 copy-start.5
  169.4 38.0 %copy-start.8 = (bf16[32,512]{1,0:T(8,128)(2,1)S(1)}, bf16[32,512]{1,0:T(8,128)(2,1)}, u32[]{:S(2)}) copy-start(bf16[32,512]{1,0:T(8,128)(2,1)} %get-tuple-element.7) | copy-start | bytes 98308
Sparse Core Ops, SparseCore 0:
  66.1 54.5 reduce-scatter.1

commit v4 on v3

--- a/solution.py
+++ b/solution.py
@@ -15,7 +15,7 @@
     return pltpu.CompilerParams(vmem_limit_bytes=mib * 1024 * 1024)
 
 
-def route_kernel(capacity, ids_hbm, w_hbm, tok_hbm, og_hbm, send_ref, pt_ref, *scratch):
+def route_kernel(capacity, ids_hbm, w_hbm, tok_hbm, og_hbm, dy_ref, x_ref, pt_ref, *scratch):
     ids_ref, w_ref, tok_ref, og_ref, scaled_ref, sems = scratch
     copies = [
         pltpu.make_async_copy(src, dst, sems.at[n])
@@ -26,9 +26,8 @@
     for copy in copies:
         copy.start()
     top, tok = ids_ref.shape
-    width = tok_ref.shape[1]
     rows = top * tok
-    slots = send_ref.shape[0]
+    slots = dy_ref.shape[0]
     c_row = lax.broadcasted_iota(jnp.int32, (rows, tok), 0)
     pick_i = (c_row % tok == lax.broadcasted_iota(jnp.int32, (rows, tok), 1)).astype(BF16)
     c_k = lax.broadcasted_iota(jnp.int32, (rows, top), 0)
@@ -62,12 +61,8 @@
     ).astype(BF16)
     og = jnp.dot(pick_i, og_ref[...], preferred_element_type=F32)
     scaled_ref[...] = (w_col * og).astype(BF16)
-    send_ref[:, :width] = jnp.dot(
-        per_token, tok_ref[...], preferred_element_type=F32
-    ).astype(BF16)
-    send_ref[:, width:] = jnp.dot(
-        table, scaled_ref[...], preferred_element_type=F32
-    ).astype(BF16)
+    x_ref[...] = jnp.dot(per_token, tok_ref[...], preferred_element_type=F32).astype(BF16)
+    dy_ref[...] = jnp.dot(table, scaled_ref[...], preferred_element_type=F32).astype(BF16)
 
 
 def route(tokens, out_grad, expert_ids, route_weights, experts, capacity):
@@ -77,9 +72,10 @@
     return pl.pallas_call(
         lambda *refs: route_kernel(capacity, *refs),
         in_specs=[pl.BlockSpec(memory_space=pltpu.HBM)] * 4,
-        out_specs=(VMEM_SPEC, VMEM_SPEC),
+        out_specs=(VMEM_SPEC, VMEM_SPEC, VMEM_SPEC),
         out_shape=(
-            jax.ShapeDtypeStruct((slots, 2 * width), BF16),
+            jax.ShapeDtypeStruct((slots, width), BF16),
+            jax.ShapeDtypeStruct((slots, width), BF16),
             jax.ShapeDtypeStruct((tok, slots), BF16),
         ),
         scratch_shapes=[
@@ -102,23 +98,22 @@
         out_ref[j] = out[:, j * part : (j + 1) * part]
 
 
-def hidden_parts(both_rows, w_down, n_rep):
-    rows = both_rows.shape[0]
-    width = both_rows.shape[1] // 2
+def hidden_parts(dy_rows, w_down, n_rep):
+    rows, width = dy_rows.shape
     part = w_down.shape[1] // n_rep
     per = 2
     return pl.pallas_call(
         hidden_kernel,
         grid=(n_rep // per,),
         in_specs=[
-            pl.BlockSpec((rows, width), lambda c: (0, 1)),
+            pl.BlockSpec((rows, width), lambda c: (0, 0)),
             pl.BlockSpec((1, per * part, width), lambda c: (0, c, 0)),
         ],
         out_specs=pl.BlockSpec((per, rows, part), lambda c: (c, 0, 0)),
         out_shape=jax.ShapeDtypeStruct((n_rep, rows, part), F32),
-        compiler_params=params(62),
+        compiler_params=params(),
         name="hidden",
-    )(both_rows, w_down)
+    )(dy_rows, w_down)
 
 
 def chunk_weights(me_ref, offset, n_rep, wg_ref, wu_ref):
@@ -129,16 +124,15 @@
 
 
 def gate_up_kernel(offset, n_rep, me_ref, rows_ref, wg_ref, wu_ref, *refs):
-    width = wg_ref.shape[1]
     weights = chunk_weights(me_ref, offset, n_rep, wg_ref, wu_ref)
-    total = jnp.dot(rows_ref[:, :width], weights, preferred_element_type=F32)
+    total = jnp.dot(rows_ref[...], weights, preferred_element_type=F32)
     for arrived in refs[:-1]:
         total = total + arrived[...].astype(F32)
     refs[-1][...] = total.astype(refs[-1].dtype)
 
 
-def gate_up(me, both_rows, w_gate, w_up, n_rep, offset, arrived, dtype, name):
-    rows = both_rows.shape[0]
+def gate_up(me, x_rows, w_gate, w_up, n_rep, offset, arrived, dtype, name):
+    rows = x_rows.shape[0]
     part = w_gate.shape[2] // n_rep
     return pl.pallas_call(
         lambda *refs: gate_up_kernel(offset, n_rep, *refs),
@@ -147,7 +141,7 @@
         out_shape=jax.ShapeDtypeStruct((rows, 2 * part), dtype),
         compiler_params=params(),
         name=name,
-    )(me, both_rows, w_gate, w_up, *arrived)
+    )(me, x_rows, w_gate, w_up, *arrived)
 
 
 def shift(rows, by):
@@ -155,20 +149,20 @@
     return lax.ppermute(rows, "rep", [(i, (i + by) % n_rep) for i in range(n_rep)])
 
 
-def gate_up_sums(me, both_rows, w_gate, w_up, n_rep):
+def gate_up_sums(me, x_rows, w_gate, w_up, n_rep):
     half = n_rep // 2
     up, down = (), ()
     for hop in range(half, 0, -1):
         term = gate_up(
-            me, both_rows, w_gate, w_up, n_rep, hop, up, BF16, "gate_up_rise_%d" % hop
+            me, x_rows, w_gate, w_up, n_rep, hop, up, BF16, "gate_up_rise_%d" % hop
         )
         up = (shift(term, 1),)
         if hop < half:
             term = gate_up(
-                me, both_rows, w_gate, w_up, n_rep, n_rep - hop, down, BF16, "gate_up_fall_%d" % hop
+                me, x_rows, w_gate, w_up, n_rep, n_rep - hop, down, BF16, "gate_up_fall_%d" % hop
             )
             down = (shift(term, -1),)
-    own = gate_up(me, both_rows, w_gate, w_up, n_rep, 0, (), F32, "gate_up_own")
+    own = gate_up(me, x_rows, w_gate, w_up, n_rep, 0, (), F32, "gate_up_own")
     return own, up[0], down[0]
 
 
@@ -246,17 +240,20 @@
     capacity = max(2, 2 * tok * top // experts)
     slots = experts * capacity
     me = lax.axis_index("rep").astype(jnp.int32).reshape(1)
-    send, per_token_t = route(tokens, out_grad, expert_ids, route_weights, experts, capacity)
+    send_dy, send_x, per_token_t = route(
+        tokens, out_grad, expert_ids, route_weights, experts, capacity
+    )
 
     def exchange(rows):
-        blocks = rows.reshape(experts, capacity, rows.shape[1])
-        return lax.all_to_all(blocks, ("outer", "local"), 0, 0, tiled=True).reshape(rows.shape)
-
-    both_rows = exchange(send)
+        blocks = rows.reshape(experts, capacity, width)
+        return lax.all_to_all(blocks, ("outer", "local"), 0, 0, tiled=True).reshape(slots, width)
+
+    dy_rows = exchange(send_dy)
     hidden = lax.psum_scatter(
-        hidden_parts(both_rows, down_weight, n_rep), "rep", scatter_dimension=0
+        hidden_parts(dy_rows, down_weight, n_rep), "rep", scatter_dimension=0
     )
-    sums = gate_up_sums(me, both_rows, gate_weight, up_weight, n_rep)
+    x_rows = exchange(send_x)
+    sums = gate_up_sums(me, x_rows, gate_weight, up_weight, n_rep)
     own = activate(hidden, *sums)
     returned = exchange(gather_matmul(me, own, gate_weight, up_weight, n_rep))
     return jnp.dot(per_token_t, returned, preferred_element_type=F32).astype(BF16)

time: 216 us -> 216 us (level)
  waiting for transfers between devices: 32.2 us -> 47.6 us
  blocking collectives: 87.4 us -> 75.1 us
  local copies, waits for them, and re-layouts: 9.24 us -> 6.72 us
    all_to_all x0 -> x1, waiting for transfers between devices: none -> 19.7 us  [exchange(): lax.all_to_all(blocks, ('outer', 'local'), 0, 0, tiled=True)]
    all_to_all x2, blocking collectives: 87.4 us -> 75.1 us  [exchange(): lax.all_to_all(blocks, ('outer', 'local'), 0, 0, tiled=True)]
    all_to_all x0 -> x1, starting transfers between devices: none -> 6.43 us  [exchange(): lax.all_to_all(blocks, ('outer', 'local'), 0, 0, tiled=True)]
    ppermute x14, starting transfers between devices: 57.1 us -> 51.5 us  [shift(): lax.ppermute(rows, 'rep', [(i, (i + by) % n_rep) for i in range(n_rep)])]
    ppermute x14, waiting for transfers between devices: 32.2 us -> 27.9 us  [shift(): lax.ppermute(rows, 'rep', [(i, (i + by) % n_rep) for i in range(n_rep)])]
    unnamed x18, local copies, waits for them, and re-layouts: 6.42 us -> 3 us
  transfers between devices with their start and end apart: 15 -> 16, of which waited for: 11 -> 9; matrix products, arithmetic and copies ran while one was open for 0% -> 1% of each run, Pallas kernels for 2% -> 2%
where the time goes in v4:
time: 216 us; the launch traced here: 215 us
  blocking collectives  75.1 us (35%)
  starting transfers between devices  58 us (27%)
  waiting for transfers between devices  47.6 us (22%)
  between operations  13.8 us (6%)
  Pallas kernels  12.8 us (6%)
  local copies, waits for them, and re-layouts  6.72 us (3%)
    all_to_all x2, blocking collectives, exchange(): lax.all_to_all(blocks, ('outer', 'local'), 0, 0, tiled=True)  75.1 us
    ppermute x14, starting transfers between devices, shift(): lax.ppermute(rows, 'rep', [(i, (i + by) % n_rep) for i in range(n_rep)])  51.5 us
    ppermute x14, waiting for transfers between devices, shift(): lax.ppermute(rows, 'rep', [(i, (i + by) % n_rep) for i in range(n_rep)])  27.9 us
    all_to_all x1, waiting for transfers between devices, exchange(): lax.all_to_all(blocks, ('outer', 'local'), 0, 0, tiled=True)  19.7 us
    all_to_all x1, starting transfers between devices, exchange(): lax.all_to_all(blocks, ('outer', 'local'), 0, 0, tiled=True)  6.43 us
  transfers between devices with their start and end apart: 16, of which 9 were waited for; matrix products, arithmetic and copies ran while one was open for 1% of the time, Pallas kernels for 2%

profile of v4, /device:TPU:1, one launch (start us, length us, event | category | flops | bytes accessed | tf_op | source)
XLA Modules:
  0.0 214.8 jit_solution(11441095009989193663)
XLA Ops:
  6.5 0.0 reduce-scatter.2.cloned.1.call-start
  6.5 2.6 %route.1 = (bf16[512,512]{1,0:T(8,128)(2,1)}, bf16[512,512]{1,0:T(8,128)(2,1)}, bf16[32,512]{1,0:T(8,128)(2,1)}) custom-call(s32[8,32]{1,0:T(8,128)} %bitcast.7, f32[8,32]{1,0:T(8,128)} %bitcast.8, bf16[32,512]{1,0:T(8,128)(2,1)} %refs_2_.10, bf16[32,512]{1,0:T(8,128)(2,1)} %refs_3_.10), custom_call_target="tpu_custom_call" | custom-call | tf_op jit(solution)/shard_map/route/pallas_call | solution.py:72
  9.1 0.0 copy-start.4
  9.2 1.3 reshape.22
  10.4 39.4 %all_to_all.15 = bf16[128,4,512]{2,1,0:T(4,128)(2,1)S(1)} all-to-all(bf16[128,4,512]{2,1,0:T(4,128)(2,1)S(1)} %reshape.22), channel_id=1, replica_groups=mesh['rep'=8,'outer'=8,'local'=16] {'outer','local'}, dimensions={0} | all-to-all | bytes 1048576 | tf_op jit(solution)/shard_map/all_to_all | solution.py:249
  49.8 0.1 reshape.23.rows_ref
  49.9 0.0 copy-done.4
  49.9 2.6 %hidden.1 = f32[8,512,128]{2,1,0:T(8,128)} custom-call(bf16[512,512]{1,0:T(8,128)(2,1)S(1)} %reshape.23.rows_ref, bf16[1,1024,512]{2,1,0:T(8,128)(2,1)S(1)} %copy-done.4), custom_call_target="tpu_custom_call" | custom-call | tf_op jit(solution)/shard_map/hidden/pallas_call | solution.py:105
  52.6 0.0 reduce-scatter.2.cloned.1.call-update
  52.6 0.0 copy-start
  52.6 0.0 copy-start.1
  52.6 0.9 reshape.24
  53.6 6.4 %all-to-all-start.1 = ((bf16[128,4,512]{2,1,0:T(4,128)(2,1)}), bf16[128,4,512]{2,1,0:T(4,128)(2,1)}, u32[]{:S(2)}, u32[]{:S(2)}) async-start(bf16[128,4,512]{2,1,0:T(4,128)(2,1)} %reshape.24), calls=%async_computation.2 | async-start | bytes 1048576 | tf_op jit(solution)/shard_map/all_to_all | solution.py:249
  60.0 19.7 %all-to-all-done.1 = bf16[128,4,512]{2,1,0:T(4,128)(2,1)} async-done(((bf16[128,4,512]{2,1,0:T(4,128)(2,1)}), bf16[128,4,512]{2,1,0:T(4,128)(2,1)}, u32[]{:S(2)}, u32[]{:S(2)}) %all-to-all-start.1) | async-done | bytes 524320 | tf_op jit(solution)/shard_map/all_to_all | solution.py:249
  79.7 1.2 reshape.25.refs_1_
  80.9 0.3 gate_up_rise_4.1
  81.2 1.9 collective-permute-start
  83.2 0.3 gate_up_fall_3.1
  83.5 13.4 %collective-permute-start.4 = (bf16[512,256]{1,0:T(8,128)(2,1)S(1)}, bf16[512,256]{1,0:T(8,128)(2,1)S(1)}, u32[]{:S(2)}, u32[]{:S(2)}) collective-permute-start(bf16[512,256]{1,0:T(8,128)(2,1)S(1)} %gate_up_fall_3.1), channel_id=1, source_target_pairs={{0,896},{128,0},{256,128},{384,256},{512,384},{640,512},{768,640},... | collective-permute-start | bytes 786440 | tf_op jit(solution)/shard_map/ppermute | solution.py:149
  96.9 6.3 %collective-permute-done.refs_4_ = bf16[512,256]{1,0:T(8,128)(2,1)S(1)} collective-permute-done((bf16[512,256]{1,0:T(8,128)(2,1)S(1)}, bf16[512,256]{1,0:T(8,128)(2,1)S(1)}, u32[]{:S(2)}, u32[]{:S(2)}) %collective-permute-start) | collective-permute-done | bytes 262176 | tf_op jit(solution)/shard_map/ppermute | solution.py:149
  103.2 0.3 gate_up_rise_3.1
  103.6 1.9 collective-permute-start.1
  105.5 0.0 collective-permute-done.4.refs_4_
  105.5 0.3 gate_up_fall_2.1
  105.9 4.6 %collective-permute-start.5 = (bf16[512,256]{1,0:T(8,128)(2,1)S(1)}, bf16[512,256]{1,0:T(8,128)(2,1)S(1)}, u32[]{:S(2)}, u32[]{:S(2)}) collective-permute-start(bf16[512,256]{1,0:T(8,128)(2,1)S(1)} %gate_up_fall_2.1), channel_id=1, source_target_pairs={{0,896},{128,0},{256,128},{384,256},{512,384},{640,512},{768,640},... | collective-permute-start | bytes 786440 | tf_op jit(solution)/shard_map/ppermute | solution.py:149
  110.4 3.8 %collective-permute-done.1.refs_4_ = bf16[512,256]{1,0:T(8,128)(2,1)S(1)} collective-permute-done((bf16[512,256]{1,0:T(8,128)(2,1)S(1)}, bf16[512,256]{1,0:T(8,128)(2,1)S(1)}, u32[]{:S(2)}, u32[]{:S(2)}) %collective-permute-start.1) | collective-permute-done | bytes 262176 | tf_op jit(solution)/shard_map/ppermute | solution.py:149
  114.3 0.3 gate_up_rise_2.1
  114.6 1.9 collective-permute-start.2
  116.6 0.0 collective-permute-done.5.refs_4_
  116.6 0.3 gate_up_fall_1.1
  116.9 4.6 %collective-permute-start.6 = (bf16[512,256]{1,0:T(8,128)(2,1)S(1)}, bf16[512,256]{1,0:T(8,128)(2,1)S(1)}, u32[]{:S(2)}, u32[]{:S(2)}) collective-permute-start(bf16[512,256]{1,0:T(8,128)(2,1)S(1)} %gate_up_fall_1.1), channel_id=1, source_target_pairs={{0,896},{128,0},{256,128},{384,256},{512,384},{640,512},{768,640},... | collective-permute-start | bytes 786440 | tf_op jit(solution)/shard_map/ppermute | solution.py:149
  121.5 2.9 %collective-permute-done.2.refs_4_ = bf16[512,256]{1,0:T(8,128)(2,1)S(1)} collective-permute-done((bf16[512,256]{1,0:T(8,128)(2,1)S(1)}, bf16[512,256]{1,0:T(8,128)(2,1)S(1)}, u32[]{:S(2)}, u32[]{:S(2)}) %collective-permute-start.2) | collective-permute-done | bytes 262176 | tf_op jit(solution)/shard_map/ppermute | solution.py:149
  124.4 0.3 gate_up_rise_1.1
  124.8 1.9 collective-permute-start.3
  126.7 0.3 gate_up_own.1.own_ref
  127.1 0.0 copy-start.3
  127.1 0.8 copy-done.3
  127.9 0.0 collective-permute-done.6.down_ref
  127.9 5.9 %collective-permute-done.3.up_ref = bf16[512,256]{1,0:T(8,128)(2,1)} collective-permute-done((bf16[512,256]{1,0:T(8,128)(2,1)S(1)}, bf16[512,256]{1,0:T(8,128)(2,1)}, u32[]{:S(2)}, u32[]{:S(2)}) %collective-permute-start.3) | collective-permute-done | bytes 262176 | tf_op jit(solution)/shard_map/ppermute | solution.py:149
  133.8 3.3 %activate.1.refs_1_ = bf16[512,256]{1,0:T(8,128)(2,1)} custom-call(f32[512,128]{1,0:T(8,128)} %bitcast.6, f32[512,256]{1,0:T(8,128)} %copy-done.3, bf16[512,256]{1,0:T(8,128)(2,1)} %collective-permute-done.3.up_ref, bf16[512,256]{1,0:T(8,128)(2,1)} %copy-done.7), custom_call_target="tpu_custom_call" | custom-call | tf_op jit(solution)/shard_map/activate/pallas_call | solution.py:184
  137.1 1.9 collective-permute-start.7
  139.0 4.6 %collective-permute-start.11 = (bf16[512,256]{1,0:T(8,128)(2,1)}, bf16[512,256]{1,0:T(8,128)(2,1)S(1)}, u32[]{:S(2)}, u32[]{:S(2)}) collective-permute-start(bf16[512,256]{1,0:T(8,128)(2,1)} %activate.1.refs_1_), channel_id=1, source_target_pairs={{0,896},{128,0},{256,128},{384,256},{512,384},{640,512},{768,640},... | collective-permute-start | bytes 786440 | tf_op jit(solution)/shard_map/ppermute | solution.py:149
  143.6 2.0 collective-permute-done.7.refs_2_
  145.6 1.9 collective-permute-start.8
  147.5 0.0 collective-permute-done.11.refs_3_
  147.5 4.6 %collective-permute-start.12 = (bf16[512,256]{1,0:T(8,128)(2,1)S(1)}, bf16[512,256]{1,0:T(8,128)(2,1)S(1)}, u32[]{:S(2)}, u32[]{:S(2)}) collective-permute-start(bf16[512,256]{1,0:T(8,128)(2,1)S(1)} %collective-permute-done.11.refs_3_), channel_id=1, source_target_pairs={{0,896},{128,0},{256,128},{384,256},{512,384},{640,512},{768,640},... | collective-permute-start | bytes 786440 | tf_op jit(solution)/shard_map/ppermute | solution.py:149
  152.1 1.8 collective-permute-done.8.refs_4_
  153.9 1.9 collective-permute-start.9
  155.8 0.0 collective-permute-done.12.refs_5_
  155.9 4.6 %collective-permute-start.13 = (bf16[512,256]{1,0:T(8,128)(2,1)S(1)}, bf16[512,256]{1,0:T(8,128)(2,1)S(1)}, u32[]{:S(2)}, u32[]{:S(2)}) collective-permute-start(bf16[512,256]{1,0:T(8,128)(2,1)S(1)} %collective-permute-done.12.refs_5_), channel_id=1, source_target_pairs={{0,896},{128,0},{256,128},{384,256},{512,384},{640,512},{768,640},... | collective-permute-start | bytes 786440 | tf_op jit(solution)/shard_map/ppermute | solution.py:149
  160.4 1.8 collective-permute-done.9.refs_6_
  162.2 1.9 collective-permute-start.10
  164.2 0.0 collective-permute-done.13.refs_7_
  164.2 0.0 copy-start.2
  164.2 1.2 copy-done.2
  165.4 0.9 copy-done.5
  166.3 1.2 row_grad_near.1.refs_4_
  167.5 3.2 %collective-permute-done.10.refs_1_ = bf16[512,256]{1,0:T(8,128)(2,1)S(1)} collective-permute-done((bf16[512,256]{1,0:T(8,128)(2,1)S(1)}, bf16[512,256]{1,0:T(8,128)(2,1)S(1)}, u32[]{:S(2)}, u32[]{:S(2)}) %collective-permute-start.10) | collective-permute-done | bytes 262176 | tf_op jit(solution)/shard_map/ppermute | solution.py:149
  170.8 0.3 row_grad_far.1
  171.1 0.0 copy-start.8
  171.1 0.1 reshape.26
  171.2 35.8 %all_to_all.16 = bf16[128,4,512]{2,1,0:T(4,128)(2,1)S(1)} all-to-all(bf16[128,4,512]{2,1,0:T(4,128)(2,1)S(1)} %reshape.26), channel_id=1, replica_groups=mesh['rep'=8,'outer'=8,'local'=16] {'outer','local'}, dimensions={0} | all-to-all | bytes 1048576 | tf_op jit(solution)/shard_map/all_to_all | solution.py:249
  207.0 0.1 reshape.27
  207.2 0.8 convolution_convert_fusion
  (9 shorter events, 0.0 us)
Async XLA Ops:
  6.5 127.2 %reduce-scatter.2.cloned.1.call-start = ((), (), s32[]{:S(2)}) async-start(), calls=%async_computation.4 | async-start | bytes 2359296 | tf_op jit(solution)/shard_map/reduce_scatter | solution.py:252
  9.1 40.8 %copy-start.4 = (bf16[1,1024,512]{2,1,0:T(8,128)(2,1)S(1)}, bf16[1,1024,512]{2,1,0:T(8,128)(2,1)}, u32[]{:S(2)}) copy-start(bf16[1,1024,512]{2,1,0:T(8,128)(2,1)} %w_ref.1) | copy-start | bytes 3145732
  49.9 2.7 %copy-start.6 = (bf16[512,512]{1,0:T(8,128)(2,1)S(1)}, bf16[512,512]{1,0:T(8,128)(2,1)}, u32[]{:S(2)}) copy-start(bf16[512,512]{1,0:T(8,128)(2,1)} %get-tuple-element.10) | copy-start | bytes 1572868
  52.6 28.3 %copy-start = (bf16[1,512,1024]{2,1,0:T(8,128)(2,1)S(1)}, bf16[1,512,1024]{2,1,0:T(8,128)(2,1)}, u32[]{:S(2)}) copy-start(bf16[1,512,1024]{2,1,0:T(8,128)(2,1)} %refs_2_.19) | copy-start | bytes 3145732
  52.6 28.3 %copy-start.1 = (bf16[1,512,1024]{2,1,0:T(8,128)(2,1)S(1)}, bf16[1,512,1024]{2,1,0:T(8,128)(2,1)}, u32[]{:S(2)}) copy-start(bf16[1,512,1024]{2,1,0:T(8,128)(2,1)} %refs_3_.19) | copy-start | bytes 3145732
  53.6 26.1 %all-to-all-start.1 = ((bf16[128,4,512]{2,1,0:T(4,128)(2,1)}), bf16[128,4,512]{2,1,0:T(4,128)(2,1)}, u32[]{:S(2)}, u32[]{:S(2)}) async-start(bf16[128,4,512]{2,1,0:T(4,128)(2,1)} %reshape.24), calls=%async_computation.2 | async-start | bytes 1048576 | tf_op jit(solution)/shard_map/all_to_all | solution.py:249
  81.2 22.0 %collective-permute-start = (bf16[512,256]{1,0:T(8,128)(2,1)S(1)}, bf16[512,256]{1,0:T(8,128)(2,1)S(1)}, u32[]{:S(2)}, u32[]{:S(2)}) collective-permute-start(bf16[512,256]{1,0:T(8,128)(2,1)S(1)} %gate_up_rise_4.1), channel_id=1, source_target_pairs={{0,128},{128,256},{256,384},{384,512},{512,640},{640,768},{768,896... | collective-permute-start | bytes 786440 | tf_op jit(solution)/shard_map/ppermute | solution.py:149
  83.5 22.0 %collective-permute-start.4 = (bf16[512,256]{1,0:T(8,128)(2,1)S(1)}, bf16[512,256]{1,0:T(8,128)(2,1)S(1)}, u32[]{:S(2)}, u32[]{:S(2)}) collective-permute-start(bf16[512,256]{1,0:T(8,128)(2,1)S(1)} %gate_up_fall_3.1), channel_id=1, source_target_pairs={{0,896},{128,0},{256,128},{384,256},{512,384},{640,512},{768,640},... | collective-permute-start | bytes 786440 | tf_op jit(solution)/shard_map/ppermute | solution.py:149
  103.6 10.7 %collective-permute-start.1 = (bf16[512,256]{1,0:T(8,128)(2,1)S(1)}, bf16[512,256]{1,0:T(8,128)(2,1)S(1)}, u32[]{:S(2)}, u32[]{:S(2)}) collective-permute-start(bf16[512,256]{1,0:T(8,128)(2,1)S(1)} %gate_up_rise_3.1), channel_id=1, source_target_pairs={{0,128},{128,256},{256,384},{384,512},{512,640},{640,768},{768,896... | collective-permute-start | bytes 786440 | tf_op jit(solution)/shard_map/ppermute | solution.py:149
  105.9 10.7 %collective-permute-start.5 = (bf16[512,256]{1,0:T(8,128)(2,1)S(1)}, bf16[512,256]{1,0:T(8,128)(2,1)S(1)}, u32[]{:S(2)}, u32[]{:S(2)}) collective-permute-start(bf16[512,256]{1,0:T(8,128)(2,1)S(1)} %gate_up_fall_2.1), channel_id=1, source_target_pairs={{0,896},{128,0},{256,128},{384,256},{512,384},{640,512},{768,640},... | collective-permute-start | bytes 786440 | tf_op jit(solution)/shard_map/ppermute | solution.py:149
  114.6 9.8 %collective-permute-start.2 = (bf16[512,256]{1,0:T(8,128)(2,1)S(1)}, bf16[512,256]{1,0:T(8,128)(2,1)S(1)}, u32[]{:S(2)}, u32[]{:S(2)}) collective-permute-start(bf16[512,256]{1,0:T(8,128)(2,1)S(1)} %gate_up_rise_2.1), channel_id=1, source_target_pairs={{0,128},{128,256},{256,384},{384,512},{512,640},{640,768},{768,896... | collective-permute-start | bytes 786440 | tf_op jit(solution)/shard_map/ppermute | solution.py:149
  116.9 10.9 %collective-permute-start.6 = (bf16[512,256]{1,0:T(8,128)(2,1)S(1)}, bf16[512,256]{1,0:T(8,128)(2,1)S(1)}, u32[]{:S(2)}, u32[]{:S(2)}) collective-permute-start(bf16[512,256]{1,0:T(8,128)(2,1)S(1)} %gate_up_fall_1.1), channel_id=1, source_target_pairs={{0,896},{128,0},{256,128},{384,256},{512,384},{640,512},{768,640},... | collective-permute-start | bytes 786440 | tf_op jit(solution)/shard_map/ppermute | solution.py:149
  124.8 9.0 %collective-permute-start.3 = (bf16[512,256]{1,0:T(8,128)(2,1)S(1)}, bf16[512,256]{1,0:T(8,128)(2,1)}, u32[]{:S(2)}, u32[]{:S(2)}) collective-permute-start(bf16[512,256]{1,0:T(8,128)(2,1)S(1)} %gate_up_rise_1.1), channel_id=1, source_target_pairs={{0,128},{128,256},{256,384},{384,512},{512,640},{640,768},{768,896... | collective-permute-start | bytes 786440 | tf_op jit(solution)/shard_map/ppermute | solution.py:149
  127.1 0.8 copy-start.3
  127.9 5.9 %copy-start.7 = (bf16[512,256]{1,0:T(8,128)(2,1)}, bf16[512,256]{1,0:T(8,128)(2,1)S(1)}, u32[]{:S(2)}) copy-start(bf16[512,256]{1,0:T(8,128)(2,1)S(1)} %collective-permute-done.6.down_ref) | copy-start | bytes 786436
  137.1 8.5 %collective-permute-start.7 = (bf16[512,256]{1,0:T(8,128)(2,1)}, bf16[512,256]{1,0:T(8,128)(2,1)S(1)}, u32[]{:S(2)}, u32[]{:S(2)}) collective-permute-start(bf16[512,256]{1,0:T(8,128)(2,1)} %activate.1.refs_1_), channel_id=1, source_target_pairs={{0,128},{128,256},{256,384},{384,512},{512,640},{640,768},{768,896... | collective-permute-start | bytes 786440 | tf_op jit(solution)/shard_map/ppermute | solution.py:149
  139.0 8.5 %collective-permute-start.11 = (bf16[512,256]{1,0:T(8,128)(2,1)}, bf16[512,256]{1,0:T(8,128)(2,1)S(1)}, u32[]{:S(2)}, u32[]{:S(2)}) collective-permute-start(bf16[512,256]{1,0:T(8,128)(2,1)} %activate.1.refs_1_), channel_id=1, source_target_pairs={{0,896},{128,0},{256,128},{384,256},{512,384},{640,512},{768,640},... | collective-permute-start | bytes 786440 | tf_op jit(solution)/shard_map/ppermute | solution.py:149
  145.6 8.3 %collective-permute-start.8 = (bf16[512,256]{1,0:T(8,128)(2,1)S(1)}, bf16[512,256]{1,0:T(8,128)(2,1)S(1)}, u32[]{:S(2)}, u32[]{:S(2)}) collective-permute-start(bf16[512,256]{1,0:T(8,128)(2,1)S(1)} %collective-permute-done.7.refs_2_), channel_id=1, source_target_pairs={{0,128},{128,256},{256,384},{384,512},{512,640},{640,768},{768,896... | collective-permute-start | bytes 786440 | tf_op jit(solution)/shard_map/ppermute | solution.py:149
  147.5 8.3 %collective-permute-start.12 = (bf16[512,256]{1,0:T(8,128)(2,1)S(1)}, bf16[512,256]{1,0:T(8,128)(2,1)S(1)}, u32[]{:S(2)}, u32[]{:S(2)}) collective-permute-start(bf16[512,256]{1,0:T(8,128)(2,1)S(1)} %collective-permute-done.11.refs_3_), channel_id=1, source_target_pairs={{0,896},{128,0},{256,128},{384,256},{512,384},{640,512},{768,640},... | collective-permute-start | bytes 786440 | tf_op jit(solution)/shard_map/ppermute | solution.py:149
  153.9 8.3 %collective-permute-start.9 = (bf16[512,256]{1,0:T(8,128)(2,1)S(1)}, bf16[512,256]{1,0:T(8,128)(2,1)S(1)}, u32[]{:S(2)}, u32[]{:S(2)}) collective-permute-start(bf16[512,256]{1,0:T(8,128)(2,1)S(1)} %collective-permute-done.8.refs_4_), channel_id=1, source_target_pairs={{0,128},{128,256},{256,384},{384,512},{512,640},{640,768},{768,896... | collective-permute-start | bytes 786440 | tf_op jit(solution)/shard_map/ppermute | solution.py:149
  155.9 8.3 %collective-permute-start.13 = (bf16[512,256]{1,0:T(8,128)(2,1)S(1)}, bf16[512,256]{1,0:T(8,128)(2,1)S(1)}, u32[]{:S(2)}, u32[]{:S(2)}) collective-permute-start(bf16[512,256]{1,0:T(8,128)(2,1)S(1)} %collective-permute-done.12.refs_5_), channel_id=1, source_target_pairs={{0,896},{128,0},{256,128},{384,256},{512,384},{640,512},{768,640},... | collective-permute-start | bytes 786440 | tf_op jit(solution)/shard_map/ppermute | solution.py:149
  162.2 8.5 %collective-permute-start.10 = (bf16[512,256]{1,0:T(8,128)(2,1)S(1)}, bf16[512,256]{1,0:T(8,128)(2,1)S(1)}, u32[]{:S(2)}, u32[]{:S(2)}) collective-permute-start(bf16[512,256]{1,0:T(8,128)(2,1)S(1)} %collective-permute-done.9.refs_6_), channel_id=1, source_target_pairs={{0,128},{128,256},{256,384},{384,512},{512,640},{640,768},{768,896... | collective-permute-start | bytes 786440 | tf_op jit(solution)/shard_map/ppermute | solution.py:149
  164.2 1.2 copy-start.2
  165.4 0.9 copy-start.5
  171.1 36.0 %copy-start.8 = (bf16[32,512]{1,0:T(8,128)(2,1)S(1)}, bf16[32,512]{1,0:T(8,128)(2,1)}, u32[]{:S(2)}) copy-start(bf16[32,512]{1,0:T(8,128)(2,1)} %get-tuple-element.8) | copy-start | bytes 98308
Sparse Core Ops, SparseCore 0:
  52.7 48.6 reduce-scatter.1

commit v5 on v4

--- a/solution.py
+++ b/solution.py
@@ -91,57 +91,61 @@
     )(expert_ids.T, route_weights.T, tokens, out_grad)
 
 
-def hidden_kernel(rows_ref, w_ref, out_ref):
-    part = out_ref.shape[2]
-    out = lax.dot_general(rows_ref[...], w_ref[0], TRANS_B, preferred_element_type=F32)
-    for j in range(out_ref.shape[0]):
-        out_ref[j] = out[:, j * part : (j + 1) * part]
-
-
-def hidden_parts(dy_rows, w_down, n_rep):
-    rows, width = dy_rows.shape
-    part = w_down.shape[1] // n_rep
-    per = 2
-    return pl.pallas_call(
-        hidden_kernel,
-        grid=(n_rep // per,),
-        in_specs=[
-            pl.BlockSpec((rows, width), lambda c: (0, 0)),
-            pl.BlockSpec((1, per * part, width), lambda c: (0, c, 0)),
-        ],
-        out_specs=pl.BlockSpec((per, rows, part), lambda c: (c, 0, 0)),
-        out_shape=jax.ShapeDtypeStruct((n_rep, rows, part), F32),
-        compiler_params=params(),
-        name="hidden",
-    )(dy_rows, w_down)
+def chunk_start(me_ref, offset, n_rep, part):
+    return pl.multiple_of(lax.rem(me_ref[0] + offset, n_rep) * part, part)
 
 
 def chunk_weights(me_ref, offset, n_rep, wg_ref, wu_ref):
     part = wg_ref.shape[2] // n_rep
-    c = lax.rem(me_ref[0] + offset, n_rep)
-    cols = pl.ds(pl.multiple_of(c * part, part), part)
+    cols = pl.ds(chunk_start(me_ref, offset, n_rep, part), part)
     return jnp.concatenate([wg_ref[0, :, cols], wu_ref[0, :, cols]], axis=1)
 
 
-def gate_up_kernel(offset, n_rep, me_ref, rows_ref, wg_ref, wu_ref, *refs):
-    weights = chunk_weights(me_ref, offset, n_rep, wg_ref, wu_ref)
-    total = jnp.dot(rows_ref[...], weights, preferred_element_type=F32)
+def gate_up_kernel(x_ref, wg_ref, wu_ref, out_ref):
+    per = out_ref.shape[0]
+    part = wg_ref.shape[2] // per
+    for j in range(per):
+        cols = slice(j * part, (j + 1) * part)
+        weights = jnp.concatenate([wg_ref[0, :, cols], wu_ref[0, :, cols]], axis=1)
+        out_ref[j] = jnp.dot(x_ref[...], weights, preferred_element_type=F32)
+
+
+def gate_up_parts(x_rows, w_gate, w_up, n_rep):
+    rows, width = x_rows.shape
+    part = w_gate.shape[2] // n_rep
+    per = 2
+    w_spec = pl.BlockSpec((1, width, per * part), lambda c: (0, 0, c))
+    return pl.pallas_call(
+        gate_up_kernel,
+        grid=(n_rep // per,),
+        in_specs=[pl.BlockSpec((rows, width), lambda c: (0, 0)), w_spec, w_spec],
+        out_specs=pl.BlockSpec((per, rows, 2 * part), lambda c: (c, 0, 0)),
+        out_shape=jax.ShapeDtypeStruct((n_rep, rows, 2 * part), F32),
+        compiler_params=params(62),
+        name="gate_up",
+    )(x_rows, w_gate, w_up)
+
+
+def hidden_kernel(offset, n_rep, me_ref, rows_ref, w_ref, *refs):
+    part = w_ref.shape[1] // n_rep
+    weights = w_ref[0, pl.ds(chunk_start(me_ref, offset, n_rep, part), part), :]
+    total = lax.dot_general(rows_ref[...], weights, TRANS_B, preferred_element_type=F32)
     for arrived in refs[:-1]:
         total = total + arrived[...].astype(F32)
     refs[-1][...] = total.astype(refs[-1].dtype)
 
 
-def gate_up(me, x_rows, w_gate, w_up, n_rep, offset, arrived, dtype, name):
-    rows = x_rows.shape[0]
-    part = w_gate.shape[2] // n_rep
-    return pl.pallas_call(
-        lambda *refs: gate_up_kernel(offset, n_rep, *refs),
-        in_specs=[pl.BlockSpec(memory_space=pltpu.SMEM)] + [VMEM_SPEC] * (3 + len(arrived)),
+def hidden_term(me, dy_rows, w_down, n_rep, offset, arrived, dtype, name):
+    rows = dy_rows.shape[0]
+    part = w_down.shape[1] // n_rep
+    return pl.pallas_call(
+        lambda *refs: hidden_kernel(offset, n_rep, *refs),
+        in_specs=[pl.BlockSpec(memory_space=pltpu.SMEM)] + [VMEM_SPEC] * (2 + len(arrived)),
         out_specs=VMEM_SPEC,
-        out_shape=jax.ShapeDtypeStruct((rows, 2 * part), dtype),
+        out_shape=jax.ShapeDtypeStruct((rows, part), dtype),
         compiler_params=params(),
         name=name,
-    )(me, x_rows, w_gate, w_up, *arrived)
+    )(me, dy_rows, w_down, *arrived)
 
 
 def shift(rows, by):
@@ -149,47 +153,45 @@
     return lax.ppermute(rows, "rep", [(i, (i + by) % n_rep) for i in range(n_rep)])
 
 
-def gate_up_sums(me, x_rows, w_gate, w_up, n_rep):
+def hidden_sums(me, dy_rows, w_down, n_rep):
     half = n_rep // 2
     up, down = (), ()
     for hop in range(half, 0, -1):
-        term = gate_up(
-            me, x_rows, w_gate, w_up, n_rep, hop, up, BF16, "gate_up_rise_%d" % hop
-        )
+        term = hidden_term(me, dy_rows, w_down, n_rep, hop, up, BF16, "hidden_rise_%d" % hop)
         up = (shift(term, 1),)
         if hop < half:
-            term = gate_up(
-                me, x_rows, w_gate, w_up, n_rep, n_rep - hop, down, BF16, "gate_up_fall_%d" % hop
+            term = hidden_term(
+                me, dy_rows, w_down, n_rep, n_rep - hop, down, BF16, "hidden_fall_%d" % hop
             )
             down = (shift(term, -1),)
-    own = gate_up(me, x_rows, w_gate, w_up, n_rep, 0, (), F32, "gate_up_own")
+    own = hidden_term(me, dy_rows, w_down, n_rep, 0, (), F32, "hidden_own")
     return own, up[0], down[0]
 
 
-def activate_kernel(h_ref, own_ref, up_ref, down_ref, out_ref):
-    part = h_ref.shape[1]
-    sums = own_ref[...] + up_ref[...].astype(F32) + down_ref[...].astype(F32)
-    hidden = h_ref[...]
-    gate = sums[:, :part]
-    up = sums[:, part:]
+def activate_kernel(gu_ref, own_ref, up_ref, down_ref, out_ref):
+    part = own_ref.shape[1]
+    hidden = own_ref[...] + up_ref[...].astype(F32) + down_ref[...].astype(F32)
+    gate = gu_ref[:, :part]
+    up = gu_ref[:, part:]
     s = jax.nn.sigmoid(gate)
     out_ref[:, :part] = (hidden * up * s * (1.0 + gate * (1.0 - s))).astype(BF16)
     out_ref[:, part:] = (hidden * gate * s).astype(BF16)
 
 
-def activate(hidden, own, up, down):
-    rows, part2 = own.shape
-    block = 128
-    spec = pl.BlockSpec((block, part2), lambda i: (i, 0))
+def activate(gate_up, own, up, down):
+    rows, part = own.shape
+    block = rows // 2
+    spec = pl.BlockSpec((block, part), lambda i: (i, 0))
+    wide = pl.BlockSpec((block, 2 * part), lambda i: (i, 0))
     return pl.pallas_call(
         activate_kernel,
         grid=(rows // block,),
-        in_specs=[pl.BlockSpec((block, part2 // 2), lambda i: (i, 0)), spec, spec, spec],
-        out_specs=spec,
-        out_shape=jax.ShapeDtypeStruct(own.shape, BF16),
+        in_specs=[wide, spec, spec, spec],
+        out_specs=wide,
+        out_shape=jax.ShapeDtypeStruct((rows, 2 * part), BF16),
         compiler_params=params(62),
         name="activate",
-    )(hidden, own, up, down)
+    )(gate_up, own, up, down)
 
 
 def row_grad_kernel(offsets, has_start, n_rep, me_ref, *refs):
@@ -248,13 +250,12 @@
         blocks = rows.reshape(experts, capacity, width)
         return lax.all_to_all(blocks, ("outer", "local"), 0, 0, tiled=True).reshape(slots, width)
 
+    x_rows = exchange(send_x)
+    gate_up = lax.psum_scatter(
+        gate_up_parts(x_rows, gate_weight, up_weight, n_rep), "rep", scatter_dimension=0
+    )
     dy_rows = exchange(send_dy)
-    hidden = lax.psum_scatter(
-        hidden_parts(dy_rows, down_weight, n_rep), "rep", scatter_dimension=0
-    )
-    x_rows = exchange(send_x)
-    sums = gate_up_sums(me, x_rows, gate_weight, up_weight, n_rep)
-    own = activate(hidden, *sums)
+    own = activate(gate_up, *hidden_sums(me, dy_rows, down_weight, n_rep))
     returned = exchange(gather_matmul(me, own, gate_weight, up_weight, n_rep))
     return jnp.dot(per_token_t, returned, preferred_element_type=F32).astype(BF16)
 

time: 216 us -> 214 us (level)
  waiting for transfers between devices: 47.6 us -> 44 us
    ppermute x14, waiting for transfers between devices: 27.9 us -> 23.4 us  [shift(): lax.ppermute(rows, 'rep', [(i, (i + by) % n_rep) for i in range(n_rep)])]
  transfers between devices with their start and end apart: 16 -> 16, of which waited for: 9 -> 9; matrix products, arithmetic and copies ran while one was open for 1% -> 0% of each run, Pallas kernels for 2% -> 2%
where the time goes in v5:
time: 214 us; the launch traced here: 213 us
  blocking collectives  76.5 us (36%)
  starting transfers between devices  57.1 us (27%)
  waiting for transfers between devices  44 us (21%)
  between operations  13.7 us (6%)
  Pallas kernels  13.6 us (6%)
  local copies, waits for them, and re-layouts  6.93 us (3%)
    all_to_all x2, blocking collectives, exchange(): lax.all_to_all(blocks, ('outer', 'local'), 0, 0, tiled=True)  76.5 us
    ppermute x14, starting transfers between devices, shift(): lax.ppermute(rows, 'rep', [(i, (i + by) % n_rep) for i in range(n_rep)])  51.7 us
    ppermute x14, waiting for transfers between devices, shift(): lax.ppermute(rows, 'rep', [(i, (i + by) % n_rep) for i in range(n_rep)])  23.4 us
    all_to_all x1, waiting for transfers between devices, exchange(): lax.all_to_all(blocks, ('outer', 'local'), 0, 0, tiled=True)  20.6 us
    all_to_all x1, starting transfers between devices, exchange(): lax.all_to_all(blocks, ('outer', 'local'), 0, 0, tiled=True)  5.41 us
    pallas_call x1, Pallas kernels, gate_up_parts(): pl.pallas_call(gate_up_kernel, grid=(n_rep // per,), in_specs=[pl.BlockSp...  5.19 us
  transfers between devices with their start and end apart: 16, of which 9 were waited for; matrix products, arithmetic and copies ran while one was open for 0% of the time, Pallas kernels for 2%

profile of v5, /device:TPU:1, one launch (start us, length us, event | category | flops | bytes accessed | tf_op | source)
XLA Modules:
  0.0 212.7 jit_solution(3836344446311451760)
XLA Ops:
  6.5 0.0 reduce-scatter.2.cloned.1.call-start
  6.5 2.6 %route.1 = (bf16[512,512]{1,0:T(8,128)(2,1)}, bf16[512,512]{1,0:T(8,128)(2,1)}, bf16[32,512]{1,0:T(8,128)(2,1)}) custom-call(s32[8,32]{1,0:T(8,128)} %bitcast.7, f32[8,32]{1,0:T(8,128)} %bitcast.8, bf16[32,512]{1,0:T(8,128)(2,1)} %refs_2_.10, bf16[32,512]{1,0:T(8,128)(2,1)} %refs_3_.2), custom_call_target="tpu_custom_call" | custom-call | tf_op jit(solution)/shard_map/route/pallas_call | solution.py:72
  9.2 1.2 reshape.22
  10.3 39.4 %all_to_all.15 = bf16[128,4,512]{2,1,0:T(4,128)(2,1)S(1)} all-to-all(bf16[128,4,512]{2,1,0:T(4,128)(2,1)S(1)} %reshape.22), channel_id=1, replica_groups=mesh['rep'=8,'outer'=8,'local'=16] {'outer','local'}, dimensions={0} | all-to-all | bytes 1048576 | tf_op jit(solution)/shard_map/all_to_all | solution.py:251
  49.7 0.9 reshape.23.x_ref
  50.6 5.2 %gate_up.1 = f32[8,512,256]{2,1,0:T(8,128)} custom-call(bf16[512,512]{1,0:T(8,128)(2,1)} %reshape.23.x_ref, bf16[1,512,1024]{2,1,0:T(8,128)(2,1)} %refs_2_.19, bf16[1,512,1024]{2,1,0:T(8,128)(2,1)} %refs_3_.3), custom_call_target="tpu_custom_call" | custom-call | tf_op jit(solution)/shard_map/gate_up/pallas_call | solution.py:118
  55.8 0.0 reduce-scatter.2.cloned.1.call-update
  55.8 0.0 copy-done.5
  55.9 0.9 reshape.24
  56.8 5.4 %all-to-all-start.1 = ((bf16[128,4,512]{2,1,0:T(4,128)(2,1)}), bf16[128,4,512]{2,1,0:T(4,128)(2,1)S(1)}, u32[]{:S(2)}, u32[]{:S(2)}) async-start(bf16[128,4,512]{2,1,0:T(4,128)(2,1)} %reshape.24), calls=%async_computation.2 | async-start | bytes 1048576 | tf_op jit(solution)/shard_map/all_to_all | solution.py:251
  62.2 20.6 %all-to-all-done.1 = bf16[128,4,512]{2,1,0:T(4,128)(2,1)S(1)} async-done(((bf16[128,4,512]{2,1,0:T(4,128)(2,1)}), bf16[128,4,512]{2,1,0:T(4,128)(2,1)S(1)}, u32[]{:S(2)}, u32[]{:S(2)}) %all-to-all-start.1) | async-done | bytes 524320 | tf_op jit(solution)/shard_map/all_to_all | solution.py:251
  82.8 0.1 reshape.25.refs_1_
  82.9 0.0 copy-done
  82.9 0.3 hidden_rise_4.1
  83.2 1.9 collective-permute-start
  85.1 0.3 hidden_fall_3.1
  85.5 13.4 %collective-permute-start.4 = (bf16[512,128]{1,0:T(8,128)(2,1)S(1)}, bf16[512,128]{1,0:T(8,128)(2,1)S(1)}, u32[]{:S(2)}, u32[]{:S(2)}) collective-permute-start(bf16[512,128]{1,0:T(8,128)(2,1)S(1)} %hidden_fall_3.1), channel_id=1, source_target_pairs={{0,896},{128,0},{256,128},{384,256},{512,384},{640,512},{768,640},... | collective-permute-start | bytes 393224 | tf_op jit(solution)/shard_map/ppermute | solution.py:153
  98.8 4.7 %collective-permute-done.refs_3_ = bf16[512,128]{1,0:T(8,128)(2,1)S(1)} collective-permute-done((bf16[512,128]{1,0:T(8,128)(2,1)S(1)}, bf16[512,128]{1,0:T(8,128)(2,1)S(1)}, u32[]{:S(2)}, u32[]{:S(2)}) %collective-permute-start) | collective-permute-done | bytes 131104 | tf_op jit(solution)/shard_map/ppermute | solution.py:153
  103.5 0.3 hidden_rise_3.1
  103.8 1.9 collective-permute-start.1
  105.8 0.0 collective-permute-done.4.refs_3_
  105.8 0.3 hidden_fall_2.1
  106.1 0.0 copy-start.1
  106.1 4.7 %collective-permute-start.5 = (bf16[512,128]{1,0:T(8,128)(2,1)S(1)}, bf16[512,128]{1,0:T(8,128)(2,1)S(1)}, u32[]{:S(2)}, u32[]{:S(2)}) collective-permute-start(bf16[512,128]{1,0:T(8,128)(2,1)S(1)} %hidden_fall_2.1), channel_id=1, source_target_pairs={{0,896},{128,0},{256,128},{384,256},{512,384},{640,512},{768,640},... | collective-permute-start | bytes 393224 | tf_op jit(solution)/shard_map/ppermute | solution.py:153
  110.8 4.5 %collective-permute-done.1.refs_3_ = bf16[512,128]{1,0:T(8,128)(2,1)S(1)} collective-permute-done((bf16[512,128]{1,0:T(8,128)(2,1)S(1)}, bf16[512,128]{1,0:T(8,128)(2,1)S(1)}, u32[]{:S(2)}, u32[]{:S(2)}) %collective-permute-start.1) | collective-permute-done | bytes 131104 | tf_op jit(solution)/shard_map/ppermute | solution.py:153
  115.3 0.3 hidden_rise_2.1
  115.6 1.9 collective-permute-start.2
  117.6 0.0 collective-permute-done.5.refs_3_
  117.6 0.3 hidden_fall_1.1
  117.9 4.6 %collective-permute-start.6 = (bf16[512,128]{1,0:T(8,128)(2,1)S(1)}, bf16[512,128]{1,0:T(8,128)(2,1)S(1)}, u32[]{:S(2)}, u32[]{:S(2)}) collective-permute-start(bf16[512,128]{1,0:T(8,128)(2,1)S(1)} %hidden_fall_1.1), channel_id=1, source_target_pairs={{0,896},{128,0},{256,128},{384,256},{512,384},{640,512},{768,640},... | collective-permute-start | bytes 393224 | tf_op jit(solution)/shard_map/ppermute | solution.py:153
  122.5 1.5 collective-permute-done.2.refs_3_
  124.0 0.3 hidden_rise_1.1
  124.3 1.9 collective-permute-start.3
  126.2 0.3 hidden_own.1.own_ref
  126.5 0.0 copy-start.4
  126.6 0.7 copy-done.4
  127.3 0.0 collective-permute-done.6.down_ref
  127.3 4.0 %collective-permute-done.3.up_ref = bf16[512,128]{1,0:T(8,128)(2,1)S(1)} collective-permute-done((bf16[512,128]{1,0:T(8,128)(2,1)S(1)}, bf16[512,128]{1,0:T(8,128)(2,1)S(1)}, u32[]{:S(2)}, u32[]{:S(2)}) %collective-permute-start.3) | collective-permute-done | bytes 131104 | tf_op jit(solution)/shard_map/ppermute | solution.py:153
  131.2 0.6 copy-done.7
  131.9 1.9 activate.1.refs_1_
  133.8 1.9 collective-permute-start.7
  135.7 4.6 %collective-permute-start.11 = (bf16[512,256]{1,0:T(8,128)(2,1)}, bf16[512,256]{1,0:T(8,128)(2,1)S(1)}, u32[]{:S(2)}, u32[]{:S(2)}) collective-permute-start(bf16[512,256]{1,0:T(8,128)(2,1)} %activate.1.refs_1_), channel_id=1, source_target_pairs={{0,896},{128,0},{256,128},{384,256},{512,384},{640,512},{768,640},... | collective-permute-start | bytes 786440 | tf_op jit(solution)/shard_map/ppermute | solution.py:153
  140.3 2.0 collective-permute-done.7.refs_2_
  142.3 1.9 collective-permute-start.8
  144.3 0.0 collective-permute-done.11.refs_3_
  144.3 4.6 %collective-permute-start.12 = (bf16[512,256]{1,0:T(8,128)(2,1)S(1)}, bf16[512,256]{1,0:T(8,128)(2,1)S(1)}, u32[]{:S(2)}, u32[]{:S(2)}) collective-permute-start(bf16[512,256]{1,0:T(8,128)(2,1)S(1)} %collective-permute-done.11.refs_3_), channel_id=1, source_target_pairs={{0,896},{128,0},{256,128},{384,256},{512,384},{640,512},{768,640},... | collective-permute-start | bytes 786440 | tf_op jit(solution)/shard_map/ppermute | solution.py:153
  148.8 1.8 collective-permute-done.8.refs_4_
  150.7 1.9 collective-permute-start.9
  152.6 0.0 collective-permute-done.12.refs_5_
  152.6 4.6 %collective-permute-start.13 = (bf16[512,256]{1,0:T(8,128)(2,1)S(1)}, bf16[512,256]{1,0:T(8,128)(2,1)S(1)}, u32[]{:S(2)}, u32[]{:S(2)}) collective-permute-start(bf16[512,256]{1,0:T(8,128)(2,1)S(1)} %collective-permute-done.12.refs_5_), channel_id=1, source_target_pairs={{0,896},{128,0},{256,128},{384,256},{512,384},{640,512},{768,640},... | collective-permute-start | bytes 786440 | tf_op jit(solution)/shard_map/ppermute | solution.py:153
  157.2 1.8 collective-permute-done.9.refs_6_
  159.0 1.9 collective-permute-start.10
  160.9 0.0 collective-permute-done.13.refs_7_
  160.9 0.0 copy-start.2
  160.9 1.2 copy-done.2
  162.1 0.9 copy-done.3
  163.1 1.2 row_grad_near.1.refs_4_
  164.3 0.0 copy-start.8
  164.3 3.0 %collective-permute-done.10.refs_1_ = bf16[512,256]{1,0:T(8,128)(2,1)S(1)} collective-permute-done((bf16[512,256]{1,0:T(8,128)(2,1)S(1)}, bf16[512,256]{1,0:T(8,128)(2,1)S(1)}, u32[]{:S(2)}, u32[]{:S(2)}) %collective-permute-start.10) | collective-permute-done | bytes 262176 | tf_op jit(solution)/shard_map/ppermute | solution.py:153
  167.3 0.3 row_grad_far.1
  167.6 0.1 reshape.26
  167.8 37.1 %all_to_all.16 = bf16[128,4,512]{2,1,0:T(4,128)(2,1)S(1)} all-to-all(bf16[128,4,512]{2,1,0:T(4,128)(2,1)S(1)} %reshape.26), channel_id=1, replica_groups=mesh['rep'=8,'outer'=8,'local'=16] {'outer','local'}, dimensions={0} | all-to-all | bytes 1048576 | tf_op jit(solution)/shard_map/all_to_all | solution.py:251
  204.9 0.1 reshape.27
  205.0 0.8 convolution_convert_fusion
  (9 shorter events, 0.0 us)
Async XLA Ops:
  6.5 124.7 %reduce-scatter.2.cloned.1.call-start = ((), (), s32[]{:S(2)}) async-start(), calls=%async_computation.4 | async-start | bytes 4718592 | tf_op jit(solution)/shard_map/reduce_scatter | solution.py:254
  50.6 5.2 %copy-start.5 = (bf16[512,512]{1,0:T(8,128)(2,1)S(1)}, bf16[512,512]{1,0:T(8,128)(2,1)}, u32[]{:S(2)}) copy-start(bf16[512,512]{1,0:T(8,128)(2,1)} %get-tuple-element.10) | copy-start | bytes 1572868
  55.8 27.1 %copy-start = (bf16[1,1024,512]{2,1,0:T(8,128)(2,1)S(1)}, bf16[1,1024,512]{2,1,0:T(8,128)(2,1)}, u32[]{:S(2)}) copy-start(bf16[1,1024,512]{2,1,0:T(8,128)(2,1)} %refs_2_.18) | copy-start | bytes 3145732
  56.8 26.0 %all-to-all-start.1 = ((bf16[128,4,512]{2,1,0:T(4,128)(2,1)}), bf16[128,4,512]{2,1,0:T(4,128)(2,1)S(1)}, u32[]{:S(2)}, u32[]{:S(2)}) async-start(bf16[128,4,512]{2,1,0:T(4,128)(2,1)} %reshape.24), calls=%async_computation.2 | async-start | bytes 1048576 | tf_op jit(solution)/shard_map/all_to_all | solution.py:251
  83.2 20.3 %collective-permute-start = (bf16[512,128]{1,0:T(8,128)(2,1)S(1)}, bf16[512,128]{1,0:T(8,128)(2,1)S(1)}, u32[]{:S(2)}, u32[]{:S(2)}) collective-permute-start(bf16[512,128]{1,0:T(8,128)(2,1)S(1)} %hidden_rise_4.1), channel_id=1, source_target_pairs={{0,128},{128,256},{256,384},{384,512},{512,640},{640,768},{768,896... | collective-permute-start | bytes 393224 | tf_op jit(solution)/shard_map/ppermute | solution.py:153
  85.5 20.3 %collective-permute-start.4 = (bf16[512,128]{1,0:T(8,128)(2,1)S(1)}, bf16[512,128]{1,0:T(8,128)(2,1)S(1)}, u32[]{:S(2)}, u32[]{:S(2)}) collective-permute-start(bf16[512,128]{1,0:T(8,128)(2,1)S(1)} %hidden_fall_3.1), channel_id=1, source_target_pairs={{0,896},{128,0},{256,128},{384,256},{512,384},{640,512},{768,640},... | collective-permute-start | bytes 393224 | tf_op jit(solution)/shard_map/ppermute | solution.py:153
  103.8 11.5 %collective-permute-start.1 = (bf16[512,128]{1,0:T(8,128)(2,1)S(1)}, bf16[512,128]{1,0:T(8,128)(2,1)S(1)}, u32[]{:S(2)}, u32[]{:S(2)}) collective-permute-start(bf16[512,128]{1,0:T(8,128)(2,1)S(1)} %hidden_rise_3.1), channel_id=1, source_target_pairs={{0,128},{128,256},{256,384},{384,512},{512,640},{640,768},{768,896... | collective-permute-start | bytes 393224 | tf_op jit(solution)/shard_map/ppermute | solution.py:153
  106.1 54.8 %copy-start.1 = (bf16[1,512,1024]{2,1,0:T(8,128)(2,1)S(1)}, bf16[1,512,1024]{2,1,0:T(8,128)(2,1)}, u32[]{:S(2)}) copy-start(bf16[1,512,1024]{2,1,0:T(8,128)(2,1)} %refs_2_.19) | copy-start | bytes 3145732
  106.1 11.5 %collective-permute-start.5 = (bf16[512,128]{1,0:T(8,128)(2,1)S(1)}, bf16[512,128]{1,0:T(8,128)(2,1)S(1)}, u32[]{:S(2)}, u32[]{:S(2)}) collective-permute-start(bf16[512,128]{1,0:T(8,128)(2,1)S(1)} %hidden_fall_2.1), channel_id=1, source_target_pairs={{0,896},{128,0},{256,128},{384,256},{512,384},{640,512},{768,640},... | collective-permute-start | bytes 393224 | tf_op jit(solution)/shard_map/ppermute | solution.py:153
  115.6 8.4 %collective-permute-start.2 = (bf16[512,128]{1,0:T(8,128)(2,1)S(1)}, bf16[512,128]{1,0:T(8,128)(2,1)S(1)}, u32[]{:S(2)}, u32[]{:S(2)}) collective-permute-start(bf16[512,128]{1,0:T(8,128)(2,1)S(1)} %hidden_rise_2.1), channel_id=1, source_target_pairs={{0,128},{128,256},{256,384},{384,512},{512,640},{640,768},{768,896... | collective-permute-start | bytes 393224 | tf_op jit(solution)/shard_map/ppermute | solution.py:153
  117.9 9.4 %collective-permute-start.6 = (bf16[512,128]{1,0:T(8,128)(2,1)S(1)}, bf16[512,128]{1,0:T(8,128)(2,1)S(1)}, u32[]{:S(2)}, u32[]{:S(2)}) collective-permute-start(bf16[512,128]{1,0:T(8,128)(2,1)S(1)} %hidden_fall_1.1), channel_id=1, source_target_pairs={{0,896},{128,0},{256,128},{384,256},{512,384},{640,512},{768,640},... | collective-permute-start | bytes 393224 | tf_op jit(solution)/shard_map/ppermute | solution.py:153
  124.3 6.9 %collective-permute-start.3 = (bf16[512,128]{1,0:T(8,128)(2,1)S(1)}, bf16[512,128]{1,0:T(8,128)(2,1)S(1)}, u32[]{:S(2)}, u32[]{:S(2)}) collective-permute-start(bf16[512,128]{1,0:T(8,128)(2,1)S(1)} %hidden_rise_1.1), channel_id=1, source_target_pairs={{0,128},{128,256},{256,384},{384,512},{512,640},{640,768},{768,896... | collective-permute-start | bytes 393224 | tf_op jit(solution)/shard_map/ppermute | solution.py:153
  126.5 0.7 copy-start.4
  127.3 4.0 %copy-start.6 = (bf16[512,128]{1,0:T(8,128)(2,1)}, bf16[512,128]{1,0:T(8,128)(2,1)S(1)}, u32[]{:S(2)}) copy-start(bf16[512,128]{1,0:T(8,128)(2,1)S(1)} %collective-permute-done.6.down_ref) | copy-start | bytes 393220
  131.2 0.6 copy-start.7
  133.8 8.5 %collective-permute-start.7 = (bf16[512,256]{1,0:T(8,128)(2,1)}, bf16[512,256]{1,0:T(8,128)(2,1)S(1)}, u32[]{:S(2)}, u32[]{:S(2)}) collective-permute-start(bf16[512,256]{1,0:T(8,128)(2,1)} %activate.1.refs_1_), channel_id=1, source_target_pairs={{0,128},{128,256},{256,384},{384,512},{512,640},{640,768},{768,896... | collective-permute-start | bytes 786440 | tf_op jit(solution)/shard_map/ppermute | solution.py:153
  135.7 8.5 %collective-permute-start.11 = (bf16[512,256]{1,0:T(8,128)(2,1)}, bf16[512,256]{1,0:T(8,128)(2,1)S(1)}, u32[]{:S(2)}, u32[]{:S(2)}) collective-permute-start(bf16[512,256]{1,0:T(8,128)(2,1)} %activate.1.refs_1_), channel_id=1, source_target_pairs={{0,896},{128,0},{256,128},{384,256},{512,384},{640,512},{768,640},... | collective-permute-start | bytes 786440 | tf_op jit(solution)/shard_map/ppermute | solution.py:153
  142.3 8.3 %collective-permute-start.8 = (bf16[512,256]{1,0:T(8,128)(2,1)S(1)}, bf16[512,256]{1,0:T(8,128)(2,1)S(1)}, u32[]{:S(2)}, u32[]{:S(2)}) collective-permute-start(bf16[512,256]{1,0:T(8,128)(2,1)S(1)} %collective-permute-done.7.refs_2_), channel_id=1, source_target_pairs={{0,128},{128,256},{256,384},{384,512},{512,640},{640,768},{768,896... | collective-permute-start | bytes 786440 | tf_op jit(solution)/shard_map/ppermute | solution.py:153
  144.3 8.3 %collective-permute-start.12 = (bf16[512,256]{1,0:T(8,128)(2,1)S(1)}, bf16[512,256]{1,0:T(8,128)(2,1)S(1)}, u32[]{:S(2)}, u32[]{:S(2)}) collective-permute-start(bf16[512,256]{1,0:T(8,128)(2,1)S(1)} %collective-permute-done.11.refs_3_), channel_id=1, source_target_pairs={{0,896},{128,0},{256,128},{384,256},{512,384},{640,512},{768,640},... | collective-permute-start | bytes 786440 | tf_op jit(solution)/shard_map/ppermute | solution.py:153
  150.7 8.3 %collective-permute-start.9 = (bf16[512,256]{1,0:T(8,128)(2,1)S(1)}, bf16[512,256]{1,0:T(8,128)(2,1)S(1)}, u32[]{:S(2)}, u32[]{:S(2)}) collective-permute-start(bf16[512,256]{1,0:T(8,128)(2,1)S(1)} %collective-permute-done.8.refs_4_), channel_id=1, source_target_pairs={{0,128},{128,256},{256,384},{384,512},{512,640},{640,768},{768,896... | collective-permute-start | bytes 786440 | tf_op jit(solution)/shard_map/ppermute | solution.py:153
  152.6 8.3 %collective-permute-start.13 = (bf16[512,256]{1,0:T(8,128)(2,1)S(1)}, bf16[512,256]{1,0:T(8,128)(2,1)S(1)}, u32[]{:S(2)}, u32[]{:S(2)}) collective-permute-start(bf16[512,256]{1,0:T(8,128)(2,1)S(1)} %collective-permute-done.12.refs_5_), channel_id=1, source_target_pairs={{0,896},{128,0},{256,128},{384,256},{512,384},{640,512},{768,640},... | collective-permute-start | bytes 786440 | tf_op jit(solution)/shard_map/ppermute | solution.py:153
  159.0 8.3 %collective-permute-start.10 = (bf16[512,256]{1,0:T(8,128)(2,1)S(1)}, bf16[512,256]{1,0:T(8,128)(2,1)S(1)}, u32[]{:S(2)}, u32[]{:S(2)}) collective-permute-start(bf16[512,256]{1,0:T(8,128)(2,1)S(1)} %collective-permute-done.9.refs_6_), channel_id=1, source_target_pairs={{0,128},{128,256},{256,384},{384,512},{512,640},{640,768},{768,896... | collective-permute-start | bytes 786440 | tf_op jit(solution)/shard_map/ppermute | solution.py:153
  160.9 1.2 copy-start.2
  162.1 0.9 copy-start.3
  164.3 40.7 %copy-start.8 = (bf16[32,512]{1,0:T(8,128)(2,1)S(1)}, bf16[32,512]{1,0:T(8,128)(2,1)}, u32[]{:S(2)}) copy-start(bf16[32,512]{1,0:T(8,128)(2,1)} %get-tuple-element.8) | copy-start | bytes 98308
Sparse Core Ops, SparseCore 0:
  56.0 66.9 reduce-scatter.1

commit v6 on v5

--- a/solution.py
+++ b/solution.py
@@ -154,23 +154,27 @@
 
 
 def hidden_sums(me, dy_rows, w_down, n_rep):
-    half = n_rep // 2
+    def term(offset, arrived, dtype, name):
+        return hidden_term(me, dy_rows, w_down, n_rep, offset % n_rep, arrived, dtype, name)
+
+    near = min(2, n_rep // 2 - 1)
     up, down = (), ()
-    for hop in range(half, 0, -1):
-        term = hidden_term(me, dy_rows, w_down, n_rep, hop, up, BF16, "hidden_rise_%d" % hop)
-        up = (shift(term, 1),)
-        if hop < half:
-            term = hidden_term(
-                me, dy_rows, w_down, n_rep, n_rep - hop, down, BF16, "hidden_fall_%d" % hop
-            )
-            down = (shift(term, -1),)
-    own = hidden_term(me, dy_rows, w_down, n_rep, 0, (), F32, "hidden_own")
-    return own, up[0], down[0]
-
-
-def activate_kernel(gu_ref, own_ref, up_ref, down_ref, out_ref):
+    for hop in range(near, 0, -1):
+        up = (shift(term(hop, up, BF16, "hidden_rise_%d" % hop), 1),)
+        down = (shift(term(-hop, down, BF16, "hidden_fall_%d" % hop), -1),)
+    straight = tuple(
+        shift(term(far, (), BF16, "hidden_far_%d" % far), far)
+        for far in range(near + 1, n_rep - near)
+    )
+    return (term(0, (), F32, "hidden_own"),) + up + down + straight
+
+
+def activate_kernel(gu_ref, own_ref, *refs):
     part = own_ref.shape[1]
-    hidden = own_ref[...] + up_ref[...].astype(F32) + down_ref[...].astype(F32)
+    out_ref = refs[-1]
+    hidden = own_ref[...]
+    for arrived in refs[:-1]:
+        hidden = hidden + arrived[...].astype(F32)
     gate = gu_ref[:, :part]
     up = gu_ref[:, part:]
     s = jax.nn.sigmoid(gate)
@@ -178,7 +182,7 @@
     out_ref[:, part:] = (hidden * gate * s).astype(BF16)
 
 
-def activate(gate_up, own, up, down):
+def activate(gate_up, own, *arrived):
     rows, part = own.shape
     block = rows // 2
     spec = pl.BlockSpec((block, part), lambda i: (i, 0))
@@ -186,12 +190,12 @@
     return pl.pallas_call(
         activate_kernel,
         grid=(rows // block,),
-        in_specs=[wide, spec, spec, spec],
+        in_specs=[wide, spec] + [spec] * len(arrived),
         out_specs=wide,
         out_shape=jax.ShapeDtypeStruct((rows, 2 * part), BF16),
         compiler_params=params(62),
         name="activate",
-    )(gate_up, own, up, down)
+    )(gate_up, own, *arrived)
 
 
 def row_grad_kernel(offsets, has_start, n_rep, me_ref, *refs):
@@ -225,13 +229,16 @@
     half = n_rep // 2
     blocks, offsets = [own], [0]
     up = down = own
+    far = shift(own, half)
     for step in range(1, half):
         up, down = shift(up, 1), shift(down, -1)
         blocks += [up, down]
         offsets += [n_rep - step, step]
-    last = shift(up, 1)
-    total = row_grad(me, blocks, offsets, w_gate, w_up, n_rep, None, F32, "row_grad_near")
-    return row_grad(me, [last], [half], w_gate, w_up, n_rep, total, BF16, "row_grad_far")
+    total = row_grad(
+        me, blocks[:-2], offsets[:-2], w_gate, w_up, n_rep, None, F32, "row_grad_near"
+    )
+    blocks, offsets = blocks[-2:] + [far], offsets[-2:] + [half]
+    return row_grad(me, blocks, offsets, w_gate, w_up, n_rep, total, BF16, "row_grad_far")
 
 
 def per_device(tokens, out_grad, expert_ids, route_weights, gate_weight, up_weight, down_weight):

time: 214 us -> 227 us (1.061)
  waiting for transfers between devices: 44 us -> 50.2 us
  starting transfers between devices: 57.1 us -> 61 us
  blocking collectives: 76.5 us -> 80 us
    reduce_scatter x1, waiting for transfers between devices: 0.01 us -> 4.12 us  [per_device(): lax.psum_scatter(gate_up_parts(x_rows, gate_weight, up_weight, n_rep), 'r...]
    ppermute x14, starting transfers between devices: 51.7 us -> 55.6 us  [shift(): lax.ppermute(rows, 'rep', [(i, (i + by) % n_rep) for i in range(n_rep)])]
    all_to_all x2, blocking collectives: 76.5 us -> 80 us  [exchange(): lax.all_to_all(blocks, ('outer', 'local'), 0, 0, tiled=True)]
  transfers between devices with their start and end apart: 16 -> 16, of which waited for: 9 -> 9; matrix products, arithmetic and copies ran while one was open for 0% -> 0% of each run, Pallas kernels for 2% -> 1%
where the time goes in v6:
time: 227 us
  blocking collectives  80 us (35%)
  starting transfers between devices  61 us (27%)
  waiting for transfers between devices  50.2 us (22%)
  Pallas kernels  13.8 us (6%)
  between operations  13.7 us (6%)
  local copies, waits for them, and re-layouts  6.98 us (3%)
    all_to_all x2, blocking collectives, exchange(): lax.all_to_all(blocks, ('outer', 'local'), 0, 0, tiled=True)  80 us
    ppermute x14, starting transfers between devices, shift(): lax.ppermute(rows, 'rep', [(i, (i + by) % n_rep) for i in range(n_rep)])  55.6 us
    ppermute x14, waiting for transfers between devices, shift(): lax.ppermute(rows, 'rep', [(i, (i + by) % n_rep) for i in range(n_rep)])  25.5 us
    all_to_all x1, waiting for transfers between devices, exchange(): lax.all_to_all(blocks, ('outer', 'local'), 0, 0, tiled=True)  20.6 us
    all_to_all x1, starting transfers between devices, exchange(): lax.all_to_all(blocks, ('outer', 'local'), 0, 0, tiled=True)  5.4 us
    pallas_call x1, Pallas kernels, gate_up_parts(): pl.pallas_call(gate_up_kernel, grid=(n_rep // per,), in_specs=[pl.BlockSp...  5.19 us
  transfers between devices with their start and end apart: 16, of which 9 were waited for; matrix products, arithmetic and copies ran while one was open for 0% of the time, Pallas kernels for 1%

profile of v6, /device:TPU:1, one launch (start us, length us, event | category | flops | bytes accessed | tf_op | source)
XLA Modules:
  0.0 226.6 jit_solution(13565558128399876077)
XLA Ops:
  6.5 0.0 reduce-scatter.2.cloned.1.call-start
  6.5 2.6 %route.1 = (bf16[512,512]{1,0:T(8,128)(2,1)}, bf16[512,512]{1,0:T(8,128)(2,1)}, bf16[32,512]{1,0:T(8,128)(2,1)}) custom-call(s32[8,32]{1,0:T(8,128)} %bitcast.7, f32[8,32]{1,0:T(8,128)} %bitcast.8, bf16[32,512]{1,0:T(8,128)(2,1)} %refs_2_.9, bf16[32,512]{1,0:T(8,128)(2,1)} %refs_3_.1), custom_call_target="tpu_custom_call" | custom-call | tf_op jit(solution)/shard_map/route/pallas_call | solution.py:72
  9.1 1.2 reshape.22
  10.3 39.4 %all_to_all.15 = bf16[128,4,512]{2,1,0:T(4,128)(2,1)S(1)} all-to-all(bf16[128,4,512]{2,1,0:T(4,128)(2,1)S(1)} %reshape.22), channel_id=1, replica_groups=mesh['rep'=8,'outer'=8,'local'=16] {'outer','local'}, dimensions={0} | all-to-all | bytes 1048576 | tf_op jit(solution)/shard_map/all_to_all | solution.py:258
  49.7 0.9 reshape.23.x_ref
  50.6 5.2 %gate_up.1 = f32[8,512,256]{2,1,0:T(8,128)} custom-call(bf16[512,512]{1,0:T(8,128)(2,1)} %reshape.23.x_ref, bf16[1,512,1024]{2,1,0:T(8,128)(2,1)} %refs_4_.1, bf16[1,512,1024]{2,1,0:T(8,128)(2,1)} %refs_5_.1), custom_call_target="tpu_custom_call" | custom-call | tf_op jit(solution)/shard_map/gate_up/pallas_call | solution.py:118
  55.8 0.0 reduce-scatter.2.cloned.1.call-update
  55.9 0.9 reshape.24
  56.8 5.4 %all-to-all-start.1 = ((bf16[128,4,512]{2,1,0:T(4,128)(2,1)}), bf16[128,4,512]{2,1,0:T(4,128)(2,1)S(1)}, u32[]{:S(2)}, u32[]{:S(2)}) async-start(bf16[128,4,512]{2,1,0:T(4,128)(2,1)} %reshape.24), calls=%async_computation.2 | async-start | bytes 1048576 | tf_op jit(solution)/shard_map/all_to_all | solution.py:258
  62.2 20.6 %all-to-all-done.1 = bf16[128,4,512]{2,1,0:T(4,128)(2,1)S(1)} async-done(((bf16[128,4,512]{2,1,0:T(4,128)(2,1)}), bf16[128,4,512]{2,1,0:T(4,128)(2,1)S(1)}, u32[]{:S(2)}, u32[]{:S(2)}) %all-to-all-start.1) | async-done | bytes 524320 | tf_op jit(solution)/shard_map/all_to_all | solution.py:258
  82.8 0.1 reshape.25.refs_1_
  82.9 0.0 copy-done
  82.9 0.3 hidden_rise_2.1
  83.2 1.9 collective-permute-start
  85.1 0.3 hidden_fall_2.1
  85.4 13.4 %collective-permute-start.2 = (bf16[512,128]{1,0:T(8,128)(2,1)S(1)}, bf16[512,128]{1,0:T(8,128)(2,1)S(1)}, u32[]{:S(2)}, u32[]{:S(2)}) collective-permute-start(bf16[512,128]{1,0:T(8,128)(2,1)S(1)} %hidden_fall_2.1), channel_id=1, source_target_pairs={{0,896},{128,0},{256,128},{384,256},{512,384},{640,512},{768,640},... | collective-permute-start | bytes 393224 | tf_op jit(solution)/shard_map/ppermute | solution.py:153
  98.8 0.3 hidden_far_3.1
  99.1 0.3 hidden_far_4.1
  99.4 0.0 copy-start.1
  99.4 0.3 hidden_far_5.1
  99.7 1.9 collective-permute-start.4
  101.7 6.3 %collective-permute-start.5 = (bf16[512,128]{1,0:T(8,128)(2,1)S(1)}, bf16[512,128]{1,0:T(8,128)(2,1)S(1)}, u32[]{:S(2)}, u32[]{:S(2)}) collective-permute-start(bf16[512,128]{1,0:T(8,128)(2,1)S(1)} %hidden_far_4.1), channel_id=1, source_target_pairs={{0,512},{128,640},{256,768},{384,896},{512,0},{640,128},{768,256},... | collective-permute-start | bytes 393224 | tf_op jit(solution)/shard_map/ppermute | solution.py:153
  108.0 2.0 collective-permute-start.6
  110.0 0.0 collective-permute-done.refs_3_
  110.0 0.3 hidden_rise_1.1
  110.3 3.5 %collective-permute-start.1 = (bf16[512,128]{1,0:T(8,128)(2,1)S(1)}, bf16[512,128]{1,0:T(8,128)(2,1)S(1)}, u32[]{:S(2)}, u32[]{:S(2)}) collective-permute-start(bf16[512,128]{1,0:T(8,128)(2,1)S(1)} %hidden_rise_1.1), channel_id=1, source_target_pairs={{0,128},{128,256},{256,384},{384,512},{512,640},{640,768},{768,896... | collective-permute-start | bytes 393224 | tf_op jit(solution)/shard_map/ppermute | solution.py:153
  113.8 0.0 collective-permute-done.2.refs_3_
  113.8 0.3 hidden_fall_1.1
  114.1 3.0 %collective-permute-start.3 = (bf16[512,128]{1,0:T(8,128)(2,1)S(1)}, bf16[512,128]{1,0:T(8,128)(2,1)}, u32[]{:S(2)}, u32[]{:S(2)}) collective-permute-start(bf16[512,128]{1,0:T(8,128)(2,1)S(1)} %hidden_fall_1.1), channel_id=1, source_target_pairs={{0,896},{128,0},{256,128},{384,256},{512,384},{640,512},{768,640},... | collective-permute-start | bytes 393224 | tf_op jit(solution)/shard_map/ppermute | solution.py:153
  117.1 0.3 hidden_own.1.own_ref
  117.4 0.7 copy-done.4
  118.1 0.1 collective-permute-done.4.refs_2_
  118.3 8.7 %collective-permute-done.5.refs_3_ = bf16[512,128]{1,0:T(8,128)(2,1)S(1)} collective-permute-done((bf16[512,128]{1,0:T(8,128)(2,1)S(1)}, bf16[512,128]{1,0:T(8,128)(2,1)S(1)}, u32[]{:S(2)}, u32[]{:S(2)}) %collective-permute-start.5) | collective-permute-done | bytes 131104 | tf_op jit(solution)/shard_map/ppermute | solution.py:153
  127.0 1.5 collective-permute-done.6.refs_4_
  128.5 0.0 collective-permute-done.1.refs_0_
  128.5 0.7 copy-done.9
  129.2 3.6 %collective-permute-done.3.refs_1_ = bf16[512,128]{1,0:T(8,128)(2,1)} collective-permute-done((bf16[512,128]{1,0:T(8,128)(2,1)S(1)}, bf16[512,128]{1,0:T(8,128)(2,1)}, u32[]{:S(2)}, u32[]{:S(2)}) %collective-permute-start.3) | collective-permute-done | bytes 131104 | tf_op jit(solution)/shard_map/ppermute | solution.py:153
  132.8 4.1 %reduce-scatter.2.cloned.1.call-done = f32[1,512,256]{2,1,0:T(8,128)} async-done(((f32[8,512,256]{2,1,0:T(8,128)}), f32[1,512,256]{2,1,0:T(8,128)}) %reduce-scatter.2.cloned.1.call-update) | async-done | bytes 524304 | tf_op jit(solution)/shard_map/reduce_scatter | solution.py:261
  136.9 0.0 copy-done.6
  136.9 2.1 activate.1.refs_1_
  139.0 1.9 collective-permute-start.7
  140.9 4.6 %collective-permute-start.10 = (bf16[512,256]{1,0:T(8,128)(2,1)}, bf16[512,256]{1,0:T(8,128)(2,1)S(1)}, u32[]{:S(2)}, u32[]{:S(2)}) collective-permute-start(bf16[512,256]{1,0:T(8,128)(2,1)} %activate.1.refs_1_), channel_id=1, source_target_pairs={{0,896},{128,0},{256,128},{384,256},{512,384},{640,512},{768,640},... | collective-permute-start | bytes 786440 | tf_op jit(solution)/shard_map/ppermute | solution.py:153
  145.5 4.0 %collective-permute-done.7.refs_2_ = bf16[512,256]{1,0:T(8,128)(2,1)S(1)} collective-permute-done((bf16[512,256]{1,0:T(8,128)(2,1)}, bf16[512,256]{1,0:T(8,128)(2,1)S(1)}, u32[]{:S(2)}, u32[]{:S(2)}) %collective-permute-start.7) | collective-permute-done | bytes 262176 | tf_op jit(solution)/shard_map/ppermute | solution.py:153
  149.5 1.9 collective-permute-start.8
  151.4 0.0 collective-permute-done.10.refs_3_
  151.4 4.6 %collective-permute-start.11 = (bf16[512,256]{1,0:T(8,128)(2,1)S(1)}, bf16[512,256]{1,0:T(8,128)(2,1)S(1)}, u32[]{:S(2)}, u32[]{:S(2)}) collective-permute-start(bf16[512,256]{1,0:T(8,128)(2,1)S(1)} %collective-permute-done.10.refs_3_), channel_id=1, source_target_pairs={{0,896},{128,0},{256,128},{384,256},{512,384},{640,512},{768,640},... | collective-permute-start | bytes 786440 | tf_op jit(solution)/shard_map/ppermute | solution.py:153
  156.0 4.2 %collective-permute-start.13 = (bf16[512,256]{1,0:T(8,128)(2,1)}, bf16[512,256]{1,0:T(8,128)(2,1)S(1)}, u32[]{:S(2)}, u32[]{:S(2)}) collective-permute-start(bf16[512,256]{1,0:T(8,128)(2,1)} %activate.1.refs_1_), channel_id=1, source_target_pairs={{0,512},{128,640},{256,768},{384,896},{512,0},{640,128},{768,256},... | collective-permute-start | bytes 786440 | tf_op jit(solution)/shard_map/ppermute | solution.py:153
  160.2 0.0 collective-permute-done.8.refs_4_
  160.2 1.9 collective-permute-start.9
  162.1 0.0 collective-permute-done.11.refs_5_
  162.1 4.6 %collective-permute-start.12 = (bf16[512,256]{1,0:T(8,128)(2,1)S(1)}, bf16[512,256]{1,0:T(8,128)(2,1)S(1)}, u32[]{:S(2)}, u32[]{:S(2)}) collective-permute-start(bf16[512,256]{1,0:T(8,128)(2,1)S(1)} %collective-permute-done.11.refs_5_), channel_id=1, source_target_pairs={{0,896},{128,0},{256,128},{384,256},{512,384},{640,512},{768,640},... | collective-permute-start | bytes 786440 | tf_op jit(solution)/shard_map/ppermute | solution.py:153
  166.7 0.0 copy-start.2
  166.8 1.2 copy-done.2
  168.0 0.9 copy-done.3
  168.9 0.9 row_grad_near.1.refs_6_
  169.8 0.0 copy-start.10
  169.8 4.9 %collective-permute-done.13.refs_3_ = bf16[512,256]{1,0:T(8,128)(2,1)S(1)} collective-permute-done((bf16[512,256]{1,0:T(8,128)(2,1)}, bf16[512,256]{1,0:T(8,128)(2,1)S(1)}, u32[]{:S(2)}, u32[]{:S(2)}) %collective-permute-start.13) | collective-permute-done | bytes 262176 | tf_op jit(solution)/shard_map/ppermute | solution.py:153
  174.8 2.5 %collective-permute-done.9.refs_1_ = bf16[512,256]{1,0:T(8,128)(2,1)S(1)} collective-permute-done((bf16[512,256]{1,0:T(8,128)(2,1)S(1)}, bf16[512,256]{1,0:T(8,128)(2,1)S(1)}, u32[]{:S(2)}, u32[]{:S(2)}) %collective-permute-start.9) | collective-permute-done | bytes 262176 | tf_op jit(solution)/shard_map/ppermute | solution.py:153
  177.3 0.0 collective-permute-done.12.refs_2_
  177.3 0.6 row_grad_far.1
  178.0 0.1 reshape.26
  178.1 40.7 %all_to_all.16 = bf16[128,4,512]{2,1,0:T(4,128)(2,1)S(1)} all-to-all(bf16[128,4,512]{2,1,0:T(4,128)(2,1)S(1)} %reshape.26), channel_id=1, replica_groups=mesh['rep'=8,'outer'=8,'local'=16] {'outer','local'}, dimensions={0} | all-to-all | bytes 1048576 | tf_op jit(solution)/shard_map/all_to_all | solution.py:258
  218.8 0.1 reshape.27
  218.9 0.8 convolution_convert_fusion
  (13 shorter events, 0.0 us)
Async XLA Ops:
  6.5 130.4 %reduce-scatter.2.cloned.1.call-start = ((), (), s32[]{:S(2)}) async-start(), calls=%async_computation.4 | async-start | bytes 4718592 | tf_op jit(solution)/shard_map/reduce_scatter | solution.py:261
  50.6 5.2 %copy-start.5 = (bf16[512,512]{1,0:T(8,128)(2,1)S(1)}, bf16[512,512]{1,0:T(8,128)(2,1)}, u32[]{:S(2)}) copy-start(bf16[512,512]{1,0:T(8,128)(2,1)} %get-tuple-element.10) | copy-start | bytes 1572868
  55.8 27.1 %copy-start = (bf16[1,1024,512]{2,1,0:T(8,128)(2,1)S(1)}, bf16[1,1024,512]{2,1,0:T(8,128)(2,1)}, u32[]{:S(2)}) copy-start(bf16[1,1024,512]{2,1,0:T(8,128)(2,1)} %refs_2_.17) | copy-start | bytes 3145732
  56.8 26.0 %all-to-all-start.1 = ((bf16[128,4,512]{2,1,0:T(4,128)(2,1)}), bf16[128,4,512]{2,1,0:T(4,128)(2,1)S(1)}, u32[]{:S(2)}, u32[]{:S(2)}) async-start(bf16[128,4,512]{2,1,0:T(4,128)(2,1)} %reshape.24), calls=%async_computation.2 | async-start | bytes 1048576 | tf_op jit(solution)/shard_map/all_to_all | solution.py:258
  83.2 26.8 %collective-permute-start = (bf16[512,128]{1,0:T(8,128)(2,1)S(1)}, bf16[512,128]{1,0:T(8,128)(2,1)S(1)}, u32[]{:S(2)}, u32[]{:S(2)}) collective-permute-start(bf16[512,128]{1,0:T(8,128)(2,1)S(1)} %hidden_rise_2.1), channel_id=1, source_target_pairs={{0,128},{128,256},{256,384},{384,512},{512,640},{640,768},{768,896... | collective-permute-start | bytes 393224 | tf_op jit(solution)/shard_map/ppermute | solution.py:153
  85.4 28.4 %collective-permute-start.2 = (bf16[512,128]{1,0:T(8,128)(2,1)S(1)}, bf16[512,128]{1,0:T(8,128)(2,1)S(1)}, u32[]{:S(2)}, u32[]{:S(2)}) collective-permute-start(bf16[512,128]{1,0:T(8,128)(2,1)S(1)} %hidden_fall_2.1), channel_id=1, source_target_pairs={{0,896},{128,0},{256,128},{384,256},{512,384},{640,512},{768,640},... | collective-permute-start | bytes 393224 | tf_op jit(solution)/shard_map/ppermute | solution.py:153
  99.4 67.3 %copy-start.1 = (bf16[1,512,1024]{2,1,0:T(8,128)(2,1)S(1)}, bf16[1,512,1024]{2,1,0:T(8,128)(2,1)}, u32[]{:S(2)}) copy-start(bf16[1,512,1024]{2,1,0:T(8,128)(2,1)} %refs_4_.1) | copy-start | bytes 3145732
  99.7 18.5 %collective-permute-start.4 = (bf16[512,128]{1,0:T(8,128)(2,1)S(1)}, bf16[512,128]{1,0:T(8,128)(2,1)S(1)}, u32[]{:S(2)}, u32[]{:S(2)}) collective-permute-start(bf16[512,128]{1,0:T(8,128)(2,1)S(1)} %hidden_far_3.1), channel_id=1, source_target_pairs={{0,384},{128,512},{256,640},{384,768},{512,896},{640,0},{768,128},... | collective-permute-start | bytes 393224 | tf_op jit(solution)/shard_map/ppermute | solution.py:153
  101.7 25.3 %collective-permute-start.5 = (bf16[512,128]{1,0:T(8,128)(2,1)S(1)}, bf16[512,128]{1,0:T(8,128)(2,1)S(1)}, u32[]{:S(2)}, u32[]{:S(2)}) collective-permute-start(bf16[512,128]{1,0:T(8,128)(2,1)S(1)} %hidden_far_4.1), channel_id=1, source_target_pairs={{0,512},{128,640},{256,768},{384,896},{512,0},{640,128},{768,256},... | collective-permute-start | bytes 393224 | tf_op jit(solution)/shard_map/ppermute | solution.py:153
  108.0 20.4 %collective-permute-start.6 = (bf16[512,128]{1,0:T(8,128)(2,1)S(1)}, bf16[512,128]{1,0:T(8,128)(2,1)S(1)}, u32[]{:S(2)}, u32[]{:S(2)}) collective-permute-start(bf16[512,128]{1,0:T(8,128)(2,1)S(1)} %hidden_far_5.1), channel_id=1, source_target_pairs={{0,640},{128,768},{256,896},{384,0},{512,128},{640,256},{768,384},... | collective-permute-start | bytes 393224 | tf_op jit(solution)/shard_map/ppermute | solution.py:153
  110.3 18.2 %collective-permute-start.1 = (bf16[512,128]{1,0:T(8,128)(2,1)S(1)}, bf16[512,128]{1,0:T(8,128)(2,1)S(1)}, u32[]{:S(2)}, u32[]{:S(2)}) collective-permute-start(bf16[512,128]{1,0:T(8,128)(2,1)S(1)} %hidden_rise_1.1), channel_id=1, source_target_pairs={{0,128},{128,256},{256,384},{384,512},{512,640},{640,768},{768,896... | collective-permute-start | bytes 393224 | tf_op jit(solution)/shard_map/ppermute | solution.py:153
  114.1 18.7 %collective-permute-start.3 = (bf16[512,128]{1,0:T(8,128)(2,1)S(1)}, bf16[512,128]{1,0:T(8,128)(2,1)}, u32[]{:S(2)}, u32[]{:S(2)}) collective-permute-start(bf16[512,128]{1,0:T(8,128)(2,1)S(1)} %hidden_fall_1.1), channel_id=1, source_target_pairs={{0,896},{128,0},{256,128},{384,256},{512,384},{640,512},{768,640},... | collective-permute-start | bytes 393224 | tf_op jit(solution)/shard_map/ppermute | solution.py:153
  117.4 0.7 copy-start.4
  118.3 18.6 %copy-start.6 = (bf16[512,128]{1,0:T(8,128)(2,1)}, bf16[512,128]{1,0:T(8,128)(2,1)S(1)}, u32[]{:S(2)}) copy-start(bf16[512,128]{1,0:T(8,128)(2,1)S(1)} %collective-permute-done.4.refs_2_) | copy-start | bytes 393220
  127.0 9.9 %copy-start.7 = (bf16[512,128]{1,0:T(8,128)(2,1)}, bf16[512,128]{1,0:T(8,128)(2,1)S(1)}, u32[]{:S(2)}) copy-start(bf16[512,128]{1,0:T(8,128)(2,1)S(1)} %collective-permute-done.5.refs_3_) | copy-start | bytes 393220
  128.5 8.4 %copy-start.8 = (bf16[512,128]{1,0:T(8,128)(2,1)}, bf16[512,128]{1,0:T(8,128)(2,1)S(1)}, u32[]{:S(2)}) copy-start(bf16[512,128]{1,0:T(8,128)(2,1)S(1)} %collective-permute-done.6.refs_4_) | copy-start | bytes 393220
  128.5 0.7 copy-start.9
  139.0 10.5 %collective-permute-start.7 = (bf16[512,256]{1,0:T(8,128)(2,1)}, bf16[512,256]{1,0:T(8,128)(2,1)S(1)}, u32[]{:S(2)}, u32[]{:S(2)}) collective-permute-start(bf16[512,256]{1,0:T(8,128)(2,1)} %activate.1.refs_1_), channel_id=1, source_target_pairs={{0,128},{128,256},{256,384},{384,512},{512,640},{640,768},{768,896... | collective-permute-start | bytes 786440 | tf_op jit(solution)/shard_map/ppermute | solution.py:153
  140.9 10.5 %collective-permute-start.10 = (bf16[512,256]{1,0:T(8,128)(2,1)}, bf16[512,256]{1,0:T(8,128)(2,1)S(1)}, u32[]{:S(2)}, u32[]{:S(2)}) collective-permute-start(bf16[512,256]{1,0:T(8,128)(2,1)} %activate.1.refs_1_), channel_id=1, source_target_pairs={{0,896},{128,0},{256,128},{384,256},{512,384},{640,512},{768,640},... | collective-permute-start | bytes 786440 | tf_op jit(solution)/shard_map/ppermute | solution.py:153
  149.5 10.7 %collective-permute-start.8 = (bf16[512,256]{1,0:T(8,128)(2,1)S(1)}, bf16[512,256]{1,0:T(8,128)(2,1)S(1)}, u32[]{:S(2)}, u32[]{:S(2)}) collective-permute-start(bf16[512,256]{1,0:T(8,128)(2,1)S(1)} %collective-permute-done.7.refs_2_), channel_id=1, source_target_pairs={{0,128},{128,256},{256,384},{384,512},{512,640},{640,768},{768,896... | collective-permute-start | bytes 786440 | tf_op jit(solution)/shard_map/ppermute | solution.py:153
  151.4 10.7 %collective-permute-start.11 = (bf16[512,256]{1,0:T(8,128)(2,1)S(1)}, bf16[512,256]{1,0:T(8,128)(2,1)S(1)}, u32[]{:S(2)}, u32[]{:S(2)}) collective-permute-start(bf16[512,256]{1,0:T(8,128)(2,1)S(1)} %collective-permute-done.10.refs_3_), channel_id=1, source_target_pairs={{0,896},{128,0},{256,128},{384,256},{512,384},{640,512},{768,640},... | collective-permute-start | bytes 786440 | tf_op jit(solution)/shard_map/ppermute | solution.py:153
  156.0 18.7 %collective-permute-start.13 = (bf16[512,256]{1,0:T(8,128)(2,1)}, bf16[512,256]{1,0:T(8,128)(2,1)S(1)}, u32[]{:S(2)}, u32[]{:S(2)}) collective-permute-start(bf16[512,256]{1,0:T(8,128)(2,1)} %activate.1.refs_1_), channel_id=1, source_target_pairs={{0,512},{128,640},{256,768},{384,896},{512,0},{640,128},{768,256},... | collective-permute-start | bytes 786440 | tf_op jit(solution)/shard_map/ppermute | solution.py:153
  160.2 17.1 %collective-permute-start.9 = (bf16[512,256]{1,0:T(8,128)(2,1)S(1)}, bf16[512,256]{1,0:T(8,128)(2,1)S(1)}, u32[]{:S(2)}, u32[]{:S(2)}) collective-permute-start(bf16[512,256]{1,0:T(8,128)(2,1)S(1)} %collective-permute-done.8.refs_4_), channel_id=1, source_target_pairs={{0,128},{128,256},{256,384},{384,512},{512,640},{640,768},{768,896... | collective-permute-start | bytes 786440 | tf_op jit(solution)/shard_map/ppermute | solution.py:153
  162.1 15.2 %collective-permute-start.12 = (bf16[512,256]{1,0:T(8,128)(2,1)S(1)}, bf16[512,256]{1,0:T(8,128)(2,1)S(1)}, u32[]{:S(2)}, u32[]{:S(2)}) collective-permute-start(bf16[512,256]{1,0:T(8,128)(2,1)S(1)} %collective-permute-done.11.refs_5_), channel_id=1, source_target_pairs={{0,896},{128,0},{256,128},{384,256},{512,384},{640,512},{768,640},... | collective-permute-start | bytes 786440 | tf_op jit(solution)/shard_map/ppermute | solution.py:153
  166.7 1.2 copy-start.2
  168.0 0.9 copy-start.3
  169.8 49.1 %copy-start.10 = (bf16[32,512]{1,0:T(8,128)(2,1)S(1)}, bf16[32,512]{1,0:T(8,128)(2,1)}, u32[]{:S(2)}) copy-start(bf16[32,512]{1,0:T(8,128)(2,1)} %get-tuple-element.8) | copy-start | bytes 98308
Sparse Core Ops, SparseCore 0:
  56.0 80.8 reduce-scatter.1

commit v7 on v3

--- a/solution.py
+++ b/solution.py
@@ -95,59 +95,29 @@
     )(expert_ids.T, route_weights.T, tokens, out_grad)
 
 
-def hidden_kernel(rows_ref, w_ref, out_ref):
-    part = out_ref.shape[2]
-    out = lax.dot_general(rows_ref[...], w_ref[0], TRANS_B, preferred_element_type=F32)
-    for j in range(out_ref.shape[0]):
-        out_ref[j] = out[:, j * part : (j + 1) * part]
-
-
-def hidden_parts(both_rows, w_down, n_rep):
-    rows = both_rows.shape[0]
-    width = both_rows.shape[1] // 2
-    part = w_down.shape[1] // n_rep
-    per = 2
-    return pl.pallas_call(
-        hidden_kernel,
-        grid=(n_rep // per,),
-        in_specs=[
-            pl.BlockSpec((rows, width), lambda c: (0, 1)),
-            pl.BlockSpec((1, per * part, width), lambda c: (0, c, 0)),
-        ],
-        out_specs=pl.BlockSpec((per, rows, part), lambda c: (c, 0, 0)),
-        out_shape=jax.ShapeDtypeStruct((n_rep, rows, part), F32),
-        compiler_params=params(62),
-        name="hidden",
-    )(both_rows, w_down)
+def chunk_start(me_ref, offset, n_rep, part):
+    return pl.multiple_of(lax.rem(me_ref[0] + offset, n_rep) * part, part)
 
 
 def chunk_weights(me_ref, offset, n_rep, wg_ref, wu_ref):
     part = wg_ref.shape[2] // n_rep
-    c = lax.rem(me_ref[0] + offset, n_rep)
-    cols = pl.ds(pl.multiple_of(c * part, part), part)
+    cols = pl.ds(chunk_start(me_ref, offset, n_rep, part), part)
     return jnp.concatenate([wg_ref[0, :, cols], wu_ref[0, :, cols]], axis=1)
 
 
-def gate_up_kernel(offset, n_rep, me_ref, rows_ref, wg_ref, wu_ref, *refs):
+def term_kernel(offset, n_rep, me_ref, rows_ref, wg_ref, wu_ref, wd_ref, *refs):
+    out_ref = refs[-1]
     width = wg_ref.shape[1]
+    part = wg_ref.shape[2] // n_rep
     weights = chunk_weights(me_ref, offset, n_rep, wg_ref, wu_ref)
-    total = jnp.dot(rows_ref[:, :width], weights, preferred_element_type=F32)
+    down = wd_ref[0, pl.ds(chunk_start(me_ref, offset, n_rep, part), part), :]
+    gate_up = jnp.dot(rows_ref[:, :width], weights, preferred_element_type=F32)
+    hidden = lax.dot_general(rows_ref[:, width:], down, TRANS_B, preferred_element_type=F32)
     for arrived in refs[:-1]:
-        total = total + arrived[...].astype(F32)
-    refs[-1][...] = total.astype(refs[-1].dtype)
-
-
-def gate_up(me, both_rows, w_gate, w_up, n_rep, offset, arrived, dtype, name):
-    rows = both_rows.shape[0]
-    part = w_gate.shape[2] // n_rep
-    return pl.pallas_call(
-        lambda *refs: gate_up_kernel(offset, n_rep, *refs),
-        in_specs=[pl.BlockSpec(memory_space=pltpu.SMEM)] + [VMEM_SPEC] * (3 + len(arrived)),
-        out_specs=VMEM_SPEC,
-        out_shape=jax.ShapeDtypeStruct((rows, 2 * part), dtype),
-        compiler_params=params(),
-        name=name,
-    )(me, both_rows, w_gate, w_up, *arrived)
+        gate_up = gate_up + arrived[:, : 2 * part].astype(F32)
+        hidden = hidden + arrived[:, 2 * part :].astype(F32)
+    out_ref[:, : 2 * part] = gate_up.astype(out_ref.dtype)
+    out_ref[:, 2 * part :] = hidden.astype(out_ref.dtype)
 
 
 def shift(rows, by):
@@ -155,47 +125,50 @@
     return lax.ppermute(rows, "rep", [(i, (i + by) % n_rep) for i in range(n_rep)])
 
 
-def gate_up_sums(me, both_rows, w_gate, w_up, n_rep):
+def width_sums(me, both_rows, w_gate, w_up, w_down, n_rep):
+    rows = both_rows.shape[0]
+    part = w_gate.shape[2] // n_rep
+
+    def term(offset, arrived, dtype, name):
+        return pl.pallas_call(
+            lambda *refs: term_kernel(offset, n_rep, *refs),
+            in_specs=[pl.BlockSpec(memory_space=pltpu.SMEM)] + [VMEM_SPEC] * (4 + len(arrived)),
+            out_specs=VMEM_SPEC,
+            out_shape=jax.ShapeDtypeStruct((rows, 3 * part), dtype),
+            compiler_params=params(),
+            name=name,
+        )(me, both_rows, w_gate, w_up, w_down, *arrived)
+
     half = n_rep // 2
     up, down = (), ()
     for hop in range(half, 0, -1):
-        term = gate_up(
-            me, both_rows, w_gate, w_up, n_rep, hop, up, BF16, "gate_up_rise_%d" % hop
-        )
-        up = (shift(term, 1),)
+        up = (shift(term(hop, up, BF16, "rise_%d" % hop), 1),)
         if hop < half:
-            term = gate_up(
-                me, both_rows, w_gate, w_up, n_rep, n_rep - hop, down, BF16, "gate_up_fall_%d" % hop
-            )
-            down = (shift(term, -1),)
-    own = gate_up(me, both_rows, w_gate, w_up, n_rep, 0, (), F32, "gate_up_own")
-    return own, up[0], down[0]
-
-
-def activate_kernel(h_ref, own_ref, up_ref, down_ref, out_ref):
-    part = h_ref.shape[1]
+            down = (shift(term(n_rep - hop, down, BF16, "fall_%d" % hop), -1),)
+    return term(0, (), F32, "own_term"), up[0], down[0]
+
+
+def activate_kernel(own_ref, up_ref, down_ref, out_ref):
+    part = own_ref.shape[1] // 3
     sums = own_ref[...] + up_ref[...].astype(F32) + down_ref[...].astype(F32)
-    hidden = h_ref[...]
     gate = sums[:, :part]
-    up = sums[:, part:]
+    up = sums[:, part : 2 * part]
+    hidden = sums[:, 2 * part :]
     s = jax.nn.sigmoid(gate)
     out_ref[:, :part] = (hidden * up * s * (1.0 + gate * (1.0 - s))).astype(BF16)
     out_ref[:, part:] = (hidden * gate * s).astype(BF16)
 
 
-def activate(hidden, own, up, down):
-    rows, part2 = own.shape
-    block = 128
-    spec = pl.BlockSpec((block, part2), lambda i: (i, 0))
+def activate(own, up, down):
+    rows, part3 = own.shape
     return pl.pallas_call(
         activate_kernel,
-        grid=(rows // block,),
-        in_specs=[pl.BlockSpec((block, part2 // 2), lambda i: (i, 0)), spec, spec, spec],
-        out_specs=spec,
-        out_shape=jax.ShapeDtypeStruct(own.shape, BF16),
-        compiler_params=params(62),
+        in_specs=[VMEM_SPEC] * 3,
+        out_specs=VMEM_SPEC,
+        out_shape=jax.ShapeDtypeStruct((rows, part3 // 3 * 2), BF16),
+        compiler_params=params(),
         name="activate",
-    )(hidden, own, up, down)
+    )(own, up, down)
 
 
 def row_grad_kernel(offsets, has_start, n_rep, me_ref, *refs):
@@ -253,11 +226,9 @@
         return lax.all_to_all(blocks, ("outer", "local"), 0, 0, tiled=True).reshape(rows.shape)
 
     both_rows = exchange(send)
-    hidden = lax.psum_scatter(
-        hidden_parts(both_rows, down_weight, n_rep), "rep", scatter_dimension=0
+    own = activate(
+        *width_sums(me, both_rows, gate_weight, up_weight, down_weight, n_rep)
     )
-    sums = gate_up_sums(me, both_rows, gate_weight, up_weight, n_rep)
-    own = activate(hidden, *sums)
     returned = exchange(gather_matmul(me, own, gate_weight, up_weight, n_rep))
     return jnp.dot(per_token_t, returned, preferred_element_type=F32).astype(BF16)
 

time: 216 us -> 190 us (0.88)
  blocking collectives: 87.4 us -> 34.3 us
  waiting for transfers between devices: 32.2 us -> 68.6 us
  starting transfers between devices: 57.1 us -> 70.9 us
  between operations: 13.6 us -> 0.32 us
  Pallas kernels: 14.7 us -> 8.14 us
  local copies, waits for them, and re-layouts: 9.24 us -> 5.69 us
    all_to_all x2 -> x1, blocking collectives: 87.4 us -> 34.3 us  [exchange(): lax.all_to_all(blocks, ('outer', 'local'), 0, 0, tiled=True)]
    all_to_all x0 -> x1, waiting for transfers between devices: none -> 30.6 us  [exchange(): lax.all_to_all(blocks, ('outer', 'local'), 0, 0, tiled=True)]
    all_to_all x0 -> x1, starting transfers between devices: none -> 20.4 us  [exchange(): lax.all_to_all(blocks, ('outer', 'local'), 0, 0, tiled=True)]
    ppermute x14, starting transfers between devices: 57.1 us -> 50.5 us  [shift(): lax.ppermute(rows, 'rep', [(i, (i + by) % n_rep) for i in range(n_rep)])]
    pallas_call x10 -> x9, Pallas kernels: 10.4 us -> 3.87 us  [the longest x8 3.66 us: term(): pl.pallas_call(lambda *refs: term_kernel(offset, n_rep, *refs), in_specs=...]
    ppermute x14, waiting for transfers between devices: 32.2 us -> 38 us  [shift(): lax.ppermute(rows, 'rep', [(i, (i + by) % n_rep) for i in range(n_rep)])]
    unnamed x18 -> x8, local copies, waits for them, and re-layouts: 6.42 us -> 1.86 us
  transfers between devices with their start and end apart: 15 -> 15, of which waited for: 11 -> 9; matrix products, arithmetic and copies ran while one was open for 0% -> 0% of each run, Pallas kernels for 2% -> 2%
where the time goes in v7:
time: 190 us; the launch traced here: 189 us
  starting transfers between devices  70.9 us (37%)
  waiting for transfers between devices  68.6 us (36%)
  blocking collectives  34.3 us (18%)
  Pallas kernels  8.14 us (4%)
  local copies, waits for them, and re-layouts  5.69 us (3%)
    ppermute x14, starting transfers between devices, shift(): lax.ppermute(rows, 'rep', [(i, (i + by) % n_rep) for i in range(n_rep)])  50.5 us
    ppermute x14, waiting for transfers between devices, shift(): lax.ppermute(rows, 'rep', [(i, (i + by) % n_rep) for i in range(n_rep)])  38 us
    all_to_all x1, blocking collectives, exchange(): lax.all_to_all(blocks, ('outer', 'local'), 0, 0, tiled=True)  34.3 us
    all_to_all x1, waiting for transfers between devices, exchange(): lax.all_to_all(blocks, ('outer', 'local'), 0, 0, tiled=True)  30.6 us
    all_to_all x1, starting transfers between devices, exchange(): lax.all_to_all(blocks, ('outer', 'local'), 0, 0, tiled=True)  20.4 us
  transfers between devices with their start and end apart: 15, of which 9 were waited for; matrix products, arithmetic and copies ran while one was open for 0% of the time, Pallas kernels for 2%

profile of v7, /device:TPU:1, one launch (start us, length us, event | category | flops | bytes accessed | tf_op | source)
XLA Modules:
  0.0 188.7 jit_solution(1397820607190932245)
XLA Ops:
  0.0 2.7 %route.1 = (bf16[512,1024]{1,0:T(8,128)(2,1)}, bf16[32,512]{1,0:T(8,128)(2,1)}) custom-call(s32[8,32]{1,0:T(8,128)} %bitcast.5, f32[8,32]{1,0:T(8,128)} %bitcast.6, bf16[32,512]{1,0:T(8,128)(2,1)} %refs_2_.10, bf16[32,512]{1,0:T(8,128)(2,1)} %refs_3_.10), custom_call_target="tpu_custom_call" | custom-call | tf_op jit(solution)/shard_map/route/pallas_call | solution.py:77
  2.7 2.2 %reshape.16 = bf16[128,4,1024]{2,1,0:T(4,128)(2,1)} reshape(bf16[512,1024]{1,0:T(8,128)(2,1)} %get-tuple-element.8) | data formatting | bytes 2097152 | tf_op jit(solution)/shard_map/reshape | solution.py:225
  5.0 20.4 %all-to-all-start = ((bf16[128,4,1024]{2,1,0:T(4,128)(2,1)}), bf16[128,4,1024]{2,1,0:T(4,128)(2,1)}, u32[]{:S(2)}, u32[]{:S(2)}) async-start(bf16[128,4,1024]{2,1,0:T(4,128)(2,1)} %reshape.16), calls=%async_computation | async-start | bytes 2097152 | tf_op jit(solution)/shard_map/all_to_all | solution.py:226
  25.4 0.0 copy-start
  25.4 0.0 copy-start.1
  25.4 30.6 %all-to-all-done = bf16[128,4,1024]{2,1,0:T(4,128)(2,1)} async-done(((bf16[128,4,1024]{2,1,0:T(4,128)(2,1)}), bf16[128,4,1024]{2,1,0:T(4,128)(2,1)}, u32[]{:S(2)}, u32[]{:S(2)}) %all-to-all-start) | async-done | bytes 1048608 | tf_op jit(solution)/shard_map/all_to_all | solution.py:226
  56.1 1.3 reshape.17.refs_1_
  57.4 0.0 copy-done
  57.4 0.0 copy-done.1
  57.4 0.0 copy-start.2
  57.4 1.2 copy-done.2
  58.6 0.5 rise_4.1
  59.1 1.9 %collective-permute-start = (bf16[512,384]{1,0:T(8,128)(2,1)S(1)}, bf16[512,384]{1,0:T(8,128)(2,1)S(1)}, u32[]{:S(2)}, u32[]{:S(2)}) collective-permute-start(bf16[512,384]{1,0:T(8,128)(2,1)S(1)} %rise_4.1), channel_id=1, source_target_pairs={{0,128},{128,256},{256,384},{384,512},{512,640},{640,768},{768,896... | collective-permute-start | bytes 1179656 | tf_op jit(solution)/shard_map/ppermute | solution.py:125
  61.0 0.5 fall_3.1
  61.5 12.3 %collective-permute-start.4 = (bf16[512,384]{1,0:T(8,128)(2,1)S(1)}, bf16[512,384]{1,0:T(8,128)(2,1)S(1)}, u32[]{:S(2)}, u32[]{:S(2)}) collective-permute-start(bf16[512,384]{1,0:T(8,128)(2,1)S(1)} %fall_3.1), channel_id=1, source_target_pairs={{0,896},{128,0},{256,128},{384,256},{512,384},{640,512},{768,640},... | collective-permute-start | bytes 1179656 | tf_op jit(solution)/shard_map/ppermute | solution.py:125
  73.8 6.9 %collective-permute-done.refs_5_ = bf16[512,384]{1,0:T(8,128)(2,1)S(1)} collective-permute-done((bf16[512,384]{1,0:T(8,128)(2,1)S(1)}, bf16[512,384]{1,0:T(8,128)(2,1)S(1)}, u32[]{:S(2)}, u32[]{:S(2)}) %collective-permute-start) | collective-permute-done | bytes 393248 | tf_op jit(solution)/shard_map/ppermute | solution.py:125
  80.7 0.5 rise_3.1
  81.2 1.9 %collective-permute-start.1 = (bf16[512,384]{1,0:T(8,128)(2,1)S(1)}, bf16[512,384]{1,0:T(8,128)(2,1)S(1)}, u32[]{:S(2)}, u32[]{:S(2)}) collective-permute-start(bf16[512,384]{1,0:T(8,128)(2,1)S(1)} %rise_3.1), channel_id=1, source_target_pairs={{0,128},{128,256},{256,384},{384,512},{512,640},{640,768},{768,896... | collective-permute-start | bytes 1179656 | tf_op jit(solution)/shard_map/ppermute | solution.py:125
  83.1 0.0 collective-permute-done.4.refs_5_
  83.1 0.5 fall_2.1
  83.6 4.6 %collective-permute-start.5 = (bf16[512,384]{1,0:T(8,128)(2,1)S(1)}, bf16[512,384]{1,0:T(8,128)(2,1)S(1)}, u32[]{:S(2)}, u32[]{:S(2)}) collective-permute-start(bf16[512,384]{1,0:T(8,128)(2,1)S(1)} %fall_2.1), channel_id=1, source_target_pairs={{0,896},{128,0},{256,128},{384,256},{512,384},{640,512},{768,640},... | collective-permute-start | bytes 1179656 | tf_op jit(solution)/shard_map/ppermute | solution.py:125
  88.1 6.0 %collective-permute-done.1.refs_5_ = bf16[512,384]{1,0:T(8,128)(2,1)S(1)} collective-permute-done((bf16[512,384]{1,0:T(8,128)(2,1)S(1)}, bf16[512,384]{1,0:T(8,128)(2,1)S(1)}, u32[]{:S(2)}, u32[]{:S(2)}) %collective-permute-start.1) | collective-permute-done | bytes 393248 | tf_op jit(solution)/shard_map/ppermute | solution.py:125
  94.1 0.5 rise_2.1
  94.6 1.9 %collective-permute-start.2 = (bf16[512,384]{1,0:T(8,128)(2,1)S(1)}, bf16[512,384]{1,0:T(8,128)(2,1)S(1)}, u32[]{:S(2)}, u32[]{:S(2)}) collective-permute-start(bf16[512,384]{1,0:T(8,128)(2,1)S(1)} %rise_2.1), channel_id=1, source_target_pairs={{0,128},{128,256},{256,384},{384,512},{512,640},{640,768},{768,896... | collective-permute-start | bytes 1179656 | tf_op jit(solution)/shard_map/ppermute | solution.py:125
  96.5 0.0 collective-permute-done.5.refs_5_
  96.5 0.5 fall_1.1
  97.0 4.6 %collective-permute-start.6 = (bf16[512,384]{1,0:T(8,128)(2,1)S(1)}, bf16[512,384]{1,0:T(8,128)(2,1)S(1)}, u32[]{:S(2)}, u32[]{:S(2)}) collective-permute-start(bf16[512,384]{1,0:T(8,128)(2,1)S(1)} %fall_1.1), channel_id=1, source_target_pairs={{0,896},{128,0},{256,128},{384,256},{512,384},{640,512},{768,640},... | collective-permute-start | bytes 1179656 | tf_op jit(solution)/shard_map/ppermute | solution.py:125
  101.6 5.0 %collective-permute-done.2.refs_5_ = bf16[512,384]{1,0:T(8,128)(2,1)S(1)} collective-permute-done((bf16[512,384]{1,0:T(8,128)(2,1)S(1)}, bf16[512,384]{1,0:T(8,128)(2,1)S(1)}, u32[]{:S(2)}, u32[]{:S(2)}) %collective-permute-start.2) | collective-permute-done | bytes 393248 | tf_op jit(solution)/shard_map/ppermute | solution.py:125
  106.6 0.4 rise_1.1
  107.1 1.9 %collective-permute-start.3 = (bf16[512,384]{1,0:T(8,128)(2,1)S(1)}, bf16[512,384]{1,0:T(8,128)(2,1)S(1)}, u32[]{:S(2)}, u32[]{:S(2)}) collective-permute-start(bf16[512,384]{1,0:T(8,128)(2,1)S(1)} %rise_1.1), channel_id=1, source_target_pairs={{0,128},{128,256},{256,384},{384,512},{512,640},{640,768},{768,896... | collective-permute-start | bytes 1179656 | tf_op jit(solution)/shard_map/ppermute | solution.py:125
  109.0 0.5 own_term.1.own_ref
  109.4 0.0 collective-permute-done.6.down_ref
  109.5 8.7 %collective-permute-done.3.up_ref = bf16[512,384]{1,0:T(8,128)(2,1)S(1)} collective-permute-done((bf16[512,384]{1,0:T(8,128)(2,1)S(1)}, bf16[512,384]{1,0:T(8,128)(2,1)S(1)}, u32[]{:S(2)}, u32[]{:S(2)}) %collective-permute-start.3) | collective-permute-done | bytes 393248 | tf_op jit(solution)/shard_map/ppermute | solution.py:125
  118.2 0.2 activate.1.refs_1_
  118.4 1.9 %collective-permute-start.7 = (bf16[512,256]{1,0:T(8,128)(2,1)S(1)}, bf16[512,256]{1,0:T(8,128)(2,1)S(1)}, u32[]{:S(2)}, u32[]{:S(2)}) collective-permute-start(bf16[512,256]{1,0:T(8,128)(2,1)S(1)} %activate.1.refs_1_), channel_id=1, source_target_pairs={{0,128},{128,256},{256,384},{384,512},{512,640},{640,768},{768,896... | collective-permute-start | bytes 786440 | tf_op jit(solution)/shard_map/ppermute | solution.py:125
  120.3 4.6 %collective-permute-start.11 = (bf16[512,256]{1,0:T(8,128)(2,1)S(1)}, bf16[512,256]{1,0:T(8,128)(2,1)S(1)}, u32[]{:S(2)}, u32[]{:S(2)}) collective-permute-start(bf16[512,256]{1,0:T(8,128)(2,1)S(1)} %activate.1.refs_1_), channel_id=1, source_target_pairs={{0,896},{128,0},{256,128},{384,256},{512,384},{640,512},{768,640},... | collective-permute-start | bytes 786440 | tf_op jit(solution)/shard_map/ppermute | solution.py:125
  124.9 1.8 collective-permute-done.7.refs_2_
  126.7 1.9 %collective-permute-start.8 = (bf16[512,256]{1,0:T(8,128)(2,1)S(1)}, bf16[512,256]{1,0:T(8,128)(2,1)S(1)}, u32[]{:S(2)}, u32[]{:S(2)}) collective-permute-start(bf16[512,256]{1,0:T(8,128)(2,1)S(1)} %collective-permute-done.7.refs_2_), channel_id=1, source_target_pairs={{0,128},{128,256},{256,384},{384,512},{512,640},{640,768},{768,896... | collective-permute-start | bytes 786440 | tf_op jit(solution)/shard_map/ppermute | solution.py:125
  128.6 0.0 collective-permute-done.11.refs_3_
  128.6 4.6 %collective-permute-start.12 = (bf16[512,256]{1,0:T(8,128)(2,1)S(1)}, bf16[512,256]{1,0:T(8,128)(2,1)S(1)}, u32[]{:S(2)}, u32[]{:S(2)}) collective-permute-start(bf16[512,256]{1,0:T(8,128)(2,1)S(1)} %collective-permute-done.11.refs_3_), channel_id=1, source_target_pairs={{0,896},{128,0},{256,128},{384,256},{512,384},{640,512},{768,640},... | collective-permute-start | bytes 786440 | tf_op jit(solution)/shard_map/ppermute | solution.py:125
  133.2 1.8 collective-permute-done.8.refs_4_
  135.0 1.9 %collective-permute-start.9 = (bf16[512,256]{1,0:T(8,128)(2,1)S(1)}, bf16[512,256]{1,0:T(8,128)(2,1)S(1)}, u32[]{:S(2)}, u32[]{:S(2)}) collective-permute-start(bf16[512,256]{1,0:T(8,128)(2,1)S(1)} %collective-permute-done.8.refs_4_), channel_id=1, source_target_pairs={{0,128},{128,256},{256,384},{384,512},{512,640},{640,768},{768,896... | collective-permute-start | bytes 786440 | tf_op jit(solution)/shard_map/ppermute | solution.py:125
  136.9 0.0 collective-permute-done.12.refs_5_
  136.9 4.6 %collective-permute-start.13 = (bf16[512,256]{1,0:T(8,128)(2,1)S(1)}, bf16[512,256]{1,0:T(8,128)(2,1)S(1)}, u32[]{:S(2)}, u32[]{:S(2)}) collective-permute-start(bf16[512,256]{1,0:T(8,128)(2,1)S(1)} %collective-permute-done.12.refs_5_), channel_id=1, source_target_pairs={{0,896},{128,0},{256,128},{384,256},{512,384},{640,512},{768,640},... | collective-permute-start | bytes 786440 | tf_op jit(solution)/shard_map/ppermute | solution.py:125
  141.5 1.8 collective-permute-done.9.refs_6_
  143.3 1.9 %collective-permute-start.10 = (bf16[512,256]{1,0:T(8,128)(2,1)S(1)}, bf16[512,256]{1,0:T(8,128)(2,1)S(1)}, u32[]{:S(2)}, u32[]{:S(2)}) collective-permute-start(bf16[512,256]{1,0:T(8,128)(2,1)S(1)} %collective-permute-done.9.refs_6_), channel_id=1, source_target_pairs={{0,128},{128,256},{256,384},{384,512},{512,640},{640,768},{768,896... | collective-permute-start | bytes 786440 | tf_op jit(solution)/shard_map/ppermute | solution.py:125
  145.2 0.0 collective-permute-done.13.refs_7_
  145.3 1.2 row_grad_near.1.refs_4_
  146.5 6.0 %collective-permute-done.10.refs_1_ = bf16[512,256]{1,0:T(8,128)(2,1)S(1)} collective-permute-done((bf16[512,256]{1,0:T(8,128)(2,1)S(1)}, bf16[512,256]{1,0:T(8,128)(2,1)S(1)}, u32[]{:S(2)}, u32[]{:S(2)}) %collective-permute-start.10) | collective-permute-done | bytes 262176 | tf_op jit(solution)/shard_map/ppermute | solution.py:125
  152.4 0.3 row_grad_far.1
  152.8 0.1 reshape.18
  152.9 34.3 %all_to_all.10 = bf16[128,4,512]{2,1,0:T(4,128)(2,1)S(1)} all-to-all(bf16[128,4,512]{2,1,0:T(4,128)(2,1)S(1)} %reshape.18), channel_id=1, replica_groups=mesh['rep'=8,'outer'=8,'local'=16] {'outer','local'}, dimensions={0} | all-to-all | bytes 1048576 | tf_op jit(solution)/shard_map/all_to_all | solution.py:226
  187.2 0.0 copy-start.3
  187.2 0.1 reshape.19
  187.3 0.6 copy-done.3
  187.9 0.8 convolution_convert_fusion
Async XLA Ops:
  5.0 51.1 %all-to-all-start = ((bf16[128,4,1024]{2,1,0:T(4,128)(2,1)}), bf16[128,4,1024]{2,1,0:T(4,128)(2,1)}, u32[]{:S(2)}, u32[]{:S(2)}) async-start(bf16[128,4,1024]{2,1,0:T(4,128)(2,1)} %reshape.16), calls=%async_computation | async-start | bytes 2097152 | tf_op jit(solution)/shard_map/all_to_all | solution.py:226
  25.4 32.0 %copy-start = (bf16[1,512,1024]{2,1,0:T(8,128)(2,1)S(1)}, bf16[1,512,1024]{2,1,0:T(8,128)(2,1)}, u32[]{:S(2)}) copy-start(bf16[1,512,1024]{2,1,0:T(8,128)(2,1)} %refs_2_.19) | copy-start | bytes 3145732
  25.4 32.0 %copy-start.1 = (bf16[1,512,1024]{2,1,0:T(8,128)(2,1)S(1)}, bf16[1,512,1024]{2,1,0:T(8,128)(2,1)}, u32[]{:S(2)}) copy-start(bf16[1,512,1024]{2,1,0:T(8,128)(2,1)} %refs_3_.19) | copy-start | bytes 3145732
  57.4 1.2 copy-start.2
  59.1 21.6 %collective-permute-start = (bf16[512,384]{1,0:T(8,128)(2,1)S(1)}, bf16[512,384]{1,0:T(8,128)(2,1)S(1)}, u32[]{:S(2)}, u32[]{:S(2)}) collective-permute-start(bf16[512,384]{1,0:T(8,128)(2,1)S(1)} %rise_4.1), channel_id=1, source_target_pairs={{0,128},{128,256},{256,384},{384,512},{512,640},{640,768},{768,896... | collective-permute-start | bytes 1179656 | tf_op jit(solution)/shard_map/ppermute | solution.py:125
  61.5 21.6 %collective-permute-start.4 = (bf16[512,384]{1,0:T(8,128)(2,1)S(1)}, bf16[512,384]{1,0:T(8,128)(2,1)S(1)}, u32[]{:S(2)}, u32[]{:S(2)}) collective-permute-start(bf16[512,384]{1,0:T(8,128)(2,1)S(1)} %fall_3.1), channel_id=1, source_target_pairs={{0,896},{128,0},{256,128},{384,256},{512,384},{640,512},{768,640},... | collective-permute-start | bytes 1179656 | tf_op jit(solution)/shard_map/ppermute | solution.py:125
  81.2 13.0 %collective-permute-start.1 = (bf16[512,384]{1,0:T(8,128)(2,1)S(1)}, bf16[512,384]{1,0:T(8,128)(2,1)S(1)}, u32[]{:S(2)}, u32[]{:S(2)}) collective-permute-start(bf16[512,384]{1,0:T(8,128)(2,1)S(1)} %rise_3.1), channel_id=1, source_target_pairs={{0,128},{128,256},{256,384},{384,512},{512,640},{640,768},{768,896... | collective-permute-start | bytes 1179656 | tf_op jit(solution)/shard_map/ppermute | solution.py:125
  83.6 12.9 %collective-permute-start.5 = (bf16[512,384]{1,0:T(8,128)(2,1)S(1)}, bf16[512,384]{1,0:T(8,128)(2,1)S(1)}, u32[]{:S(2)}, u32[]{:S(2)}) collective-permute-start(bf16[512,384]{1,0:T(8,128)(2,1)S(1)} %fall_2.1), channel_id=1, source_target_pairs={{0,896},{128,0},{256,128},{384,256},{512,384},{640,512},{768,640},... | collective-permute-start | bytes 1179656 | tf_op jit(solution)/shard_map/ppermute | solution.py:125
  94.6 12.0 %collective-permute-start.2 = (bf16[512,384]{1,0:T(8,128)(2,1)S(1)}, bf16[512,384]{1,0:T(8,128)(2,1)S(1)}, u32[]{:S(2)}, u32[]{:S(2)}) collective-permute-start(bf16[512,384]{1,0:T(8,128)(2,1)S(1)} %rise_2.1), channel_id=1, source_target_pairs={{0,128},{128,256},{256,384},{384,512},{512,640},{640,768},{768,896... | collective-permute-start | bytes 1179656 | tf_op jit(solution)/shard_map/ppermute | solution.py:125
  97.0 12.5 %collective-permute-start.6 = (bf16[512,384]{1,0:T(8,128)(2,1)S(1)}, bf16[512,384]{1,0:T(8,128)(2,1)S(1)}, u32[]{:S(2)}, u32[]{:S(2)}) collective-permute-start(bf16[512,384]{1,0:T(8,128)(2,1)S(1)} %fall_1.1), channel_id=1, source_target_pairs={{0,896},{128,0},{256,128},{384,256},{512,384},{640,512},{768,640},... | collective-permute-start | bytes 1179656 | tf_op jit(solution)/shard_map/ppermute | solution.py:125
  107.1 11.1 %collective-permute-start.3 = (bf16[512,384]{1,0:T(8,128)(2,1)S(1)}, bf16[512,384]{1,0:T(8,128)(2,1)S(1)}, u32[]{:S(2)}, u32[]{:S(2)}) collective-permute-start(bf16[512,384]{1,0:T(8,128)(2,1)S(1)} %rise_1.1), channel_id=1, source_target_pairs={{0,128},{128,256},{256,384},{384,512},{512,640},{640,768},{768,896... | collective-permute-start | bytes 1179656 | tf_op jit(solution)/shard_map/ppermute | solution.py:125
  118.4 8.3 %collective-permute-start.7 = (bf16[512,256]{1,0:T(8,128)(2,1)S(1)}, bf16[512,256]{1,0:T(8,128)(2,1)S(1)}, u32[]{:S(2)}, u32[]{:S(2)}) collective-permute-start(bf16[512,256]{1,0:T(8,128)(2,1)S(1)} %activate.1.refs_1_), channel_id=1, source_target_pairs={{0,128},{128,256},{256,384},{384,512},{512,640},{640,768},{768,896... | collective-permute-start | bytes 786440 | tf_op jit(solution)/shard_map/ppermute | solution.py:125
  120.3 8.3 %collective-permute-start.11 = (bf16[512,256]{1,0:T(8,128)(2,1)S(1)}, bf16[512,256]{1,0:T(8,128)(2,1)S(1)}, u32[]{:S(2)}, u32[]{:S(2)}) collective-permute-start(bf16[512,256]{1,0:T(8,128)(2,1)S(1)} %activate.1.refs_1_), channel_id=1, source_target_pairs={{0,896},{128,0},{256,128},{384,256},{512,384},{640,512},{768,640},... | collective-permute-start | bytes 786440 | tf_op jit(solution)/shard_map/ppermute | solution.py:125
  126.7 8.3 %collective-permute-start.8 = (bf16[512,256]{1,0:T(8,128)(2,1)S(1)}, bf16[512,256]{1,0:T(8,128)(2,1)S(1)}, u32[]{:S(2)}, u32[]{:S(2)}) collective-permute-start(bf16[512,256]{1,0:T(8,128)(2,1)S(1)} %collective-permute-done.7.refs_2_), channel_id=1, source_target_pairs={{0,128},{128,256},{256,384},{384,512},{512,640},{640,768},{768,896... | collective-permute-start | bytes 786440 | tf_op jit(solution)/shard_map/ppermute | solution.py:125
  128.6 8.3 %collective-permute-start.12 = (bf16[512,256]{1,0:T(8,128)(2,1)S(1)}, bf16[512,256]{1,0:T(8,128)(2,1)S(1)}, u32[]{:S(2)}, u32[]{:S(2)}) collective-permute-start(bf16[512,256]{1,0:T(8,128)(2,1)S(1)} %collective-permute-done.11.refs_3_), channel_id=1, source_target_pairs={{0,896},{128,0},{256,128},{384,256},{512,384},{640,512},{768,640},... | collective-permute-start | bytes 786440 | tf_op jit(solution)/shard_map/ppermute | solution.py:125
  135.0 8.3 %collective-permute-start.9 = (bf16[512,256]{1,0:T(8,128)(2,1)S(1)}, bf16[512,256]{1,0:T(8,128)(2,1)S(1)}, u32[]{:S(2)}, u32[]{:S(2)}) collective-permute-start(bf16[512,256]{1,0:T(8,128)(2,1)S(1)} %collective-permute-done.8.refs_4_), channel_id=1, source_target_pairs={{0,128},{128,256},{256,384},{384,512},{512,640},{640,768},{768,896... | collective-permute-start | bytes 786440 | tf_op jit(solution)/shard_map/ppermute | solution.py:125
  136.9 8.3 %collective-permute-start.13 = (bf16[512,256]{1,0:T(8,128)(2,1)S(1)}, bf16[512,256]{1,0:T(8,128)(2,1)S(1)}, u32[]{:S(2)}, u32[]{:S(2)}) collective-permute-start(bf16[512,256]{1,0:T(8,128)(2,1)S(1)} %collective-permute-done.12.refs_5_), channel_id=1, source_target_pairs={{0,896},{128,0},{256,128},{384,256},{512,384},{640,512},{768,640},... | collective-permute-start | bytes 786440 | tf_op jit(solution)/shard_map/ppermute | solution.py:125
  143.3 9.1 %collective-permute-start.10 = (bf16[512,256]{1,0:T(8,128)(2,1)S(1)}, bf16[512,256]{1,0:T(8,128)(2,1)S(1)}, u32[]{:S(2)}, u32[]{:S(2)}) collective-permute-start(bf16[512,256]{1,0:T(8,128)(2,1)S(1)} %collective-permute-done.9.refs_6_), channel_id=1, source_target_pairs={{0,128},{128,256},{256,384},{384,512},{512,640},{640,768},{768,896... | collective-permute-start | bytes 786440 | tf_op jit(solution)/shard_map/ppermute | solution.py:125
  187.2 0.8 copy-start.3

commit v8 on v7

--- a/solution.py
+++ b/solution.py
@@ -28,7 +28,7 @@
     top, tok = ids_ref.shape
     width = tok_ref.shape[1]
     rows = top * tok
-    slots = send_ref.shape[0]
+    slots = pt_ref.shape[1]
     c_row = lax.broadcasted_iota(jnp.int32, (rows, tok), 0)
     pick_i = (c_row % tok == lax.broadcasted_iota(jnp.int32, (rows, tok), 1)).astype(BF16)
     c_k = lax.broadcasted_iota(jnp.int32, (rows, top), 0)
@@ -54,19 +54,27 @@
     ids_row = jnp.sum(jnp.where(sub == lane, ids_col, 0.0), axis=0, keepdims=True)
     earlier = (ids_col == ids_row) & (order_sub < order_lane)
     slot_row = jnp.sum(jnp.where(earlier, 1.0, 0.0), axis=0, keepdims=True)
-    code = jnp.where(slot_row < capacity, ids_row * capacity + slot_row, -1.0).astype(jnp.int32)
-    table = (lax.broadcasted_iota(jnp.int32, (slots, rows), 0) == code).astype(F32).astype(BF16)
-    per_token = jnp.dot(table, pick_i, preferred_element_type=F32).astype(BF16)
+    kept = slot_row < capacity
+
+    def table(size, stride, offset):
+        code = jnp.where(kept, ids_row * stride + slot_row + offset, -1.0).astype(jnp.int32)
+        slot = lax.broadcasted_iota(jnp.int32, (size, rows), 0)
+        return (slot == code).astype(F32).astype(BF16)
+
     pt_ref[...] = lax.dot_general(
-        pick_i, table, (((0,), (1,)), ((), ())), preferred_element_type=F32
+        pick_i,
+        table(slots, capacity, 0),
+        (((0,), (1,)), ((), ())),
+        preferred_element_type=F32,
     ).astype(BF16)
     og = jnp.dot(pick_i, og_ref[...], preferred_element_type=F32)
     scaled_ref[...] = (w_col * og).astype(BF16)
-    send_ref[:, :width] = jnp.dot(
-        per_token, tok_ref[...], preferred_element_type=F32
-    ).astype(BF16)
-    send_ref[:, width:] = jnp.dot(
-        table, scaled_ref[...], preferred_element_type=F32
+    for_x = table(2 * slots, 2 * capacity, 0)
+    per_token = jnp.dot(for_x, pick_i, preferred_element_type=F32).astype(BF16)
+    for_dy = table(2 * slots, 2 * capacity, capacity)
+    send_ref[...] = (
+        jnp.dot(per_token, tok_ref[...], preferred_element_type=F32)
+        + jnp.dot(for_dy, scaled_ref[...], preferred_element_type=F32)
     ).astype(BF16)
 
 
@@ -79,7 +87,7 @@
         in_specs=[pl.BlockSpec(memory_space=pltpu.HBM)] * 4,
         out_specs=(VMEM_SPEC, VMEM_SPEC),
         out_shape=(
-            jax.ShapeDtypeStruct((slots, 2 * width), BF16),
+            jax.ShapeDtypeStruct((2 * slots, width), BF16),
             jax.ShapeDtypeStruct((tok, slots), BF16),
         ),
         scratch_shapes=[
@@ -95,6 +103,33 @@
     )(expert_ids.T, route_weights.T, tokens, out_grad)
 
 
+def split_kernel(capacity, in_ref, out_ref):
+    width = in_ref.shape[1]
+    block = 32 * capacity
+    rows = block // 2
+    r = lax.broadcasted_iota(jnp.int32, (rows, block), 0)
+    place = (r // capacity) * (2 * capacity) + r % capacity
+    lane = lax.broadcasted_iota(jnp.int32, (rows, block), 1)
+    for half in range(2):
+        pick = (lane == place + half * capacity).astype(F32).astype(BF16)
+        for b in range(in_ref.shape[0] // block):
+            out_ref[b * rows : (b + 1) * rows, half * width : (half + 1) * width] = jnp.dot(
+                pick, in_ref[b * block : (b + 1) * block, :], preferred_element_type=F32
+            ).astype(BF16)
+
+
+def split(received, capacity):
+    rows, width = received.shape
+    return pl.pallas_call(
+        lambda *refs: split_kernel(capacity, *refs),
+        in_specs=[VMEM_SPEC],
+        out_specs=VMEM_SPEC,
+        out_shape=jax.ShapeDtypeStruct((rows // 2, 2 * width), BF16),
+        compiler_params=params(),
+        name="split",
+    )(received)
+
+
 def chunk_start(me_ref, offset, n_rep, part):
     return pl.multiple_of(lax.rem(me_ref[0] + offset, n_rep) * part, part)
 
@@ -222,10 +257,10 @@
     send, per_token_t = route(tokens, out_grad, expert_ids, route_weights, experts, capacity)
 
     def exchange(rows):
-        blocks = rows.reshape(experts, capacity, rows.shape[1])
+        blocks = rows.reshape(experts, rows.shape[0] // experts, width)
         return lax.all_to_all(blocks, ("outer", "local"), 0, 0, tiled=True).reshape(rows.shape)
 
-    both_rows = exchange(send)
+    both_rows = split(exchange(send), capacity)
     own = activate(
         *width_sums(me, both_rows, gate_weight, up_weight, down_weight, n_rep)
     )

time: 190 us -> 187 us (0.984)
  local copies, waits for them, and re-layouts: 5.69 us -> 1.97 us
    reshape x2 -> x1, local copies, waits for them, and re-layouts: 2.37 us -> 0.12 us  [exchange(): blocks = rows.reshape(experts, rows.shape[0] // experts, width)]
where the time goes in v8:
time: 187 us; the launch traced here: 186 us
  starting transfers between devices  70.6 us (38%)
  waiting for transfers between devices  69.1 us (37%)
  blocking collectives  34.2 us (18%)
  Pallas kernels  8.99 us (5%)
  local copies, waits for them, and re-layouts  1.97 us (1%)
    ppermute x14, starting transfers between devices, shift(): lax.ppermute(rows, 'rep', [(i, (i + by) % n_rep) for i in range(n_rep)])  51.1 us
    ppermute x14, waiting for transfers between devices, shift(): lax.ppermute(rows, 'rep', [(i, (i + by) % n_rep) for i in range(n_rep)])  38.1 us
    all_to_all x1, blocking collectives, exchange(): lax.all_to_all(blocks, ('outer', 'local'), 0, 0, tiled=True)  34.2 us
    all_to_all x1, waiting for transfers between devices, exchange(): lax.all_to_all(blocks, ('outer', 'local'), 0, 0, tiled=True)  31 us
    all_to_all x1, starting transfers between devices, exchange(): lax.all_to_all(blocks, ('outer', 'local'), 0, 0, tiled=True)  19.5 us
  transfers between devices with their start and end apart: 15, of which 9 were waited for; matrix products, arithmetic and copies ran while one was open for 0% of the time, Pallas kernels for 2%

profile of v8, /device:TPU:1, one launch (start us, length us, event | category | flops | bytes accessed | tf_op | source)
XLA Modules:
  0.0 185.9 jit_solution(16292471838252231075)
XLA Ops:
  0.0 3.1 %route.1 = (bf16[1024,512]{1,0:T(8,128)(2,1)}, bf16[32,512]{1,0:T(8,128)(2,1)}) custom-call(s32[8,32]{1,0:T(8,128)} %bitcast.9, f32[8,32]{1,0:T(8,128)} %bitcast.10, bf16[32,512]{1,0:T(8,128)(2,1)} %refs_2_.10, bf16[32,512]{1,0:T(8,128)(2,1)} %refs_3_.10), custom_call_target="tpu_custom_call" | custom-call | tf_op jit(solution)/shard_map/route/pallas_call | solution.py:85
  3.1 0.0 copy-start.2
  3.1 19.5 %all-to-all-start = ((bf16[128,8,512]{2,1,0:T(8,128)(2,1)}), bf16[128,8,512]{2,1,0:T(8,128)(2,1)S(1)}, u32[]{:S(2)}, u32[]{:S(2)}) async-start(bf16[128,8,512]{2,1,0:T(8,128)(2,1)} %bitcast.8), calls=%async_computation | async-start | bytes 2097152 | tf_op jit(solution)/shard_map/all_to_all | solution.py:261
  22.6 31.0 %all-to-all-done = bf16[128,8,512]{2,1,0:T(8,128)(2,1)S(1)} async-done(((bf16[128,8,512]{2,1,0:T(8,128)(2,1)}), bf16[128,8,512]{2,1,0:T(8,128)(2,1)S(1)}, u32[]{:S(2)}, u32[]{:S(2)}) %all-to-all-start) | async-done | bytes 1048608 | tf_op jit(solution)/shard_map/all_to_all | solution.py:261
  53.7 0.0 copy-start
  53.7 0.0 copy-start.1
  53.7 0.4 split.1.refs_1_
  54.1 0.0 copy-done.2
  54.1 0.8 copy-done
  54.9 0.3 copy-done.1
  55.2 0.5 rise_4.1
  55.7 1.9 %collective-permute-start = (bf16[512,384]{1,0:T(8,128)(2,1)S(1)}, bf16[512,384]{1,0:T(8,128)(2,1)S(1)}, u32[]{:S(2)}, u32[]{:S(2)}) collective-permute-start(bf16[512,384]{1,0:T(8,128)(2,1)S(1)} %rise_4.1), channel_id=1, source_target_pairs={{0,128},{128,256},{256,384},{384,512},{512,640},{640,768},{768,896... | collective-permute-start | bytes 1179656 | tf_op jit(solution)/shard_map/ppermute | solution.py:160
  57.6 0.5 fall_3.1
  58.1 12.9 %collective-permute-start.4 = (bf16[512,384]{1,0:T(8,128)(2,1)S(1)}, bf16[512,384]{1,0:T(8,128)(2,1)S(1)}, u32[]{:S(2)}, u32[]{:S(2)}) collective-permute-start(bf16[512,384]{1,0:T(8,128)(2,1)S(1)} %fall_3.1), channel_id=1, source_target_pairs={{0,896},{128,0},{256,128},{384,256},{512,384},{640,512},{768,640},... | collective-permute-start | bytes 1179656 | tf_op jit(solution)/shard_map/ppermute | solution.py:160
  71.0 6.9 %collective-permute-done.refs_5_ = bf16[512,384]{1,0:T(8,128)(2,1)S(1)} collective-permute-done((bf16[512,384]{1,0:T(8,128)(2,1)S(1)}, bf16[512,384]{1,0:T(8,128)(2,1)S(1)}, u32[]{:S(2)}, u32[]{:S(2)}) %collective-permute-start) | collective-permute-done | bytes 393248 | tf_op jit(solution)/shard_map/ppermute | solution.py:160
  77.8 0.5 rise_3.1
  78.3 1.9 %collective-permute-start.1 = (bf16[512,384]{1,0:T(8,128)(2,1)S(1)}, bf16[512,384]{1,0:T(8,128)(2,1)S(1)}, u32[]{:S(2)}, u32[]{:S(2)}) collective-permute-start(bf16[512,384]{1,0:T(8,128)(2,1)S(1)} %rise_3.1), channel_id=1, source_target_pairs={{0,128},{128,256},{256,384},{384,512},{512,640},{640,768},{768,896... | collective-permute-start | bytes 1179656 | tf_op jit(solution)/shard_map/ppermute | solution.py:160
  80.2 0.0 collective-permute-done.4.refs_5_
  80.2 0.5 fall_2.1
  80.7 4.6 %collective-permute-start.5 = (bf16[512,384]{1,0:T(8,128)(2,1)S(1)}, bf16[512,384]{1,0:T(8,128)(2,1)S(1)}, u32[]{:S(2)}, u32[]{:S(2)}) collective-permute-start(bf16[512,384]{1,0:T(8,128)(2,1)S(1)} %fall_2.1), channel_id=1, source_target_pairs={{0,896},{128,0},{256,128},{384,256},{512,384},{640,512},{768,640},... | collective-permute-start | bytes 1179656 | tf_op jit(solution)/shard_map/ppermute | solution.py:160
  85.3 6.0 %collective-permute-done.1.refs_5_ = bf16[512,384]{1,0:T(8,128)(2,1)S(1)} collective-permute-done((bf16[512,384]{1,0:T(8,128)(2,1)S(1)}, bf16[512,384]{1,0:T(8,128)(2,1)S(1)}, u32[]{:S(2)}, u32[]{:S(2)}) %collective-permute-start.1) | collective-permute-done | bytes 393248 | tf_op jit(solution)/shard_map/ppermute | solution.py:160
  91.3 0.5 rise_2.1
  91.7 1.9 %collective-permute-start.2 = (bf16[512,384]{1,0:T(8,128)(2,1)S(1)}, bf16[512,384]{1,0:T(8,128)(2,1)S(1)}, u32[]{:S(2)}, u32[]{:S(2)}) collective-permute-start(bf16[512,384]{1,0:T(8,128)(2,1)S(1)} %rise_2.1), channel_id=1, source_target_pairs={{0,128},{128,256},{256,384},{384,512},{512,640},{640,768},{768,896... | collective-permute-start | bytes 1179656 | tf_op jit(solution)/shard_map/ppermute | solution.py:160
  93.7 0.0 collective-permute-done.5.refs_5_
  93.7 0.5 fall_1.1
  94.2 4.6 %collective-permute-start.6 = (bf16[512,384]{1,0:T(8,128)(2,1)S(1)}, bf16[512,384]{1,0:T(8,128)(2,1)S(1)}, u32[]{:S(2)}, u32[]{:S(2)}) collective-permute-start(bf16[512,384]{1,0:T(8,128)(2,1)S(1)} %fall_1.1), channel_id=1, source_target_pairs={{0,896},{128,0},{256,128},{384,256},{512,384},{640,512},{768,640},... | collective-permute-start | bytes 1179656 | tf_op jit(solution)/shard_map/ppermute | solution.py:160
  98.7 5.1 %collective-permute-done.2.refs_5_ = bf16[512,384]{1,0:T(8,128)(2,1)S(1)} collective-permute-done((bf16[512,384]{1,0:T(8,128)(2,1)S(1)}, bf16[512,384]{1,0:T(8,128)(2,1)S(1)}, u32[]{:S(2)}, u32[]{:S(2)}) %collective-permute-start.2) | collective-permute-done | bytes 393248 | tf_op jit(solution)/shard_map/ppermute | solution.py:160
  103.8 0.5 rise_1.1
  104.3 1.9 %collective-permute-start.3 = (bf16[512,384]{1,0:T(8,128)(2,1)S(1)}, bf16[512,384]{1,0:T(8,128)(2,1)S(1)}, u32[]{:S(2)}, u32[]{:S(2)}) collective-permute-start(bf16[512,384]{1,0:T(8,128)(2,1)S(1)} %rise_1.1), channel_id=1, source_target_pairs={{0,128},{128,256},{256,384},{384,512},{512,640},{640,768},{768,896... | collective-permute-start | bytes 1179656 | tf_op jit(solution)/shard_map/ppermute | solution.py:160
  106.2 0.5 own_term.1.own_ref
  106.7 0.0 collective-permute-done.6.down_ref
  106.7 8.7 %collective-permute-done.3.up_ref = bf16[512,384]{1,0:T(8,128)(2,1)S(1)} collective-permute-done((bf16[512,384]{1,0:T(8,128)(2,1)S(1)}, bf16[512,384]{1,0:T(8,128)(2,1)S(1)}, u32[]{:S(2)}, u32[]{:S(2)}) %collective-permute-start.3) | collective-permute-done | bytes 393248 | tf_op jit(solution)/shard_map/ppermute | solution.py:160
  115.4 0.2 activate.1.refs_1_
  115.6 1.9 %collective-permute-start.7 = (bf16[512,256]{1,0:T(8,128)(2,1)S(1)}, bf16[512,256]{1,0:T(8,128)(2,1)S(1)}, u32[]{:S(2)}, u32[]{:S(2)}) collective-permute-start(bf16[512,256]{1,0:T(8,128)(2,1)S(1)} %activate.1.refs_1_), channel_id=1, source_target_pairs={{0,128},{128,256},{256,384},{384,512},{512,640},{640,768},{768,896... | collective-permute-start | bytes 786440 | tf_op jit(solution)/shard_map/ppermute | solution.py:160
  117.6 4.6 %collective-permute-start.11 = (bf16[512,256]{1,0:T(8,128)(2,1)S(1)}, bf16[512,256]{1,0:T(8,128)(2,1)S(1)}, u32[]{:S(2)}, u32[]{:S(2)}) collective-permute-start(bf16[512,256]{1,0:T(8,128)(2,1)S(1)} %activate.1.refs_1_), channel_id=1, source_target_pairs={{0,896},{128,0},{256,128},{384,256},{512,384},{640,512},{768,640},... | collective-permute-start | bytes 786440 | tf_op jit(solution)/shard_map/ppermute | solution.py:160
  122.1 1.8 collective-permute-done.7.refs_2_
  124.0 1.9 %collective-permute-start.8 = (bf16[512,256]{1,0:T(8,128)(2,1)S(1)}, bf16[512,256]{1,0:T(8,128)(2,1)S(1)}, u32[]{:S(2)}, u32[]{:S(2)}) collective-permute-start(bf16[512,256]{1,0:T(8,128)(2,1)S(1)} %collective-permute-done.7.refs_2_), channel_id=1, source_target_pairs={{0,128},{128,256},{256,384},{384,512},{512,640},{640,768},{768,896... | collective-permute-start | bytes 786440 | tf_op jit(solution)/shard_map/ppermute | solution.py:160
  125.9 0.0 collective-permute-done.11.refs_3_
  125.9 4.6 %collective-permute-start.12 = (bf16[512,256]{1,0:T(8,128)(2,1)S(1)}, bf16[512,256]{1,0:T(8,128)(2,1)S(1)}, u32[]{:S(2)}, u32[]{:S(2)}) collective-permute-start(bf16[512,256]{1,0:T(8,128)(2,1)S(1)} %collective-permute-done.11.refs_3_), channel_id=1, source_target_pairs={{0,896},{128,0},{256,128},{384,256},{512,384},{640,512},{768,640},... | collective-permute-start | bytes 786440 | tf_op jit(solution)/shard_map/ppermute | solution.py:160
  130.5 1.8 collective-permute-done.8.refs_4_
  132.3 1.9 %collective-permute-start.9 = (bf16[512,256]{1,0:T(8,128)(2,1)S(1)}, bf16[512,256]{1,0:T(8,128)(2,1)S(1)}, u32[]{:S(2)}, u32[]{:S(2)}) collective-permute-start(bf16[512,256]{1,0:T(8,128)(2,1)S(1)} %collective-permute-done.8.refs_4_), channel_id=1, source_target_pairs={{0,128},{128,256},{256,384},{384,512},{512,640},{640,768},{768,896... | collective-permute-start | bytes 786440 | tf_op jit(solution)/shard_map/ppermute | solution.py:160
  134.2 0.0 collective-permute-done.12.refs_5_
  134.2 4.6 %collective-permute-start.13 = (bf16[512,256]{1,0:T(8,128)(2,1)S(1)}, bf16[512,256]{1,0:T(8,128)(2,1)S(1)}, u32[]{:S(2)}, u32[]{:S(2)}) collective-permute-start(bf16[512,256]{1,0:T(8,128)(2,1)S(1)} %collective-permute-done.12.refs_5_), channel_id=1, source_target_pairs={{0,896},{128,0},{256,128},{384,256},{512,384},{640,512},{768,640},... | collective-permute-start | bytes 786440 | tf_op jit(solution)/shard_map/ppermute | solution.py:160
  138.8 1.8 collective-permute-done.9.refs_6_
  140.6 1.9 %collective-permute-start.10 = (bf16[512,256]{1,0:T(8,128)(2,1)S(1)}, bf16[512,256]{1,0:T(8,128)(2,1)S(1)}, u32[]{:S(2)}, u32[]{:S(2)}) collective-permute-start(bf16[512,256]{1,0:T(8,128)(2,1)S(1)} %collective-permute-done.9.refs_6_), channel_id=1, source_target_pairs={{0,128},{128,256},{256,384},{384,512},{512,640},{640,768},{768,896... | collective-permute-start | bytes 786440 | tf_op jit(solution)/shard_map/ppermute | solution.py:160
  142.5 0.0 collective-permute-done.13.refs_7_
  142.5 1.2 row_grad_near.1.refs_4_
  143.7 5.9 %collective-permute-done.10.refs_1_ = bf16[512,256]{1,0:T(8,128)(2,1)S(1)} collective-permute-done((bf16[512,256]{1,0:T(8,128)(2,1)S(1)}, bf16[512,256]{1,0:T(8,128)(2,1)S(1)}, u32[]{:S(2)}, u32[]{:S(2)}) %collective-permute-start.10) | collective-permute-done | bytes 262176 | tf_op jit(solution)/shard_map/ppermute | solution.py:160
  149.7 0.3 row_grad_far.1
  150.0 0.1 reshape.18
  150.1 34.2 %all_to_all.10 = bf16[128,4,512]{2,1,0:T(4,128)(2,1)S(1)} all-to-all(bf16[128,4,512]{2,1,0:T(4,128)(2,1)S(1)} %reshape.18), channel_id=1, replica_groups=mesh['rep'=8,'outer'=8,'local'=16] {'outer','local'}, dimensions={0} | all-to-all | bytes 1048576 | tf_op jit(solution)/shard_map/all_to_all | solution.py:261
  184.3 0.0 copy-start.3
  184.3 0.1 reshape.19
  184.4 0.6 copy-done.3
  185.1 0.8 convolution_convert_fusion
Async XLA Ops:
  3.1 51.0 %copy-start.2 = (bf16[1,1024,512]{2,1,0:T(8,128)(2,1)S(1)}, bf16[1,1024,512]{2,1,0:T(8,128)(2,1)}, u32[]{:S(2)}) copy-start(bf16[1,1024,512]{2,1,0:T(8,128)(2,1)} %refs_4_.15) | copy-start | bytes 3145732
  3.1 50.5 %all-to-all-start = ((bf16[128,8,512]{2,1,0:T(8,128)(2,1)}), bf16[128,8,512]{2,1,0:T(8,128)(2,1)S(1)}, u32[]{:S(2)}, u32[]{:S(2)}) async-start(bf16[128,8,512]{2,1,0:T(8,128)(2,1)} %bitcast.8), calls=%async_computation | async-start | bytes 2097152 | tf_op jit(solution)/shard_map/all_to_all | solution.py:261
  53.7 1.2 copy-start
  53.7 1.5 copy-start.1
  55.7 22.2 %collective-permute-start = (bf16[512,384]{1,0:T(8,128)(2,1)S(1)}, bf16[512,384]{1,0:T(8,128)(2,1)S(1)}, u32[]{:S(2)}, u32[]{:S(2)}) collective-permute-start(bf16[512,384]{1,0:T(8,128)(2,1)S(1)} %rise_4.1), channel_id=1, source_target_pairs={{0,128},{128,256},{256,384},{384,512},{512,640},{640,768},{768,896... | collective-permute-start | bytes 1179656 | tf_op jit(solution)/shard_map/ppermute | solution.py:160
  58.1 22.2 %collective-permute-start.4 = (bf16[512,384]{1,0:T(8,128)(2,1)S(1)}, bf16[512,384]{1,0:T(8,128)(2,1)S(1)}, u32[]{:S(2)}, u32[]{:S(2)}) collective-permute-start(bf16[512,384]{1,0:T(8,128)(2,1)S(1)} %fall_3.1), channel_id=1, source_target_pairs={{0,896},{128,0},{256,128},{384,256},{512,384},{640,512},{768,640},... | collective-permute-start | bytes 1179656 | tf_op jit(solution)/shard_map/ppermute | solution.py:160
  78.3 13.0 %collective-permute-start.1 = (bf16[512,384]{1,0:T(8,128)(2,1)S(1)}, bf16[512,384]{1,0:T(8,128)(2,1)S(1)}, u32[]{:S(2)}, u32[]{:S(2)}) collective-permute-start(bf16[512,384]{1,0:T(8,128)(2,1)S(1)} %rise_3.1), channel_id=1, source_target_pairs={{0,128},{128,256},{256,384},{384,512},{512,640},{640,768},{768,896... | collective-permute-start | bytes 1179656 | tf_op jit(solution)/shard_map/ppermute | solution.py:160
  80.7 13.0 %collective-permute-start.5 = (bf16[512,384]{1,0:T(8,128)(2,1)S(1)}, bf16[512,384]{1,0:T(8,128)(2,1)S(1)}, u32[]{:S(2)}, u32[]{:S(2)}) collective-permute-start(bf16[512,384]{1,0:T(8,128)(2,1)S(1)} %fall_2.1), channel_id=1, source_target_pairs={{0,896},{128,0},{256,128},{384,256},{512,384},{640,512},{768,640},... | collective-permute-start | bytes 1179656 | tf_op jit(solution)/shard_map/ppermute | solution.py:160
  91.7 12.1 %collective-permute-start.2 = (bf16[512,384]{1,0:T(8,128)(2,1)S(1)}, bf16[512,384]{1,0:T(8,128)(2,1)S(1)}, u32[]{:S(2)}, u32[]{:S(2)}) collective-permute-start(bf16[512,384]{1,0:T(8,128)(2,1)S(1)} %rise_2.1), channel_id=1, source_target_pairs={{0,128},{128,256},{256,384},{384,512},{512,640},{640,768},{768,896... | collective-permute-start | bytes 1179656 | tf_op jit(solution)/shard_map/ppermute | solution.py:160
  94.2 12.5 %collective-permute-start.6 = (bf16[512,384]{1,0:T(8,128)(2,1)S(1)}, bf16[512,384]{1,0:T(8,128)(2,1)S(1)}, u32[]{:S(2)}, u32[]{:S(2)}) collective-permute-start(bf16[512,384]{1,0:T(8,128)(2,1)S(1)} %fall_1.1), channel_id=1, source_target_pairs={{0,896},{128,0},{256,128},{384,256},{512,384},{640,512},{768,640},... | collective-permute-start | bytes 1179656 | tf_op jit(solution)/shard_map/ppermute | solution.py:160
  104.3 11.1 %collective-permute-start.3 = (bf16[512,384]{1,0:T(8,128)(2,1)S(1)}, bf16[512,384]{1,0:T(8,128)(2,1)S(1)}, u32[]{:S(2)}, u32[]{:S(2)}) collective-permute-start(bf16[512,384]{1,0:T(8,128)(2,1)S(1)} %rise_1.1), channel_id=1, source_target_pairs={{0,128},{128,256},{256,384},{384,512},{512,640},{640,768},{768,896... | collective-permute-start | bytes 1179656 | tf_op jit(solution)/shard_map/ppermute | solution.py:160
  115.6 8.3 %collective-permute-start.7 = (bf16[512,256]{1,0:T(8,128)(2,1)S(1)}, bf16[512,256]{1,0:T(8,128)(2,1)S(1)}, u32[]{:S(2)}, u32[]{:S(2)}) collective-permute-start(bf16[512,256]{1,0:T(8,128)(2,1)S(1)} %activate.1.refs_1_), channel_id=1, source_target_pairs={{0,128},{128,256},{256,384},{384,512},{512,640},{640,768},{768,896... | collective-permute-start | bytes 786440 | tf_op jit(solution)/shard_map/ppermute | solution.py:160
  117.6 8.3 %collective-permute-start.11 = (bf16[512,256]{1,0:T(8,128)(2,1)S(1)}, bf16[512,256]{1,0:T(8,128)(2,1)S(1)}, u32[]{:S(2)}, u32[]{:S(2)}) collective-permute-start(bf16[512,256]{1,0:T(8,128)(2,1)S(1)} %activate.1.refs_1_), channel_id=1, source_target_pairs={{0,896},{128,0},{256,128},{384,256},{512,384},{640,512},{768,640},... | collective-permute-start | bytes 786440 | tf_op jit(solution)/shard_map/ppermute | solution.py:160
  124.0 8.3 %collective-permute-start.8 = (bf16[512,256]{1,0:T(8,128)(2,1)S(1)}, bf16[512,256]{1,0:T(8,128)(2,1)S(1)}, u32[]{:S(2)}, u32[]{:S(2)}) collective-permute-start(bf16[512,256]{1,0:T(8,128)(2,1)S(1)} %collective-permute-done.7.refs_2_), channel_id=1, source_target_pairs={{0,128},{128,256},{256,384},{384,512},{512,640},{640,768},{768,896... | collective-permute-start | bytes 786440 | tf_op jit(solution)/shard_map/ppermute | solution.py:160
  125.9 8.3 %collective-permute-start.12 = (bf16[512,256]{1,0:T(8,128)(2,1)S(1)}, bf16[512,256]{1,0:T(8,128)(2,1)S(1)}, u32[]{:S(2)}, u32[]{:S(2)}) collective-permute-start(bf16[512,256]{1,0:T(8,128)(2,1)S(1)} %collective-permute-done.11.refs_3_), channel_id=1, source_target_pairs={{0,896},{128,0},{256,128},{384,256},{512,384},{640,512},{768,640},... | collective-permute-start | bytes 786440 | tf_op jit(solution)/shard_map/ppermute | solution.py:160
  132.3 8.3 %collective-permute-start.9 = (bf16[512,256]{1,0:T(8,128)(2,1)S(1)}, bf16[512,256]{1,0:T(8,128)(2,1)S(1)}, u32[]{:S(2)}, u32[]{:S(2)}) collective-permute-start(bf16[512,256]{1,0:T(8,128)(2,1)S(1)} %collective-permute-done.8.refs_4_), channel_id=1, source_target_pairs={{0,128},{128,256},{256,384},{384,512},{512,640},{640,768},{768,896... | collective-permute-start | bytes 786440 | tf_op jit(solution)/shard_map/ppermute | solution.py:160
  134.2 8.3 %collective-permute-start.13 = (bf16[512,256]{1,0:T(8,128)(2,1)S(1)}, bf16[512,256]{1,0:T(8,128)(2,1)S(1)}, u32[]{:S(2)}, u32[]{:S(2)}) collective-permute-start(bf16[512,256]{1,0:T(8,128)(2,1)S(1)} %collective-permute-done.12.refs_5_), channel_id=1, source_target_pairs={{0,896},{128,0},{256,128},{384,256},{512,384},{640,512},{768,640},... | collective-permute-start | bytes 786440 | tf_op jit(solution)/shard_map/ppermute | solution.py:160
  140.6 9.1 %collective-permute-start.10 = (bf16[512,256]{1,0:T(8,128)(2,1)S(1)}, bf16[512,256]{1,0:T(8,128)(2,1)S(1)}, u32[]{:S(2)}, u32[]{:S(2)}) collective-permute-start(bf16[512,256]{1,0:T(8,128)(2,1)S(1)} %collective-permute-done.9.refs_6_), channel_id=1, source_target_pairs={{0,128},{128,256},{256,384},{384,512},{512,640},{640,768},{768,896... | collective-permute-start | bytes 786440 | tf_op jit(solution)/shard_map/ppermute | solution.py:160
  184.3 0.8 copy-start.3

commit v9 on v8

--- a/solution.py
+++ b/solution.py
@@ -246,6 +246,22 @@
     return row_grad(me, [last], [half], w_gate, w_up, n_rep, total, BF16, "row_grad_far")
 
 
+def combine_kernel(pt_ref, rows_ref, out_ref):
+    total = jnp.dot(pt_ref[...], rows_ref[...], preferred_element_type=F32)
+    out_ref[...] = total.astype(BF16)
+
+
+def combine(per_token_t, returned):
+    return pl.pallas_call(
+        combine_kernel,
+        in_specs=[VMEM_SPEC] * 2,
+        out_specs=VMEM_SPEC,
+        out_shape=jax.ShapeDtypeStruct((per_token_t.shape[0], returned.shape[1]), BF16),
+        compiler_params=params(),
+        name="combine",
+    )(per_token_t, returned)
+
+
 def per_device(tokens, out_grad, expert_ids, route_weights, gate_weight, up_weight, down_weight):
     tok, width = tokens.shape
     top = expert_ids.shape[1]
@@ -265,7 +281,7 @@
         *width_sums(me, both_rows, gate_weight, up_weight, down_weight, n_rep)
     )
     returned = exchange(gather_matmul(me, own, gate_weight, up_weight, n_rep))
-    return jnp.dot(per_token_t, returned, preferred_element_type=F32).astype(BF16)
+    return combine(per_token_t, returned)
 
 
 def solution(mesh):

time: 187 us -> 187 us (level)
  no operation moved by 1% of the time
where the time goes in v9:
time: 187 us; the launch traced here: 186 us
  starting transfers between devices  70.6 us (38%)
  waiting for transfers between devices  69.1 us (37%)
  blocking collectives  34.2 us (18%)
  Pallas kernels  9.8 us (5%)
  local copies, waits for them, and re-layouts  1.97 us (1%)
    ppermute x14, starting transfers between devices, shift(): lax.ppermute(rows, 'rep', [(i, (i + by) % n_rep) for i in range(n_rep)])  51.1 us
    ppermute x14, waiting for transfers between devices, shift(): lax.ppermute(rows, 'rep', [(i, (i + by) % n_rep) for i in range(n_rep)])  38.1 us
    all_to_all x1, blocking collectives, exchange(): lax.all_to_all(blocks, ('outer', 'local'), 0, 0, tiled=True)  34.2 us
    all_to_all x1, waiting for transfers between devices, exchange(): lax.all_to_all(blocks, ('outer', 'local'), 0, 0, tiled=True)  31 us
    all_to_all x1, starting transfers between devices, exchange(): lax.all_to_all(blocks, ('outer', 'local'), 0, 0, tiled=True)  19.5 us
  transfers between devices with their start and end apart: 15, of which 9 were waited for; matrix products, arithmetic and copies ran while one was open for 0% of the time, Pallas kernels for 2%

profile of v9, /device:TPU:1, one launch (start us, length us, event | category | flops | bytes accessed | tf_op | source)
XLA Modules:
  0.0 185.9 jit_solution(18399682950608301600)
XLA Ops:
  0.0 3.1 %route.1 = (bf16[1024,512]{1,0:T(8,128)(2,1)}, bf16[32,512]{1,0:T(8,128)(2,1)}) custom-call(s32[8,32]{1,0:T(8,128)} %bitcast.7, f32[8,32]{1,0:T(8,128)} %bitcast.8, bf16[32,512]{1,0:T(8,128)(2,1)} %refs_2_.10, bf16[32,512]{1,0:T(8,128)(2,1)} %refs_3_.10), custom_call_target="tpu_custom_call" | custom-call | tf_op jit(solution)/shard_map/route/pallas_call | solution.py:85
  3.1 0.0 copy-start.2
  3.1 19.5 %all-to-all-start = ((bf16[128,8,512]{2,1,0:T(8,128)(2,1)}), bf16[128,8,512]{2,1,0:T(8,128)(2,1)S(1)}, u32[]{:S(2)}, u32[]{:S(2)}) async-start(bf16[128,8,512]{2,1,0:T(8,128)(2,1)} %bitcast.6), calls=%async_computation | async-start | bytes 2097152 | tf_op jit(solution)/shard_map/all_to_all | solution.py:277
  22.6 31.0 %all-to-all-done = bf16[128,8,512]{2,1,0:T(8,128)(2,1)S(1)} async-done(((bf16[128,8,512]{2,1,0:T(8,128)(2,1)}), bf16[128,8,512]{2,1,0:T(8,128)(2,1)S(1)}, u32[]{:S(2)}, u32[]{:S(2)}) %all-to-all-start) | async-done | bytes 1048608 | tf_op jit(solution)/shard_map/all_to_all | solution.py:277
  53.7 0.0 copy-start
  53.7 0.0 copy-start.1
  53.7 0.4 split.1.refs_1_
  54.1 0.0 copy-done.2
  54.1 0.8 copy-done
  54.9 0.3 copy-done.1
  55.2 0.5 rise_4.1
  55.7 1.9 %collective-permute-start = (bf16[512,384]{1,0:T(8,128)(2,1)S(1)}, bf16[512,384]{1,0:T(8,128)(2,1)S(1)}, u32[]{:S(2)}, u32[]{:S(2)}) collective-permute-start(bf16[512,384]{1,0:T(8,128)(2,1)S(1)} %rise_4.1), channel_id=1, source_target_pairs={{0,128},{128,256},{256,384},{384,512},{512,640},{640,768},{768,896... | collective-permute-start | bytes 1179656 | tf_op jit(solution)/shard_map/ppermute | solution.py:160
  57.6 0.5 fall_3.1
  58.1 12.9 %collective-permute-start.4 = (bf16[512,384]{1,0:T(8,128)(2,1)S(1)}, bf16[512,384]{1,0:T(8,128)(2,1)S(1)}, u32[]{:S(2)}, u32[]{:S(2)}) collective-permute-start(bf16[512,384]{1,0:T(8,128)(2,1)S(1)} %fall_3.1), channel_id=1, source_target_pairs={{0,896},{128,0},{256,128},{384,256},{512,384},{640,512},{768,640},... | collective-permute-start | bytes 1179656 | tf_op jit(solution)/shard_map/ppermute | solution.py:160
  71.0 6.9 %collective-permute-done.refs_5_ = bf16[512,384]{1,0:T(8,128)(2,1)S(1)} collective-permute-done((bf16[512,384]{1,0:T(8,128)(2,1)S(1)}, bf16[512,384]{1,0:T(8,128)(2,1)S(1)}, u32[]{:S(2)}, u32[]{:S(2)}) %collective-permute-start) | collective-permute-done | bytes 393248 | tf_op jit(solution)/shard_map/ppermute | solution.py:160
  77.8 0.5 rise_3.1
  78.3 1.9 %collective-permute-start.1 = (bf16[512,384]{1,0:T(8,128)(2,1)S(1)}, bf16[512,384]{1,0:T(8,128)(2,1)S(1)}, u32[]{:S(2)}, u32[]{:S(2)}) collective-permute-start(bf16[512,384]{1,0:T(8,128)(2,1)S(1)} %rise_3.1), channel_id=1, source_target_pairs={{0,128},{128,256},{256,384},{384,512},{512,640},{640,768},{768,896... | collective-permute-start | bytes 1179656 | tf_op jit(solution)/shard_map/ppermute | solution.py:160
  80.2 0.0 collective-permute-done.4.refs_5_
  80.2 0.5 fall_2.1
  80.7 4.6 %collective-permute-start.5 = (bf16[512,384]{1,0:T(8,128)(2,1)S(1)}, bf16[512,384]{1,0:T(8,128)(2,1)S(1)}, u32[]{:S(2)}, u32[]{:S(2)}) collective-permute-start(bf16[512,384]{1,0:T(8,128)(2,1)S(1)} %fall_2.1), channel_id=1, source_target_pairs={{0,896},{128,0},{256,128},{384,256},{512,384},{640,512},{768,640},... | collective-permute-start | bytes 1179656 | tf_op jit(solution)/shard_map/ppermute | solution.py:160
  85.3 6.0 %collective-permute-done.1.refs_5_ = bf16[512,384]{1,0:T(8,128)(2,1)S(1)} collective-permute-done((bf16[512,384]{1,0:T(8,128)(2,1)S(1)}, bf16[512,384]{1,0:T(8,128)(2,1)S(1)}, u32[]{:S(2)}, u32[]{:S(2)}) %collective-permute-start.1) | collective-permute-done | bytes 393248 | tf_op jit(solution)/shard_map/ppermute | solution.py:160
  91.3 0.5 rise_2.1
  91.7 1.9 %collective-permute-start.2 = (bf16[512,384]{1,0:T(8,128)(2,1)S(1)}, bf16[512,384]{1,0:T(8,128)(2,1)S(1)}, u32[]{:S(2)}, u32[]{:S(2)}) collective-permute-start(bf16[512,384]{1,0:T(8,128)(2,1)S(1)} %rise_2.1), channel_id=1, source_target_pairs={{0,128},{128,256},{256,384},{384,512},{512,640},{640,768},{768,896... | collective-permute-start | bytes 1179656 | tf_op jit(solution)/shard_map/ppermute | solution.py:160
  93.7 0.0 collective-permute-done.5.refs_5_
  93.7 0.5 fall_1.1
  94.2 4.6 %collective-permute-start.6 = (bf16[512,384]{1,0:T(8,128)(2,1)S(1)}, bf16[512,384]{1,0:T(8,128)(2,1)S(1)}, u32[]{:S(2)}, u32[]{:S(2)}) collective-permute-start(bf16[512,384]{1,0:T(8,128)(2,1)S(1)} %fall_1.1), channel_id=1, source_target_pairs={{0,896},{128,0},{256,128},{384,256},{512,384},{640,512},{768,640},... | collective-permute-start | bytes 1179656 | tf_op jit(solution)/shard_map/ppermute | solution.py:160
  98.7 5.1 %collective-permute-done.2.refs_5_ = bf16[512,384]{1,0:T(8,128)(2,1)S(1)} collective-permute-done((bf16[512,384]{1,0:T(8,128)(2,1)S(1)}, bf16[512,384]{1,0:T(8,128)(2,1)S(1)}, u32[]{:S(2)}, u32[]{:S(2)}) %collective-permute-start.2) | collective-permute-done | bytes 393248 | tf_op jit(solution)/shard_map/ppermute | solution.py:160
  103.8 0.5 rise_1.1
  104.3 1.9 %collective-permute-start.3 = (bf16[512,384]{1,0:T(8,128)(2,1)S(1)}, bf16[512,384]{1,0:T(8,128)(2,1)S(1)}, u32[]{:S(2)}, u32[]{:S(2)}) collective-permute-start(bf16[512,384]{1,0:T(8,128)(2,1)S(1)} %rise_1.1), channel_id=1, source_target_pairs={{0,128},{128,256},{256,384},{384,512},{512,640},{640,768},{768,896... | collective-permute-start | bytes 1179656 | tf_op jit(solution)/shard_map/ppermute | solution.py:160
  106.2 0.5 own_term.1.own_ref
  106.7 0.0 collective-permute-done.6.down_ref
  106.7 8.7 %collective-permute-done.3.up_ref = bf16[512,384]{1,0:T(8,128)(2,1)S(1)} collective-permute-done((bf16[512,384]{1,0:T(8,128)(2,1)S(1)}, bf16[512,384]{1,0:T(8,128)(2,1)S(1)}, u32[]{:S(2)}, u32[]{:S(2)}) %collective-permute-start.3) | collective-permute-done | bytes 393248 | tf_op jit(solution)/shard_map/ppermute | solution.py:160
  115.4 0.2 activate.1.refs_1_
  115.6 1.9 %collective-permute-start.7 = (bf16[512,256]{1,0:T(8,128)(2,1)S(1)}, bf16[512,256]{1,0:T(8,128)(2,1)S(1)}, u32[]{:S(2)}, u32[]{:S(2)}) collective-permute-start(bf16[512,256]{1,0:T(8,128)(2,1)S(1)} %activate.1.refs_1_), channel_id=1, source_target_pairs={{0,128},{128,256},{256,384},{384,512},{512,640},{640,768},{768,896... | collective-permute-start | bytes 786440 | tf_op jit(solution)/shard_map/ppermute | solution.py:160
  117.6 4.6 %collective-permute-start.11 = (bf16[512,256]{1,0:T(8,128)(2,1)S(1)}, bf16[512,256]{1,0:T(8,128)(2,1)S(1)}, u32[]{:S(2)}, u32[]{:S(2)}) collective-permute-start(bf16[512,256]{1,0:T(8,128)(2,1)S(1)} %activate.1.refs_1_), channel_id=1, source_target_pairs={{0,896},{128,0},{256,128},{384,256},{512,384},{640,512},{768,640},... | collective-permute-start | bytes 786440 | tf_op jit(solution)/shard_map/ppermute | solution.py:160
  122.1 1.8 collective-permute-done.7.refs_2_
  124.0 1.9 %collective-permute-start.8 = (bf16[512,256]{1,0:T(8,128)(2,1)S(1)}, bf16[512,256]{1,0:T(8,128)(2,1)S(1)}, u32[]{:S(2)}, u32[]{:S(2)}) collective-permute-start(bf16[512,256]{1,0:T(8,128)(2,1)S(1)} %collective-permute-done.7.refs_2_), channel_id=1, source_target_pairs={{0,128},{128,256},{256,384},{384,512},{512,640},{640,768},{768,896... | collective-permute-start | bytes 786440 | tf_op jit(solution)/shard_map/ppermute | solution.py:160
  125.9 0.0 collective-permute-done.11.refs_3_
  125.9 4.6 %collective-permute-start.12 = (bf16[512,256]{1,0:T(8,128)(2,1)S(1)}, bf16[512,256]{1,0:T(8,128)(2,1)S(1)}, u32[]{:S(2)}, u32[]{:S(2)}) collective-permute-start(bf16[512,256]{1,0:T(8,128)(2,1)S(1)} %collective-permute-done.11.refs_3_), channel_id=1, source_target_pairs={{0,896},{128,0},{256,128},{384,256},{512,384},{640,512},{768,640},... | collective-permute-start | bytes 786440 | tf_op jit(solution)/shard_map/ppermute | solution.py:160
  130.5 1.8 collective-permute-done.8.refs_4_
  132.3 1.9 %collective-permute-start.9 = (bf16[512,256]{1,0:T(8,128)(2,1)S(1)}, bf16[512,256]{1,0:T(8,128)(2,1)S(1)}, u32[]{:S(2)}, u32[]{:S(2)}) collective-permute-start(bf16[512,256]{1,0:T(8,128)(2,1)S(1)} %collective-permute-done.8.refs_4_), channel_id=1, source_target_pairs={{0,128},{128,256},{256,384},{384,512},{512,640},{640,768},{768,896... | collective-permute-start | bytes 786440 | tf_op jit(solution)/shard_map/ppermute | solution.py:160
  134.2 0.0 collective-permute-done.12.refs_5_
  134.2 4.6 %collective-permute-start.13 = (bf16[512,256]{1,0:T(8,128)(2,1)S(1)}, bf16[512,256]{1,0:T(8,128)(2,1)S(1)}, u32[]{:S(2)}, u32[]{:S(2)}) collective-permute-start(bf16[512,256]{1,0:T(8,128)(2,1)S(1)} %collective-permute-done.12.refs_5_), channel_id=1, source_target_pairs={{0,896},{128,0},{256,128},{384,256},{512,384},{640,512},{768,640},... | collective-permute-start | bytes 786440 | tf_op jit(solution)/shard_map/ppermute | solution.py:160
  138.8 1.8 collective-permute-done.9.refs_6_
  140.6 1.9 %collective-permute-start.10 = (bf16[512,256]{1,0:T(8,128)(2,1)S(1)}, bf16[512,256]{1,0:T(8,128)(2,1)S(1)}, u32[]{:S(2)}, u32[]{:S(2)}) collective-permute-start(bf16[512,256]{1,0:T(8,128)(2,1)S(1)} %collective-permute-done.9.refs_6_), channel_id=1, source_target_pairs={{0,128},{128,256},{256,384},{384,512},{512,640},{640,768},{768,896... | collective-permute-start | bytes 786440 | tf_op jit(solution)/shard_map/ppermute | solution.py:160
  142.5 0.0 collective-permute-done.13.refs_7_
  142.5 1.2 row_grad_near.1.refs_4_
  143.7 5.9 %collective-permute-done.10.refs_1_ = bf16[512,256]{1,0:T(8,128)(2,1)S(1)} collective-permute-done((bf16[512,256]{1,0:T(8,128)(2,1)S(1)}, bf16[512,256]{1,0:T(8,128)(2,1)S(1)}, u32[]{:S(2)}, u32[]{:S(2)}) %collective-permute-start.10) | collective-permute-done | bytes 262176 | tf_op jit(solution)/shard_map/ppermute | solution.py:160
  149.7 0.3 row_grad_far.1
  150.0 0.1 reshape.18
  150.1 34.2 %all_to_all.10 = bf16[128,4,512]{2,1,0:T(4,128)(2,1)S(1)} all-to-all(bf16[128,4,512]{2,1,0:T(4,128)(2,1)S(1)} %reshape.18), channel_id=1, replica_groups=mesh['rep'=8,'outer'=8,'local'=16] {'outer','local'}, dimensions={0} | all-to-all | bytes 1048576 | tf_op jit(solution)/shard_map/all_to_all | solution.py:277
  184.3 0.0 copy-start.3
  184.3 0.1 reshape.19.rows_ref
  184.4 0.6 copy-done.3
  185.1 0.8 combine.1
Async XLA Ops:
  3.1 51.0 %copy-start.2 = (bf16[1,1024,512]{2,1,0:T(8,128)(2,1)S(1)}, bf16[1,1024,512]{2,1,0:T(8,128)(2,1)}, u32[]{:S(2)}) copy-start(bf16[1,1024,512]{2,1,0:T(8,128)(2,1)} %refs_4_.15) | copy-start | bytes 3145732
  3.1 50.5 %all-to-all-start = ((bf16[128,8,512]{2,1,0:T(8,128)(2,1)}), bf16[128,8,512]{2,1,0:T(8,128)(2,1)S(1)}, u32[]{:S(2)}, u32[]{:S(2)}) async-start(bf16[128,8,512]{2,1,0:T(8,128)(2,1)} %bitcast.6), calls=%async_computation | async-start | bytes 2097152 | tf_op jit(solution)/shard_map/all_to_all | solution.py:277
  53.7 1.2 copy-start
  53.7 1.5 copy-start.1
  55.7 22.2 %collective-permute-start = (bf16[512,384]{1,0:T(8,128)(2,1)S(1)}, bf16[512,384]{1,0:T(8,128)(2,1)S(1)}, u32[]{:S(2)}, u32[]{:S(2)}) collective-permute-start(bf16[512,384]{1,0:T(8,128)(2,1)S(1)} %rise_4.1), channel_id=1, source_target_pairs={{0,128},{128,256},{256,384},{384,512},{512,640},{640,768},{768,896... | collective-permute-start | bytes 1179656 | tf_op jit(solution)/shard_map/ppermute | solution.py:160
  58.1 22.2 %collective-permute-start.4 = (bf16[512,384]{1,0:T(8,128)(2,1)S(1)}, bf16[512,384]{1,0:T(8,128)(2,1)S(1)}, u32[]{:S(2)}, u32[]{:S(2)}) collective-permute-start(bf16[512,384]{1,0:T(8,128)(2,1)S(1)} %fall_3.1), channel_id=1, source_target_pairs={{0,896},{128,0},{256,128},{384,256},{512,384},{640,512},{768,640},... | collective-permute-start | bytes 1179656 | tf_op jit(solution)/shard_map/ppermute | solution.py:160
  78.3 13.0 %collective-permute-start.1 = (bf16[512,384]{1,0:T(8,128)(2,1)S(1)}, bf16[512,384]{1,0:T(8,128)(2,1)S(1)}, u32[]{:S(2)}, u32[]{:S(2)}) collective-permute-start(bf16[512,384]{1,0:T(8,128)(2,1)S(1)} %rise_3.1), channel_id=1, source_target_pairs={{0,128},{128,256},{256,384},{384,512},{512,640},{640,768},{768,896... | collective-permute-start | bytes 1179656 | tf_op jit(solution)/shard_map/ppermute | solution.py:160
  80.7 13.0 %collective-permute-start.5 = (bf16[512,384]{1,0:T(8,128)(2,1)S(1)}, bf16[512,384]{1,0:T(8,128)(2,1)S(1)}, u32[]{:S(2)}, u32[]{:S(2)}) collective-permute-start(bf16[512,384]{1,0:T(8,128)(2,1)S(1)} %fall_2.1), channel_id=1, source_target_pairs={{0,896},{128,0},{256,128},{384,256},{512,384},{640,512},{768,640},... | collective-permute-start | bytes 1179656 | tf_op jit(solution)/shard_map/ppermute | solution.py:160
  91.7 12.1 %collective-permute-start.2 = (bf16[512,384]{1,0:T(8,128)(2,1)S(1)}, bf16[512,384]{1,0:T(8,128)(2,1)S(1)}, u32[]{:S(2)}, u32[]{:S(2)}) collective-permute-start(bf16[512,384]{1,0:T(8,128)(2,1)S(1)} %rise_2.1), channel_id=1, source_target_pairs={{0,128},{128,256},{256,384},{384,512},{512,640},{640,768},{768,896... | collective-permute-start | bytes 1179656 | tf_op jit(solution)/shard_map/ppermute | solution.py:160
  94.2 12.5 %collective-permute-start.6 = (bf16[512,384]{1,0:T(8,128)(2,1)S(1)}, bf16[512,384]{1,0:T(8,128)(2,1)S(1)}, u32[]{:S(2)}, u32[]{:S(2)}) collective-permute-start(bf16[512,384]{1,0:T(8,128)(2,1)S(1)} %fall_1.1), channel_id=1, source_target_pairs={{0,896},{128,0},{256,128},{384,256},{512,384},{640,512},{768,640},... | collective-permute-start | bytes 1179656 | tf_op jit(solution)/shard_map/ppermute | solution.py:160
  104.3 11.1 %collective-permute-start.3 = (bf16[512,384]{1,0:T(8,128)(2,1)S(1)}, bf16[512,384]{1,0:T(8,128)(2,1)S(1)}, u32[]{:S(2)}, u32[]{:S(2)}) collective-permute-start(bf16[512,384]{1,0:T(8,128)(2,1)S(1)} %rise_1.1), channel_id=1, source_target_pairs={{0,128},{128,256},{256,384},{384,512},{512,640},{640,768},{768,896... | collective-permute-start | bytes 1179656 | tf_op jit(solution)/shard_map/ppermute | solution.py:160
  115.6 8.3 %collective-permute-start.7 = (bf16[512,256]{1,0:T(8,128)(2,1)S(1)}, bf16[512,256]{1,0:T(8,128)(2,1)S(1)}, u32[]{:S(2)}, u32[]{:S(2)}) collective-permute-start(bf16[512,256]{1,0:T(8,128)(2,1)S(1)} %activate.1.refs_1_), channel_id=1, source_target_pairs={{0,128},{128,256},{256,384},{384,512},{512,640},{640,768},{768,896... | collective-permute-start | bytes 786440 | tf_op jit(solution)/shard_map/ppermute | solution.py:160
  117.6 8.3 %collective-permute-start.11 = (bf16[512,256]{1,0:T(8,128)(2,1)S(1)}, bf16[512,256]{1,0:T(8,128)(2,1)S(1)}, u32[]{:S(2)}, u32[]{:S(2)}) collective-permute-start(bf16[512,256]{1,0:T(8,128)(2,1)S(1)} %activate.1.refs_1_), channel_id=1, source_target_pairs={{0,896},{128,0},{256,128},{384,256},{512,384},{640,512},{768,640},... | collective-permute-start | bytes 786440 | tf_op jit(solution)/shard_map/ppermute | solution.py:160
  124.0 8.3 %collective-permute-start.8 = (bf16[512,256]{1,0:T(8,128)(2,1)S(1)}, bf16[512,256]{1,0:T(8,128)(2,1)S(1)}, u32[]{:S(2)}, u32[]{:S(2)}) collective-permute-start(bf16[512,256]{1,0:T(8,128)(2,1)S(1)} %collective-permute-done.7.refs_2_), channel_id=1, source_target_pairs={{0,128},{128,256},{256,384},{384,512},{512,640},{640,768},{768,896... | collective-permute-start | bytes 786440 | tf_op jit(solution)/shard_map/ppermute | solution.py:160
  125.9 8.3 %collective-permute-start.12 = (bf16[512,256]{1,0:T(8,128)(2,1)S(1)}, bf16[512,256]{1,0:T(8,128)(2,1)S(1)}, u32[]{:S(2)}, u32[]{:S(2)}) collective-permute-start(bf16[512,256]{1,0:T(8,128)(2,1)S(1)} %collective-permute-done.11.refs_3_), channel_id=1, source_target_pairs={{0,896},{128,0},{256,128},{384,256},{512,384},{640,512},{768,640},... | collective-permute-start | bytes 786440 | tf_op jit(solution)/shard_map/ppermute | solution.py:160
  132.3 8.3 %collective-permute-start.9 = (bf16[512,256]{1,0:T(8,128)(2,1)S(1)}, bf16[512,256]{1,0:T(8,128)(2,1)S(1)}, u32[]{:S(2)}, u32[]{:S(2)}) collective-permute-start(bf16[512,256]{1,0:T(8,128)(2,1)S(1)} %collective-permute-done.8.refs_4_), channel_id=1, source_target_pairs={{0,128},{128,256},{256,384},{384,512},{512,640},{640,768},{768,896... | collective-permute-start | bytes 786440 | tf_op jit(solution)/shard_map/ppermute | solution.py:160
  134.2 8.3 %collective-permute-start.13 = (bf16[512,256]{1,0:T(8,128)(2,1)S(1)}, bf16[512,256]{1,0:T(8,128)(2,1)S(1)}, u32[]{:S(2)}, u32[]{:S(2)}) collective-permute-start(bf16[512,256]{1,0:T(8,128)(2,1)S(1)} %collective-permute-done.12.refs_5_), channel_id=1, source_target_pairs={{0,896},{128,0},{256,128},{384,256},{512,384},{640,512},{768,640},... | collective-permute-start | bytes 786440 | tf_op jit(solution)/shard_map/ppermute | solution.py:160
  140.6 9.1 %collective-permute-start.10 = (bf16[512,256]{1,0:T(8,128)(2,1)S(1)}, bf16[512,256]{1,0:T(8,128)(2,1)S(1)}, u32[]{:S(2)}, u32[]{:S(2)}) collective-permute-start(bf16[512,256]{1,0:T(8,128)(2,1)S(1)} %collective-permute-done.9.refs_6_), channel_id=1, source_target_pairs={{0,128},{128,256},{256,384},{384,512},{512,640},{640,768},{768,896... | collective-permute-start | bytes 786440 | tf_op jit(solution)/shard_map/ppermute | solution.py:160
  184.3 0.8 copy-start.3
